TPU v7x, 128 devices: a whole 4x4x4 slice. The times are simulated.
128 devices in a mesh: seq: 32 (over z, y_hi, x), chan: 4 (over y_lo, core).
Axes of the slice: x: 4, y: 4 (y_hi: 2, y_lo: 2; y = y_hi * 2 + y_lo), z: 4, core: 2. Of those that a mesh axis runs over, the one named last changes fastest.
Arguments:
- query_proj: bfloat16 [128, 131072], P('chan', 'seq'), may hold values from -6 to 6
- key_proj: bfloat16 [128, 131072], P('chan', 'seq'), may hold values from -6 to 6
- value_proj: bfloat16 [128, 131072], P('chan', 'seq'), may hold values from -6 to 6
- out_cotangent: bfloat16 [128, 131072], P('chan', 'seq'), may hold values from -6 to 6
- filter_raw: float32 [32, 131072], P(None, 'seq'), may hold values from -6 to 6
Outputs:
- query_grad: bfloat16 [128, 131072], P('chan', 'seq')
- key_grad: bfloat16 [128, 131072], P('chan', 'seq')
- value_grad: bfloat16 [128, 131072], P('chan', 'seq')
- filter_grad: float32 [32, 131072], P('chan', 'seq')
All inputs are finite; a program needn't handle non-finite values.
Results may differ from a plain program's by a relative error of at most 0.004.
Values sent between devices are 32-bit elements; how exact they have to be, the bound alone decides.
No kernel may reach another device: no remote copies, remote signals or barrier semaphores. Data moves between devices by JAX's collectives and lax.ppermute only.
A program may use at most 128 MiB of HBM per device.

v0:
```python
import math

import jax
import jax.numpy as jnp
from jax import lax
from jax.sharding import PartitionSpec as P

PRECISE = lax.Precision.HIGHEST
TWO_PI = 2.0 * math.pi


def phase_table(row_count, col_count, period):
    product = (
        jnp.arange(row_count, dtype=jnp.int32)[:, None]
        * jnp.arange(col_count, dtype=jnp.int32)[None, :]
        % period
    )
    angles = product.astype(jnp.float32) * (TWO_PI / period)
    return (jnp.cos(angles), jnp.sin(angles))


def rotate(real_part, imag_part, cos_table, sin_table, sign):
    return (
        real_part * cos_table - sign * imag_part * sin_table,
        imag_part * cos_table + sign * real_part * sin_table,
    )


def complex_apply(real_part, imag_part, cos_table, sin_table, form, sign):
    real_cos = jnp.einsum(form, real_part, cos_table, precision=PRECISE)
    real_sin = jnp.einsum(form, real_part, sin_table, precision=PRECISE)
    imag_cos = jnp.einsum(form, imag_part, cos_table, precision=PRECISE)
    imag_sin = jnp.einsum(form, imag_part, sin_table, precision=PRECISE)
    return (real_cos - sign * imag_sin, imag_cos + sign * real_sin)


def local_forward(received):
    real_part, imag_part = (received[0], received[1])
    items, paired, width = real_part.shape
    inner = min(128, width)
    outer = width // inner
    real_part = real_part.reshape(items, paired, outer, inner)
    imag_part = imag_part.reshape(items, paired, outer, inner)
    cos_first, sin_first = phase_table(outer, outer, outer)
    real_part, imag_part = complex_apply(
        real_part, imag_part, cos_first, sin_first, "mkab,ac->mkcb", -1.0
    )
    cos_turn, sin_turn = phase_table(outer, inner, width)
    real_part, imag_part = rotate(real_part, imag_part, cos_turn, sin_turn, -1.0)
    cos_last, sin_last = phase_table(inner, inner, inner)
    real_part, imag_part = complex_apply(
        real_part, imag_part, cos_last, sin_last, "mkcb,bd->mkcd", -1.0
    )
    return jnp.stack([real_part, imag_part])


def local_inverse(spectra):
    real_part, imag_part = (spectra[0], spectra[1])
    items, paired, outer, inner = real_part.shape
    width = outer * inner
    cos_last, sin_last = phase_table(inner, inner, inner)
    real_part, imag_part = complex_apply(
        real_part, imag_part, cos_last, sin_last, "mkcd,db->mkcb", 1.0
    )
    cos_turn, sin_turn = phase_table(outer, inner, width)
    real_part, imag_part = rotate(real_part, imag_part, cos_turn, sin_turn, 1.0)
    cos_first, sin_first = phase_table(outer, outer, outer)
    real_part, imag_part = complex_apply(
        real_part, imag_part, cos_first, sin_first, "mkcb,ca->mkab", 1.0
    )
    return (real_part.reshape(items, paired, width), imag_part.reshape(items, paired, width))


def forward_spectra(signal):
    parts = lax.axis_size("seq")
    channels, width = signal.shape
    block = width // parts
    full_len = 2 * parts * width
    classes = 2 * parts
    split_rows = signal.reshape(channels, parts, block)
    received = lax.all_to_all(split_rows, "seq", split_axis=1, concat_axis=1, tiled=True)
    cos_small, sin_small = phase_table(parts, classes, classes)
    real_part = jnp.einsum("mtr,tk->mkr", received, cos_small, precision=PRECISE)
    imag_part = -jnp.einsum("mtr,tk->mkr", received, sin_small, precision=PRECISE)
    position = lax.axis_index("seq") * block + jnp.arange(block, dtype=jnp.int32)
    turned = jnp.arange(classes, dtype=jnp.int32)[:, None] * position[None, :] % full_len
    angles = turned.astype(jnp.float32) * (TWO_PI / full_len)
    real_part, imag_part = rotate(real_part, imag_part, jnp.cos(angles), jnp.sin(angles), -1.0)
    mixed = jnp.stack([real_part, imag_part])
    return local_forward(lax.all_to_all(mixed, "seq", split_axis=2, concat_axis=3, tiled=True))


def inverse_signal(spectra):
    parts = lax.axis_size("seq")
    real_part, imag_part = local_inverse(spectra)
    channels, paired, width = real_part.shape
    block = width // parts
    full_len = 2 * parts * width
    classes = 2 * parts
    own_class = lax.axis_index("seq") * 2 + jnp.arange(paired, dtype=jnp.int32)
    turned = own_class[:, None] * jnp.arange(width, dtype=jnp.int32)[None, :] % full_len
    angles = turned.astype(jnp.float32) * (TWO_PI / full_len)
    real_part, imag_part = rotate(real_part, imag_part, jnp.cos(angles), jnp.sin(angles), 1.0)
    stacked = jnp.stack([real_part, imag_part]).reshape(2, channels, paired, parts, block)
    received = lax.all_to_all(stacked, "seq", split_axis=3, concat_axis=2, tiled=True)
    cos_small, sin_small = phase_table(classes, parts, classes)
    real_in = received[0][:, :, 0, :]
    imag_in = received[1][:, :, 0, :]
    real_sum = jnp.einsum("mkr,kt->mtr", real_in, cos_small, precision=PRECISE)
    real_sum = real_sum - jnp.einsum("mkr,kt->mtr", imag_in, sin_small, precision=PRECISE)
    row_blocks = real_sum[:, None] * (1.0 / full_len)
    back = lax.all_to_all(row_blocks, "seq", split_axis=2, concat_axis=3, tiled=True)
    count = back.shape[1]
    back = back.reshape(channels, count, width)
    return (back[:, 0], back[:, count - 1])


def to_natural(spectra):
    parts = lax.axis_size("seq")
    channels, paired, outer, inner = (
        spectra.shape[1],
        spectra.shape[2],
        spectra.shape[3],
        spectra.shape[4],
    )
    shaped = spectra.reshape(2, channels, paired, outer, parts, inner // parts)
    moved = lax.all_to_all(shaped, "seq", split_axis=4, concat_axis=2, tiled=True)
    return moved.transpose(0, 1, 4, 5, 3, 2).reshape(2, channels, -1)


def from_natural(flat, outer, inner):
    parts = lax.axis_size("seq")
    channels = flat.shape[1]
    shaped = flat.reshape(2, channels, inner // parts, outer, 2 * parts)
    shaped = shaped.transpose(0, 1, 4, 3, 2).reshape(
        2, channels, 2 * parts, outer, 1, inner // parts
    )
    moved = lax.all_to_all(shaped, "seq", split_axis=2, concat_axis=4, tiled=True)
    return moved.reshape(2, channels, 2, outer, inner)


def complex_times(first, second, conjugate):
    sign = -1.0 if conjugate else 1.0
    real_part = first[0] * second[0] - sign * first[1] * second[1]
    imag_part = first[1] * second[0] + sign * first[0] * second[1]
    return jnp.stack([real_part, imag_part])


def shards(query_proj, key_proj, value_proj, out_cotangent, filter_raw):
    parts = lax.axis_size("seq")
    slab, width = query_proj.shape
    scale = 1.0 / math.sqrt(parts * width)
    key_float = key_proj.astype(jnp.float32)
    value_float = value_proj.astype(jnp.float32)
    cotangent_float = out_cotangent.astype(jnp.float32)
    gated = key_float * value_float
    carried = query_proj.astype(jnp.float32) * cotangent_float
    spectra = forward_spectra(jnp.concatenate([gated, carried, filter_raw * scale], axis=0))
    outer, inner = (spectra.shape[3], spectra.shape[4])
    spectra = to_natural(spectra)
    gated_spec = spectra[:, :slab]
    carried_spec = spectra[:, slab : 2 * slab]
    filter_spec = spectra[:, 2 * slab :]
    products = jnp.concatenate(
        [
            complex_times(gated_spec, filter_spec, False),
            complex_times(carried_spec, filter_spec, True),
            complex_times(carried_spec, gated_spec, True),
        ],
        axis=1,
    )
    products = from_natural(products, outer, inner)
    filter_part = products[:, 2 * slab :]
    real_rows, unused_rows = inverse_signal(
        jnp.concatenate([products[:, : 2 * slab], filter_part], axis=1)
    )
    conv_out = real_rows[:slab]
    adjoint = real_rows[slab : 2 * slab]
    filter_rows = real_rows[2 * slab :]
    filter_grad = lax.psum_scatter(filter_rows, "chan", scatter_dimension=0, tiled=True) * scale
    query_grad = (conv_out * cotangent_float).astype(jnp.bfloat16)
    key_grad = (adjoint * value_float).astype(jnp.bfloat16)
    value_grad = (adjoint * key_float).astype(jnp.bfloat16)
    return (query_grad, key_grad, value_grad, filter_grad)


def solution(mesh):
    placed = (
        P("chan", "seq"),
        P("chan", "seq"),
        P("chan", "seq"),
        P("chan", "seq"),
        P(None, "seq"),
    )
    return jax.shard_map(
        shards,
        mesh=mesh,
        in_specs=placed,
        out_specs=(P("chan", "seq"), P("chan", "seq"), P("chan", "seq"), P("chan", "seq")),
        check_vma=False,
    )
```

profile of v0, /device:TPU:1, one launch (start us, length us, event | category | flops | bytes accessed | tf_op | source)
XLA Modules:
  0.0 694.5 jit_solution(2289428009742377025)
XLA Ops:
  10.9 11.3 %all-to-all-start = ((f32[96,32,128]{2,0,1:T(8,128)}), f32[96,32,128]{2,0,1:T(8,128)S(1)}, u32[]{:S(2)}, u32[]{:S(2)}) async-start(f32[96,32,128]{2,0,1:T(8,128)} %copy_bitcast_fusion.2), calls=%async_computation | async-start | bytes 3145728 | tf_op jit(solution)/shard_map/all_to_all | solution.py:81
  22.4 22.4 %all-to-all-done = f32[96,32,128]{2,0,1:T(8,128)S(1)} async-done(((f32[96,32,128]{2,0,1:T(8,128)}), f32[96,32,128]{2,0,1:T(8,128)S(1)}, u32[]{:S(2)}, u32[]{:S(2)}) %all-to-all-start) | async-done | bytes 1572896 | tf_op jit(solution)/shard_map/all_to_all | solution.py:81
  48.4 4.3 subtract_bitcast_fusion
  53.8 6.3 copy.95
  60.1 6.5 all-to-all-start.1
  66.6 80.7 %all-to-all-done.1 = f32[2,96,64,128]{3,1,0,2:T(8,128)} async-done(((f32[2,96,64,128]{3,1,0,2:T(8,128)}), f32[2,96,64,128]{3,1,0,2:T(8,128)}, u32[]{:S(2)}, u32[]{:S(2)}) %all-to-all-start.1) | async-done | bytes 6291488 | tf_op jit(solution)/shard_map/all_to_all | solution.py:90
  147.4 6.4 copy.148
  169.4 4.7 fusion.4
  174.1 5.2 multiply_subtract_fusion.4
  179.2 5.5 copy.98
  184.7 6.5 multiply_add_fusion.4
  191.2 5.5 copy.99
  196.7 4.5 pad_maximum_fusion
  203.1 113.4 %all_to_all.77 = f32[2,96,2,32,32,4]{1,3,5,2,0,4:T(8,128)S(1)} all-to-all(f32[2,96,2,32,32,4]{1,3,5,2,0,4:T(8,128)S(1)} %copy.100), channel_id=1, replica_groups=mesh['seq'=32,'chan'=4] {'seq'}, dimensions={4} | all-to-all | bytes 12582912 | tf_op jit(solution)/shard_map/all_to_all | solution.py:127
  316.5 4.3 copy.101
  320.9 8.1 %copy.102 = f32[2,96,1,4,32,64]{1,5,4,3,0,2:T(8,128)S(1)} copy(f32[2,96,1,4,32,64]{1,4,3,2,5,0:T(8,128)} %bitcast.184) | data formatting | bytes 12582912 | tf_op jit(solution)/shard_map/transpose | solution.py:128
  329.0 7.1 %multiply_subtract_fusion.2 = (f32[1,32,8192]{1,2,0:T(8,128)S(1)}, f32[1,32,8192]{1,2,0:T(8,128)}, f32[1,32,8192]{1,2,0:T(8,128)}, f32[1,32,8192]{1,2,0:T(8,128)}) fusion(f32[2,96,8192]{1,2,0:T(8,128)S(1)} %bitcast.177), kind=kLoop, calls=%fused_computation.11 | loop fusion | flops 3670016 | bytes 10485760 | tf_op jit(solution)/shard_map/sub | solution.py:144
  336.1 4.4 multiply_subtract_fusion
  340.5 10.0 %maximum_maximum_fusion = f32[2,96,8192]{1,2,0:T(8,128)S(1)} fusion(f32[1,32,8192]{1,2,0:T(8,128)} %get-tuple-element.11, f32[1,32,8192]{1,2,0:T(8,128)} %get-tuple-element.10, f32[1,32,8192]{1,2,0:T(8,128)} %get-tuple-element.8, f32[1,32,8192]{1,2,0:T(8,128)} %get-tuple-element.7, f32[1,32,8192]{1,2,0:T(8,128)} %get-tuple-element.9, ...), kind=kLoop, calls=%fused_computation.1 | loop fusion | flops 7864320 | bytes 12582912 | tf_op jit(solution)/shard_map/concatenate | solution.py:164
  350.5 8.1 %copy.103 = f32[2,96,64,32,1,4]{1,3,5,0,4,2:T(8,128)} copy(f32[2,96,64,32,1,4]{1,2,3,5,0,4:T(8,128)S(1)} %bitcast.185) | data formatting | bytes 12582912 | tf_op jit(solution)/shard_map/reshape | solution.py:135
  358.6 9.3 %all-to-all-start.3 = ((f32[2,96,64,32,1,4]{1,3,5,0,4,2:T(8,128)}), f32[2,96,64,32,1,4]{1,3,5,0,4,2:T(8,128)}, u32[]{:S(2)}, u32[]{:S(2)}) async-start(f32[2,96,64,32,1,4]{1,3,5,0,4,2:T(8,128)} %copy.103), calls=%async_computation.3 | async-start | bytes 16777216 | tf_op jit(solution)/shard_map/all_to_all | solution.py:138
  368.3 111.0 %all-to-all-done.3 = f32[2,96,64,32,1,4]{1,3,5,0,4,2:T(8,128)} async-done(((f32[2,96,64,32,1,4]{1,3,5,0,4,2:T(8,128)}), f32[2,96,64,32,1,4]{1,3,5,0,4,2:T(8,128)}, u32[]{:S(2)}, u32[]{:S(2)}) %all-to-all-start.3) | async-done | bytes 6291488 | tf_op jit(solution)/shard_map/all_to_all | solution.py:138
  479.3 4.4 copy.104
  489.6 4.6 copy.108
  494.2 4.5 fusion.42
  501.2 6.0 copy.106
  507.2 5.0 fusion.44
  527.5 3.8 fusion.1
  532.1 7.7 %copy.111 = f32[2,96,2,32,128]{4,2,1,0,3:T(2,128)} copy(f32[2,96,2,32,128]{4,3,2,1,0:T(8,128)S(1)} %pad_maximum_fusion.2) | data formatting | bytes 12582912 | tf_op jit(solution)/shard_map/stack | solution.py:104
  539.8 87.3 %all_to_all.78 = f32[2,96,2,32,128]{4,2,1,0,3:T(2,128)S(1)} all-to-all(f32[2,96,2,32,128]{4,2,1,0,3:T(2,128)} %copy.111), channel_id=1, replica_groups=mesh['seq'=32,'chan'=4] {'seq'}, dimensions={3} | all-to-all | bytes 12582912 | tf_op jit(solution)/shard_map/all_to_all | solution.py:105
  636.7 29.7 %all_to_all.79 = f32[96,1,32,128]{3,0,1,2:T(8,128)S(1)} all-to-all(f32[96,1,32,128]{3,0,1,2:T(8,128)S(1)} %copy.115), channel_id=1, replica_groups=mesh['seq'=32,'chan'=4] {'seq'}, dimensions={2} | all-to-all | bytes 3145728 | tf_op jit(solution)/shard_map/all_to_all | solution.py:112
  670.9 14.9 %reduce-scatter.2.cloned.1.call-done = f32[8,4096]{1,0:T(8,128)} async-done(((f32[32,4096]{1,0:T(8,128)}), f32[8,4096]{1,0:T(8,128)}) %reduce-scatter.2.cloned.1.call-update) | async-done | bytes 131088 | tf_op jit(solution)/shard_map/reduce_scatter | solution.py:180
  (56 shorter events, 66.2 us)
Async XLA Ops:
  10.9 33.9 %all-to-all-start = ((f32[96,32,128]{2,0,1:T(8,128)}), f32[96,32,128]{2,0,1:T(8,128)S(1)}, u32[]{:S(2)}, u32[]{:S(2)}) async-start(f32[96,32,128]{2,0,1:T(8,128)} %copy_bitcast_fusion.2), calls=%async_computation | async-start | bytes 3145728 | tf_op jit(solution)/shard_map/all_to_all | solution.py:81
  60.1 87.3 %all-to-all-start.1 = ((f32[2,96,64,128]{3,1,0,2:T(8,128)}), f32[2,96,64,128]{3,1,0,2:T(8,128)}, u32[]{:S(2)}, u32[]{:S(2)}) async-start(f32[2,96,64,128]{3,1,0,2:T(8,128)} %copy.95), calls=%async_computation.1 | async-start | bytes 12582912 | tf_op jit(solution)/shard_map/all_to_all | solution.py:90
  166.3 7.8 %copy-start = (f32[32,96,2,128]{3,0,2,1:T(8,128)}, f32[32,96,2,128]{3,0,2,1:T(8,128)S(1)}, u32[]{:S(2)}) copy-start(f32[32,96,2,128]{3,0,2,1:T(8,128)S(1)} %multiply_subtract_fusion.6) | copy-start | bytes 9437188
  358.6 120.7 %all-to-all-start.3 = ((f32[2,96,64,32,1,4]{1,3,5,0,4,2:T(8,128)}), f32[2,96,64,32,1,4]{1,3,5,0,4,2:T(8,128)}, u32[]{:S(2)}, u32[]{:S(2)}) async-start(f32[2,96,64,32,1,4]{1,3,5,0,4,2:T(8,128)} %copy.103), calls=%async_computation.3 | async-start | bytes 16777216 | tf_op jit(solution)/shard_map/all_to_all | solution.py:138
  367.9 317.8 %reduce-scatter.2.cloned.1.call-start = ((), (), s32[]{:S(2)}) async-start(), calls=%async_computation.7 | async-start | bytes 655360 | tf_op jit(solution)/shard_map/reduce_scatter | solution.py:180
  494.2 4.5 copy-start.2
  507.2 5.0 copy-start.1
  507.2 5.0 copy-start.3
  666.5 1.9 copy-start.4
  666.6 3.1 copy-start.5
  666.6 3.1 copy-start.6
Sparse Core Ops, SparseCore 0:
  668.2 17.4 reduce-scatter.1
where the time goes:
time: 705 us; the launch traced here: 695 us
  blocking collectives  230 us (33%)
  waiting for transfers between devices  229 us (32%)
  local copies, waits for them, and re-layouts  81.9 us (12%)
  matrix products  75.3 us (11%)
  other arithmetic  35.9 us (5%)
  starting transfers between devices  27.2 us (4%)
  between operations  14.8 us (2%)
    all_to_all x1, blocking collectives, to_natural(): lax.all_to_all(shaped, 'seq', split_axis=4, concat_axis=2, tiled=True)  113 us
    all_to_all x1, waiting for transfers between devices, from_natural(): lax.all_to_all(shaped, 'seq', split_axis=2, concat_axis=4, tiled=True)  111 us
    all_to_all x1, blocking collectives, inverse_signal(): lax.all_to_all(stacked, 'seq', split_axis=3, concat_axis=2, tiled=True)  87.3 us
    all_to_all x1, waiting for transfers between devices, forward_spectra(): lax.all_to_all(mixed, 'seq', split_axis=2, concat_axis=3, tiled=True)  80.7 us
    all_to_all x1, blocking collectives, inverse_signal(): lax.all_to_all(row_blocks, 'seq', split_axis=2, concat_axis=3, tiled=True)  29.7 us
    all_to_all x1, waiting for transfers between devices, forward_spectra(): lax.all_to_all(split_rows, 'seq', split_axis=1, concat_axis=1, tiled=True)  22.4 us
    dot_general x4, matrix products, complex_apply(): real_cos = jnp.einsum(form, real_part, cos_table, precision=PRECISE)  16.2 us
    dot_general x4, matrix products, complex_apply(): imag_cos = jnp.einsum(form, imag_part, cos_table, precision=PRECISE)  15.7 us
  transfers between devices with their start and end apart: 4, of which 4 were waited for; matrix products, arithmetic and copies ran while one was open for 0% of the time, Pallas kernels for 0%

commit v1 on v0

v1 whole, which is shorter than its diff:
```python
import math

import jax
import jax.numpy as jnp
import ml_dtypes
import numpy as np
from jax import lax
from jax.experimental import pallas as pl
from jax.experimental.pallas import tpu as pltpu
from jax.sharding import PartitionSpec as P

F32 = jnp.float32
BF16 = jnp.bfloat16
OUTER = 8
MIDDLE = 128
INNER = 128
SIGNALS = 3
VMEM_BYTES = 48 * 1024 * 1024


def halves(table):
    table = table.astype(np.float32)
    high = table.astype(ml_dtypes.bfloat16)
    low = (table - high.astype(np.float32)).astype(ml_dtypes.bfloat16)
    return high, low


def tables(scale):
    rows = OUTER * MIDDLE
    length = rows * INNER
    j = np.arange(OUTER)[:, None, None]
    k0 = np.arange(MIDDLE)[None, :, None]
    m0 = np.arange(MIDDLE)[None, None, :]
    angle = 2.0 * np.pi * m0 * (j + OUTER * k0 + 0.25) / rows
    cos, sin = np.cos(angle), np.sin(angle)
    mid = np.concatenate(
        [np.concatenate([cos, sin], axis=2), np.concatenate([-sin, cos], axis=2)], axis=1
    )
    mid_back = mid.transpose(0, 2, 1)
    l = np.arange(INNER)
    turn = 2.0 * np.pi * l[None, None, :] * (j + OUTER * k0 + 0.25) / length
    turn_table = np.stack([np.cos(turn), np.sin(turn)], axis=1).astype(np.float32)
    angle = 2.0 * np.pi * ((l[:, None] * l[None, :]) % INNER) / INNER
    cos, sin = np.cos(angle), np.sin(angle)
    last = np.concatenate(
        [np.concatenate([cos, -sin], axis=1), np.concatenate([sin, cos], axis=1)], axis=0
    )
    last_back = last.T * scale
    return (
        np.stack(halves(mid), axis=1),
        np.stack(halves(mid_back), axis=1),
        turn_table,
        np.stack(halves(last), axis=0),
        np.stack(halves(last_back), axis=0),
    )


def times(pair, cos, sin):
    return pair[0] * cos - pair[1] * sin, pair[1] * cos + pair[0] * sin


def add(first, second):
    return first[0] + second[0], first[1] + second[1]


def sub(first, second):
    return first[0] - second[0], first[1] - second[1]


def quarter(pair, sign):
    return (-pair[1], pair[0]) if sign > 0 else (pair[1], -pair[0])


def eighth(pair, sign):
    root = math.sqrt(0.5)
    if sign > 0:
        return (pair[0] - pair[1]) * root, (pair[0] + pair[1]) * root
    return (pair[0] + pair[1]) * root, (pair[1] - pair[0]) * root


def four_point(z, sign):
    s0, d0 = add(z[0], z[2]), sub(z[0], z[2])
    s1, d1 = add(z[1], z[3]), quarter(sub(z[1], z[3]), sign)
    return [add(s0, s1), add(d0, d1), sub(s0, s1), sub(d0, d1)]


def eight_point(z, sign):
    even = four_point([add(z[b], z[b + 4]) for b in range(4)], sign)
    odd = [sub(z[b], z[b + 4]) for b in range(4)]
    odd[1] = eighth(odd[1], sign)
    odd[2] = quarter(odd[2], sign)
    odd[3] = quarter(eighth(odd[3], sign), sign)
    odd = four_point(odd, sign)
    return [even[0], odd[0], even[1], odd[1], even[2], odd[2], even[3], odd[3]]


def split(value):
    high = value.astype(BF16)
    return high, (value - high.astype(F32)).astype(BF16)


def dot(first, second):
    return jnp.dot(first, second, preferred_element_type=F32)


def table_first(table, data):
    high, low = split(data)
    return dot(table[0], high) + dot(table[0], low) + dot(table[1], high)


def table_last(data, table):
    high, low = split(data)
    return dot(high, table[0]) + dot(low, table[0]) + dot(high, table[1])


def convolve_kernel(
    x_ref, mid_ref, mid_back_ref, turn_ref, last_ref, last_back_ref, y_ref, first_ref, final_ref
):
    blocks, _, block_rows, _ = x_ref.shape
    per = blocks // OUTER
    chunk = 16
    shift = [(math.cos(math.pi * b / 16), math.sin(math.pi * b / 16)) for b in range(OUTER)]

    def opening(step, carry):
        row = step * chunk
        inner_block = row // block_rows
        start = pl.multiple_of(row % block_rows, chunk)
        row = pl.multiple_of(row, chunk)
        for a in range(SIGNALS):
            z = []
            for b in range(OUTER):
                value = x_ref[b * per + inner_block, a, pl.ds(start, chunk), :]
                cos, sin = shift[b]
                z.append((value * cos, value * (-sin)))
            z = eight_point(z, -1)
            for j in range(OUTER):
                for part in range(2):
                    high, low = split(z[j][part])
                    columns = slice(a * INNER, (a + 1) * INNER)
                    first_ref[j, 0, pl.ds(part * MIDDLE + row, chunk), columns] = high
                    first_ref[j, 1, pl.ds(part * MIDDLE + row, chunk), columns] = low
        return carry

    lax.fori_loop(0, MIDDLE // chunk, opening, 0)

    last = (last_ref[0], last_ref[1])
    last_back = (last_back_ref[0], last_back_ref[1])

    def body(j, carry):
        high, low = first_ref[j, 0], first_ref[j, 1]
        table = (mid_ref[j, 0], mid_ref[j, 1])
        mixed = dot(table[0], high) + dot(table[0], low) + dot(table[1], high)
        cos, sin = turn_ref[j, 0], turn_ref[j, 1]
        spectra = []
        for a in range(SIGNALS):
            columns = slice(a * INNER, (a + 1) * INNER)
            real, imag = times((mixed[:MIDDLE, columns], mixed[MIDDLE:, columns]), cos, -sin)
            out = table_last(jnp.concatenate([real, imag], axis=1), last)
            spectra.append((out[:, :INNER], out[:, INNER:]))
        gated, carried, filters = spectra
        products = (
            times(gated, filters[0], filters[1]),
            times(carried, filters[0], -filters[1]),
            times(carried, gated[0], -gated[1]),
        )
        reals, imags = [], []
        for a in range(SIGNALS):
            out = table_last(jnp.concatenate(products[a], axis=1), last_back)
            real, imag = times((out[:, :INNER], out[:, INNER:]), cos, sin)
            reals.append(real)
            imags.append(imag)
        stacked = jnp.concatenate(
            [jnp.concatenate(reals, axis=1), jnp.concatenate(imags, axis=1)], axis=0
        )
        final_ref[j] = table_first((mid_back_ref[j, 0], mid_back_ref[j, 1]), stacked)
        return carry

    lax.fori_loop(0, OUTER, body, 0)

    rows = 8

    def closing(step, carry):
        row = step * rows
        inner_block = row // block_rows
        start = pl.multiple_of(row % block_rows, rows)
        row = pl.multiple_of(row, rows)
        for a in range(SIGNALS):
            columns = slice(a * INNER, (a + 1) * INNER)
            z = [
                (
                    final_ref[j, pl.ds(row, rows), columns],
                    final_ref[j, pl.ds(MIDDLE + row, rows), columns],
                )
                for j in range(OUTER)
            ]
            z = eight_point(z, 1)
            for b in range(OUTER):
                cos, sin = shift[b]
                y_ref[b * per + inner_block, a, pl.ds(start, rows), :] = z[b][0] * cos - z[b][1] * sin
        return carry

    lax.fori_loop(0, MIDDLE // rows, closing, 0)


def in_vmem(count):
    return [pl.BlockSpec(memory_space=pltpu.VMEM)] * count


def convolve(received, scale):
    constants = [jnp.asarray(table) for table in tables(scale)]
    return pl.pallas_call(
        convolve_kernel,
        out_shape=jax.ShapeDtypeStruct(received.shape, F32),
        in_specs=in_vmem(6),
        out_specs=pl.BlockSpec(memory_space=pltpu.VMEM),
        scratch_shapes=[
            pltpu.VMEM((OUTER, 2, 2 * MIDDLE, SIGNALS * INNER), BF16),
            pltpu.VMEM((OUTER, 2 * MIDDLE, SIGNALS * INNER), F32),
        ],
        compiler_params=pltpu.CompilerParams(vmem_limit_bytes=VMEM_BYTES),
        name="convolve",
    )(received, *constants)


def shards(query_proj, key_proj, value_proj, out_cotangent, filter_raw):
    slab, width = query_proj.shape
    parts = lax.axis_size("seq")
    length = parts * width
    scale = 1.0 / (length * math.sqrt(length))
    key_float = key_proj.astype(F32)
    value_float = value_proj.astype(F32)
    cotangent_float = out_cotangent.astype(F32)
    gated = key_float * value_float
    carried = query_proj.astype(F32) * cotangent_float
    sent = jnp.stack([gated, carried, filter_raw], axis=1)
    sent = sent.reshape(slab, SIGNALS, width // INNER, INNER)
    received = lax.all_to_all(sent, "seq", split_axis=0, concat_axis=0, tiled=True)
    signals = convolve(received, scale)
    back = lax.all_to_all(signals, "seq", split_axis=0, concat_axis=0, tiled=True)
    filter_grad = lax.psum_scatter(back[:, 2], "chan", scatter_dimension=0, tiled=True)
    conv_out = back[:, 0].reshape(slab, width)
    adjoint = back[:, 1].reshape(slab, width)
    query_grad = (conv_out * cotangent_float).astype(BF16)
    key_grad = (adjoint * value_float).astype(BF16)
    value_grad = (adjoint * key_float).astype(BF16)
    return (query_grad, key_grad, value_grad, filter_grad.reshape(-1, width))


def solution(mesh):
    placed = (
        P("chan", "seq"),
        P("chan", "seq"),
        P("chan", "seq"),
        P("chan", "seq"),
        P(None, "seq"),
    )
    return jax.shard_map(
        shards,
        mesh=mesh,
        in_specs=placed,
        out_specs=(P("chan", "seq"), P("chan", "seq"), P("chan", "seq"), P("chan", "seq")),
        check_vma=False,
    )
```

time: 705 us -> 112 us (0.16); the launches traced: 695 us -> 112 us
  waiting for transfers between devices: 229 us -> 15.9 us
  blocking collectives: 230 us -> 61.1 us
  local copies, waits for them, and re-layouts: 81.9 us -> 2.91 us
  matrix products: 75.3 us -> 0 us
  other arithmetic: 35.9 us -> 2.82 us
  starting transfers between devices: 27.2 us -> 0.04 us
  Pallas kernels: 0 us -> 14.9 us
    all_to_all x3 -> x0, waiting for transfers between devices: 214 us -> none  [the longest x1 111 us: from_natural(): lax.all_to_all(shaped, 'seq', split_axis=2, concat_axis=4, tiled=True)]
    all_to_all x3 -> x2, blocking collectives: 230 us -> 61.1 us  [the longest x1 33.8 us: shards(): lax.all_to_all(sent, 'seq', split_axis=0, concat_axis=0, tiled=True)]
    dot_general x20 -> x0, matrix products: 75.3 us -> none  [the longest x4 16.2 us: complex_apply(): real_cos = jnp.einsum(form, real_part, cos_table, precision=PRECISE)]
    all_to_all x3 -> x0, starting transfers between devices: 27.2 us -> none  [the longest x1 11.3 us: forward_spectra(): lax.all_to_all(split_rows, 'seq', split_axis=1, concat_axis=1, tiled=True)]
    all_to_all x4 -> x0, local copies, waits for them, and re-layouts: 16 us -> none  [the longest x1 6.43 us: forward_spectra(): lax.all_to_all(mixed, 'seq', split_axis=2, concat_axis=3, tiled=True)]
    another operation x3 -> x0, local copies, waits for them, and re-layouts: 15.8 us -> none  [the longest x1 7.72 us: inverse_signal(): jnp.stack([real_part, imag_part]).reshape(2, channels, paired, parts, block)]
    pallas_call x0 -> x1, Pallas kernels: none -> 14.9 us  [convolve(): pl.pallas_call(convolve_kernel, out_shape=jax.ShapeDtypeStruct(received.s...]
    sub x2 -> x0, other arithmetic: 11.5 us -> none  [complex_times(): real_part = first[0] * second[0] - sign * first[1] * second[1]]
  transfers between devices with their start and end apart: 4 -> 1, of which waited for: 4 -> 1; matrix products, arithmetic and copies ran while one was open for 0% -> 1% of each run, Pallas kernels for 0% -> 0%
where the time goes in v1:
time: 112 us
  blocking collectives  61.1 us (55%)
  waiting for transfers between devices  15.9 us (14%)
  Pallas kernels  14.9 us (13%)
  between operations  14.2 us (13%)
  local copies, waits for them, and re-layouts  2.91 us (3%)
  other arithmetic  2.82 us (3%)
    all_to_all x1, blocking collectives, shards(): lax.all_to_all(sent, 'seq', split_axis=0, concat_axis=0, tiled=True)  33.8 us
    all_to_all x1, blocking collectives, shards(): lax.all_to_all(signals, 'seq', split_axis=0, concat_axis=0, tiled=True)  27.3 us
    reduce_scatter x1, waiting for transfers between devices, shards(): lax.psum_scatter(back[:, 2], 'chan', scatter_dimension=0, tiled=True)  15.9 us
    pallas_call x1, Pallas kernels, convolve(): pl.pallas_call(convolve_kernel, out_shape=jax.ShapeDtypeStruct(received.s...  14.9 us
  transfers between devices with their start and end apart: 1, of which 1 were waited for; matrix products, arithmetic and copies ran while one was open for 1% of the time, Pallas kernels for 0%

profile of v1, /device:TPU:1, one launch (start us, length us, event | category | flops | bytes accessed | tf_op | source)
XLA Modules:
  0.0 111.8 jit_solution(16691448971963149734)
XLA Ops:
  7.2 0.0 copy-start.6
  7.2 0.0 copy-start.5
  7.2 0.0 copy-start.3
  7.2 0.0 reduce-scatter.2.cloned.1.call-start
  7.2 1.2 %fusion.3 = f32[4,8,32,128]{3,1,2,0:T(8,128)S(1)} fusion(bf16[32,4096]{1,0:T(8,128)(2,1)} %param.13, bf16[32,4096]{1,0:T(8,128)(2,1)} %param.10), kind=kLoop, calls=%fused_computation.9 | loop fusion | flops 393216 | bytes 1048576
  8.4 0.1 copy.15
  8.5 0.0 copy-done.6
  8.5 0.1 copy.16
  8.6 0.0 copy-done.5
  8.6 0.0 copy-done.3
  8.6 0.1 fusion.1
  8.7 0.1 copy.14
  8.8 0.1 pad_maximum_fusion
  9.0 0.0 copy-start
  9.0 0.0 copy-start.1
  9.0 0.0 copy-start.2
  9.0 33.8 %all_to_all.10.x_ref = f32[32,3,32,128]{3,2,1,0:T(8,128)S(1)} all-to-all(f32[32,3,32,128]{3,2,1,0:T(8,128)S(1)} %pad_maximum_fusion), channel_id=1, replica_groups=mesh['seq'=32,'chan'=4] {'seq'}, dimensions={0} | all-to-all | bytes 3145728 | tf_op jit(solution)/shard_map/all_to_all | solution.py:237
  42.8 0.0 copy-done
  42.8 0.0 copy-done.1
  42.8 0.0 copy-done.2
  42.8 14.9 %convolve.1 = f32[32,3,32,128]{3,2,1,0:T(8,128)S(1)} custom-call(f32[32,3,32,128]{3,2,1,0:T(8,128)S(1)} %all_to_all.10.x_ref, bf16[8,2,256,256]{3,2,1,0:T(8,128)(2,1)} %constant.10.clone.mid_ref, bf16[8,2,256,256]{3,2,1,0:T(8,128)(2,1)} %constant.11.clone.mid_back_ref, f32[8,2,128,128]{3,2,1,0:T(8,128)S(1)} %copy-done, bf16[2,256,256]{2,1,0:T(8,128)(2,1)S(1)} %copy-done.2, ...), custom_call_target="tpu_custom_call" | custom-call | tf_op jit(solution)/shard_map/convolve/pallas_call | solution.py:211
  57.7 27.3 %all_to_all.11 = f32[32,3,32,128]{3,2,1,0:T(8,128)S(1)} all-to-all(f32[32,3,32,128]{3,2,1,0:T(8,128)S(1)} %convolve.1), channel_id=1, replica_groups=mesh['seq'=32,'chan'=4] {'seq'}, dimensions={0} | all-to-all | bytes 3145728 | tf_op jit(solution)/shard_map/all_to_all | solution.py:239
  85.0 0.0 copy-start.4
  85.0 0.9 slice_bitcast_fusion
  85.9 0.0 reduce-scatter.2.cloned.1.call-update
  86.0 0.0 copy-done.4
  86.0 1.5 %fusion = (bf16[32,4096]{1,0:T(8,128)(2,1)}, bf16[32,4096]{1,0:T(8,128)(2,1)}, bf16[32,4096]{1,0:T(8,128)(2,1)}) fusion(bf16[32,4096]{1,0:T(8,128)(2,1)S(1)} %copy-done.3, f32[4,8,32,128]{3,2,1,0:T(8,128)S(1)} %bitcast.26, bf16[32,4096]{1,0:T(8,128)(2,1)S(1)} %copy-done.5, bf16[32,4096]{1,0:T(8,128)(2,1)S(1)} %copy-done.4, f32[4,8,32,128]{3,2,1,0:T(8,128)S(1)} %bitcast.27), kind=kLoop, calls=%fused_computation.6 | loop fusion | flops 1179648 | bytes 2621440 | tf_op jit(solution)/shard_map/convert_element_type | solution.py:245
  87.4 15.9 %reduce-scatter.2.cloned.1.call-done = f32[8,32,128]{2,1,0:T(8,128)} async-done(((f32[32,32,128]{2,1,0:T(8,128)}), f32[8,32,128]{2,1,0:T(8,128)}) %reduce-scatter.2.cloned.1.call-update) | async-done | bytes 131088 | tf_op jit(solution)/shard_map/reduce_scatter | solution.py:240
  103.3 1.6 %copy.24 = f32[1,8,32,128]{3,1,2,0:T(8,128)} copy(f32[1,8,32,128]{3,2,1,0:T(8,128)} %bitcast.32) | data formatting | bytes 262144
Async XLA Ops:
  7.2 1.3 %copy-start.6 = (f32[32,4096]{1,0:T(8,128)S(1)}, f32[32,4096]{1,0:T(8,128)}, u32[]{:S(2)}) copy-start(f32[32,4096]{1,0:T(8,128)} %param.14) | copy-start | bytes 1572868
  7.2 1.4 %copy-start.5 = (bf16[32,4096]{1,0:T(8,128)(2,1)S(1)}, bf16[32,4096]{1,0:T(8,128)(2,1)}, u32[]{:S(2)}) copy-start(bf16[32,4096]{1,0:T(8,128)(2,1)} %param.12) | copy-start | bytes 786436
  7.2 1.4 %copy-start.3 = (bf16[32,4096]{1,0:T(8,128)(2,1)S(1)}, bf16[32,4096]{1,0:T(8,128)(2,1)}, u32[]{:S(2)}) copy-start(bf16[32,4096]{1,0:T(8,128)(2,1)} %param.11) | copy-start | bytes 786436
  7.2 96.1 %reduce-scatter.2.cloned.1.call-start = ((), (), s32[]{:S(2)}) async-start(), calls=%async_computation.3 | async-start | bytes 655360 | tf_op jit(solution)/shard_map/reduce_scatter | solution.py:240
  9.0 33.9 %copy-start = (f32[8,2,128,128]{3,2,1,0:T(8,128)S(1)}, f32[8,2,128,128]{3,2,1,0:T(8,128)}, u32[]{:S(2)}) copy-start(f32[8,2,128,128]{3,2,1,0:T(8,128)} %constant.12.clone.turn_ref) | copy-start | bytes 3145732
  9.0 33.8 %copy-start.1 = (bf16[2,256,256]{2,1,0:T(8,128)(2,1)S(1)}, bf16[2,256,256]{2,1,0:T(8,128)(2,1)}, u32[]{:S(2)}) copy-start(bf16[2,256,256]{2,1,0:T(8,128)(2,1)} %constant.14.clone.last_back_ref) | copy-start | bytes 786436
  9.0 33.8 %copy-start.2 = (bf16[2,256,256]{2,1,0:T(8,128)(2,1)S(1)}, bf16[2,256,256]{2,1,0:T(8,128)(2,1)}, u32[]{:S(2)}) copy-start(bf16[2,256,256]{2,1,0:T(8,128)(2,1)} %constant.13.clone.last_ref) | copy-start | bytes 786436
  85.0 1.0 copy-start.4
Sparse Core Ops, SparseCore 0:
  86.1 17.1 reduce-scatter.1

commit v2 on v1

--- a/solution.py
+++ b/solution.py
@@ -237,7 +237,10 @@
     received = lax.all_to_all(sent, "seq", split_axis=0, concat_axis=0, tiled=True)
     signals = convolve(received, scale)
     back = lax.all_to_all(signals, "seq", split_axis=0, concat_axis=0, tiled=True)
-    filter_grad = lax.psum_scatter(back[:, 2], "chan", scatter_dimension=0, tiled=True)
+    groups = lax.axis_size("chan")
+    rows = back[:, 2].reshape(groups, slab // groups, width // INNER, INNER)
+    rows = lax.all_to_all(rows, "chan", split_axis=0, concat_axis=0, tiled=True)
+    filter_grad = jnp.sum(rows, axis=0)
     conv_out = back[:, 0].reshape(slab, width)
     adjoint = back[:, 1].reshape(slab, width)
     query_grad = (conv_out * cotangent_float).astype(BF16)

time: 112 us -> 95.1 us (0.85)
  between operations: 14.2 us -> 0.76 us
  waiting for transfers between devices: 15.9 us -> 6.52 us
  starting transfers between devices: 0.04 us -> 6.71 us
    reduce_scatter x1 -> x0, waiting for transfers between devices: 15.9 us -> none  [shards(): lax.psum_scatter(back[:, 2], 'chan', scatter_dimension=0, tiled=True)]
    all_to_all x0 -> x1, starting transfers between devices: none -> 6.71 us  [shards(): rows = lax.all_to_all(rows, 'chan', split_axis=0, concat_axis=0, tiled=True)]
    all_to_all x0 -> x1, waiting for transfers between devices: none -> 6.52 us  [shards(): rows = lax.all_to_all(rows, 'chan', split_axis=0, concat_axis=0, tiled=True)]
  transfers between devices with their start and end apart: 1 -> 1, of which waited for: 1 -> 1; matrix products, arithmetic and copies ran while one was open for 1% -> 2% of each run, Pallas kernels for 0% -> 0%
where the time goes in v2:
time: 95.1 us; the launch traced here: 94.8 us
  blocking collectives  61.1 us (64%)
  Pallas kernels  14.9 us (16%)
  starting transfers between devices  6.71 us (7%)
  waiting for transfers between devices  6.52 us (7%)
  other arithmetic  2.86 us (3%)
  local copies, waits for them, and re-layouts  2.01 us (2%)
    all_to_all x1, blocking collectives, shards(): lax.all_to_all(sent, 'seq', split_axis=0, concat_axis=0, tiled=True)  33.8 us
    all_to_all x1, blocking collectives, shards(): lax.all_to_all(signals, 'seq', split_axis=0, concat_axis=0, tiled=True)  27.3 us
    pallas_call x1, Pallas kernels, convolve(): pl.pallas_call(convolve_kernel, out_shape=jax.ShapeDtypeStruct(received.s...  14.9 us
    all_to_all x1, starting transfers between devices, shards(): rows = lax.all_to_all(rows, 'chan', split_axis=0, concat_axis=0, tiled=True)  6.71 us
    all_to_all x1, waiting for transfers between devices, shards(): rows = lax.all_to_all(rows, 'chan', split_axis=0, concat_axis=0, tiled=True)  6.52 us
  transfers between devices with their start and end apart: 1, of which 1 were waited for; matrix products, arithmetic and copies ran while one was open for 2% of the time, Pallas kernels for 0%

profile of v2, /device:TPU:1, one launch (start us, length us, event | category | flops | bytes accessed | tf_op | source)
XLA Modules:
  0.0 94.8 jit_solution(14653546480300009360)
XLA Ops:
  0.6 0.0 copy-start.6
  0.6 0.0 copy-start.5
  0.7 0.0 copy-start.3
  0.7 1.2 %fusion.3 = f32[4,8,32,128]{3,1,2,0:T(8,128)S(1)} fusion(bf16[32,4096]{1,0:T(8,128)(2,1)} %param.13, bf16[32,4096]{1,0:T(8,128)(2,1)} %param.10), kind=kLoop, calls=%fused_computation.9 | loop fusion | flops 393216 | bytes 1048576
  1.8 0.1 copy.15
  1.9 0.0 copy-done.6
  1.9 0.1 copy.16
  2.0 0.0 copy-done.5
  2.1 0.0 copy-done.3
  2.1 0.1 fusion.1
  2.1 0.1 copy.14
  2.2 0.1 pad_maximum_fusion
  2.4 0.0 copy-start
  2.4 0.0 copy-start.1
  2.4 0.0 copy-start.2
  2.4 33.8 %all_to_all.15.x_ref = f32[32,3,32,128]{3,2,1,0:T(8,128)S(1)} all-to-all(f32[32,3,32,128]{3,2,1,0:T(8,128)S(1)} %pad_maximum_fusion), channel_id=1, replica_groups=mesh['seq'=32,'chan'=4] {'seq'}, dimensions={0} | all-to-all | bytes 3145728 | tf_op jit(solution)/shard_map/all_to_all | solution.py:237
  36.2 0.0 copy-done
  36.3 0.0 copy-done.1
  36.3 0.0 copy-done.2
  36.3 14.9 %convolve.1 = f32[32,3,32,128]{3,2,1,0:T(8,128)S(1)} custom-call(f32[32,3,32,128]{3,2,1,0:T(8,128)S(1)} %all_to_all.15.x_ref, bf16[8,2,256,256]{3,2,1,0:T(8,128)(2,1)} %constant.12.clone.mid_ref, bf16[8,2,256,256]{3,2,1,0:T(8,128)(2,1)} %constant.13.clone.mid_back_ref, f32[8,2,128,128]{3,2,1,0:T(8,128)S(1)} %copy-done, bf16[2,256,256]{2,1,0:T(8,128)(2,1)S(1)} %copy-done.2, ...), custom_call_target="tpu_custom_call" | custom-call | tf_op jit(solution)/shard_map/convolve/pallas_call | solution.py:211
  51.1 27.3 %all_to_all.16 = f32[32,3,32,128]{3,2,1,0:T(8,128)S(1)} all-to-all(f32[32,3,32,128]{3,2,1,0:T(8,128)S(1)} %convolve.1), channel_id=1, replica_groups=mesh['seq'=32,'chan'=4] {'seq'}, dimensions={0} | all-to-all | bytes 3145728 | tf_op jit(solution)/shard_map/all_to_all | solution.py:239
  78.4 0.0 copy-start.4
  78.4 1.0 %fusion.5 = (f32[32,1,32,128]{3,2,1,0:T(8,128)}, f32[32,1,32,128]{3,2,1,0:T(8,128)S(1)}, f32[32,1,32,128]{3,2,1,0:T(8,128)S(1)}) fusion(f32[32,3,32,128]{3,2,1,0:T(8,128)S(1)} %all_to_all.16), kind=kLoop, calls=%fused_computation.12 | loop fusion | bytes 3145728 | tf_op jit(solution)/shard_map/slice | solution.py:241
  79.4 6.7 %all-to-all-start.2 = ((f32[4,8,32,128]{3,2,1,0:T(8,128)}), f32[4,8,32,128]{3,2,1,0:T(8,128)S(1)}, u32[]{:S(2)}, u32[]{:S(2)}) async-start(f32[4,8,32,128]{3,2,1,0:T(8,128)} %bitcast), calls=%async_computation.2 | async-start | bytes 1048576 | tf_op jit(solution)/shard_map/all_to_all | solution.py:242
  86.1 0.0 copy-done.4
  86.1 1.5 %fusion = (bf16[32,4096]{1,0:T(8,128)(2,1)}, bf16[32,4096]{1,0:T(8,128)(2,1)}, bf16[32,4096]{1,0:T(8,128)(2,1)}) fusion(bf16[32,4096]{1,0:T(8,128)(2,1)S(1)} %copy-done.3, f32[4,8,32,128]{3,2,1,0:T(8,128)S(1)} %bitcast.25, bf16[32,4096]{1,0:T(8,128)(2,1)S(1)} %copy-done.5, bf16[32,4096]{1,0:T(8,128)(2,1)S(1)} %copy-done.4, f32[4,8,32,128]{3,2,1,0:T(8,128)S(1)} %bitcast.26), kind=kLoop, calls=%fused_computation.6 | loop fusion | flops 1179648 | bytes 2621440 | tf_op jit(solution)/shard_map/convert_element_type | solution.py:248
  87.5 6.5 %all-to-all-done.2 = f32[4,8,32,128]{3,2,1,0:T(8,128)S(1)} async-done(((f32[4,8,32,128]{3,2,1,0:T(8,128)}), f32[4,8,32,128]{3,2,1,0:T(8,128)S(1)}, u32[]{:S(2)}, u32[]{:S(2)}) %all-to-all-start.2) | async-done | bytes 524320 | tf_op jit(solution)/shard_map/all_to_all | solution.py:242
  94.1 0.7 copy.24
  (1 shorter events, 0.0 us)
Async XLA Ops:
  0.6 1.3 %copy-start.6 = (f32[32,4096]{1,0:T(8,128)S(1)}, f32[32,4096]{1,0:T(8,128)}, u32[]{:S(2)}) copy-start(f32[32,4096]{1,0:T(8,128)} %param.14) | copy-start | bytes 1572868
  0.6 1.4 %copy-start.5 = (bf16[32,4096]{1,0:T(8,128)(2,1)S(1)}, bf16[32,4096]{1,0:T(8,128)(2,1)}, u32[]{:S(2)}) copy-start(bf16[32,4096]{1,0:T(8,128)(2,1)} %param.12) | copy-start | bytes 786436
  0.7 1.4 %copy-start.3 = (bf16[32,4096]{1,0:T(8,128)(2,1)S(1)}, bf16[32,4096]{1,0:T(8,128)(2,1)}, u32[]{:S(2)}) copy-start(bf16[32,4096]{1,0:T(8,128)(2,1)} %param.11) | copy-start | bytes 786436
  2.4 33.9 %copy-start = (f32[8,2,128,128]{3,2,1,0:T(8,128)S(1)}, f32[8,2,128,128]{3,2,1,0:T(8,128)}, u32[]{:S(2)}) copy-start(f32[8,2,128,128]{3,2,1,0:T(8,128)} %constant.14.clone.turn_ref) | copy-start | bytes 3145732
  2.4 33.8 %copy-start.1 = (bf16[2,256,256]{2,1,0:T(8,128)(2,1)S(1)}, bf16[2,256,256]{2,1,0:T(8,128)(2,1)}, u32[]{:S(2)}) copy-start(bf16[2,256,256]{2,1,0:T(8,128)(2,1)} %constant.16.clone.last_back_ref) | copy-start | bytes 786436
  2.4 33.8 %copy-start.2 = (bf16[2,256,256]{2,1,0:T(8,128)(2,1)S(1)}, bf16[2,256,256]{2,1,0:T(8,128)(2,1)}, u32[]{:S(2)}) copy-start(bf16[2,256,256]{2,1,0:T(8,128)(2,1)} %constant.15.clone.last_ref) | copy-start | bytes 786436
  78.4 7.7 %copy-start.4 = (bf16[32,4096]{1,0:T(8,128)(2,1)S(1)}, bf16[32,4096]{1,0:T(8,128)(2,1)}, u32[]{:S(2)}) copy-start(bf16[32,4096]{1,0:T(8,128)(2,1)} %param.13) | copy-start | bytes 786436
  79.4 14.7 %all-to-all-start.2 = ((f32[4,8,32,128]{3,2,1,0:T(8,128)}), f32[4,8,32,128]{3,2,1,0:T(8,128)S(1)}, u32[]{:S(2)}, u32[]{:S(2)}) async-start(f32[4,8,32,128]{3,2,1,0:T(8,128)} %bitcast), calls=%async_computation.2 | async-start | bytes 1048576 | tf_op jit(solution)/shard_map/all_to_all | solution.py:242

commit v3 on v1

v3 whole, which is shorter than its diff:
```python
import math

import jax
import jax.numpy as jnp
import ml_dtypes
import numpy as np
from jax import lax
from jax.experimental import pallas as pl
from jax.experimental.pallas import tpu as pltpu
from jax.sharding import PartitionSpec as P

F32 = jnp.float32
BF16 = jnp.bfloat16
SIGNALS = 3
ROWS = 256
TURNS = 4
INNER = 128
CHUNK = 16
VMEM_BYTES = 28 * 1024 * 1024


def halves(table):
    table = table.astype(np.float32)
    high = table.astype(ml_dtypes.bfloat16)
    low = (table - high.astype(np.float32)).astype(ml_dtypes.bfloat16)
    return np.stack([high, low])


def tables(scale):
    width = TURNS * INNER
    k = np.arange(ROWS)[:, None] + 0.25
    angle = 2.0 * np.pi * k * np.arange(ROWS)[None, :] / ROWS
    first = np.concatenate([np.cos(angle), -np.sin(angle)], axis=0)
    turn = 2.0 * np.pi * k * np.arange(width)[None, :] / (ROWS * width)
    turn = np.stack([np.cos(turn), np.sin(turn)]).astype(np.float32)
    l = np.arange(INNER)
    lasts = []
    for j in range(TURNS):
        angle = 2.0 * np.pi * (l[:, None] * (j + TURNS * l[None, :]) % width) / width
        cos, sin = np.cos(angle), np.sin(angle)
        lasts.append(
            np.concatenate(
                [np.concatenate([cos, -sin], axis=1), np.concatenate([sin, cos], axis=1)], axis=0
            )
        )
    last = np.stack(lasts)
    return (
        halves(first),
        halves(first.T),
        turn,
        halves(last),
        halves(last.transpose(0, 2, 1) * scale),
    )


def times(pair, cos, sin):
    return pair[0] * cos - pair[1] * sin, pair[1] * cos + pair[0] * sin


def add(first, second):
    return first[0] + second[0], first[1] + second[1]


def sub(first, second):
    return first[0] - second[0], first[1] - second[1]


def quarter(pair, sign):
    return (-pair[1], pair[0]) if sign > 0 else (pair[1], -pair[0])


def four_point(z, sign):
    s0, d0 = add(z[0], z[2]), sub(z[0], z[2])
    s1, d1 = add(z[1], z[3]), sub(z[1], z[3])
    if sign > 0:
        return [
            add(s0, s1),
            (d0[0] - d1[1], d0[1] + d1[0]),
            sub(s0, s1),
            (d0[0] + d1[1], d0[1] - d1[0]),
        ]
    return [
        add(s0, s1),
        (d0[0] + d1[1], d0[1] - d1[0]),
        sub(s0, s1),
        (d0[0] - d1[1], d0[1] + d1[0]),
    ]


def split(value):
    high = value.astype(BF16)
    return high, (value - high.astype(F32)).astype(BF16)


def dot(first, second):
    return jnp.dot(first, second, preferred_element_type=F32)


def lanes(index):
    return slice(index * INNER, (index + 1) * INNER)


def convolve_kernel(
    x_ref,
    first_ref,
    first_back_ref,
    turn_ref,
    last_ref,
    last_back_ref,
    y_ref,
    mixed_ref,
    z_ref,
    spectra_ref,
    product_ref,
    u_ref,
    v_ref,
):
    blocks, _, _, block_rows, _ = x_ref.shape
    chunks = [slice(i, i + CHUNK) for i in range(0, ROWS, CHUNK)]

    for a in (2, 0, 1):
        for pair in range(TURNS // 2):
            data = jnp.concatenate(
                [x_ref[:, a, 2 * pair + p].reshape(ROWS, INNER) for p in range(2)], axis=1
            )
            high, low = split(data)
            mixed_ref[a, :, slice(2 * pair * INNER, 2 * (pair + 1) * INNER)] = (
                dot(first_ref[0], high) + dot(first_ref[0], low) + dot(first_ref[1], high)
            )
        for rows in chunks:
            imag_rows = slice(ROWS + rows.start, ROWS + rows.stop)
            z = []
            for p in range(TURNS):
                cos, sin = turn_ref[0, rows, lanes(p)], turn_ref[1, rows, lanes(p)]
                pair = (mixed_ref[a, rows, lanes(p)], mixed_ref[a, imag_rows, lanes(p)])
                z.append(times(pair, cos, -sin))
            z = four_point(z, -1)
            for j in range(TURNS):
                for part in range(2):
                    high, low = split(z[j][part])
                    z_ref[0, j, a, rows, lanes(part)] = high
                    z_ref[1, j, a, rows, lanes(part)] = low

    for j in range(TURNS):
        for a in (2, 0, 1):
            high, low = z_ref[0, j, a], z_ref[1, j, a]
            spectra_ref[j, a] = (
                dot(high, last_ref[0, j]) + dot(low, last_ref[0, j]) + dot(high, last_ref[1, j])
            )
        for rows in chunks:
            gated, carried, filters = [
                (spectra_ref[j, a, rows, lanes(0)], spectra_ref[j, a, rows, lanes(1)])
                for a in range(SIGNALS)
            ]
            products = (
                times(gated, filters[0], filters[1]),
                times(carried, filters[0], -filters[1]),
                times(carried, gated[0], -gated[1]),
            )
            for a in range(SIGNALS):
                for part in range(2):
                    product_ref[j, a, rows, lanes(part)] = products[a][part].astype(BF16)
        for a in range(SIGNALS):
            data = product_ref[j, a]
            u_ref[j, a] = dot(data, last_back_ref[0, j]) + dot(data, last_back_ref[1, j])

    for a in range(SIGNALS):
        for rows in chunks:
            imag_rows = slice(ROWS + rows.start, ROWS + rows.stop)
            z = [(u_ref[j, a, rows, lanes(0)], u_ref[j, a, rows, lanes(1)]) for j in range(TURNS)]
            z = four_point(z, 1)
            for p in range(TURNS):
                cos, sin = turn_ref[0, rows, lanes(p)], turn_ref[1, rows, lanes(p)]
                real, imag = times(z[p], cos, sin)
                v_ref[a, rows, lanes(p)] = real.astype(BF16)
                v_ref[a, imag_rows, lanes(p)] = imag.astype(BF16)
        for pair in range(TURNS // 2):
            data = v_ref[a, :, slice(2 * pair * INNER, 2 * (pair + 1) * INNER)]
            out = dot(first_back_ref[0], data) + dot(first_back_ref[1], data)
            for p in range(2):
                y_ref[:, a, 2 * pair + p] = out[:, lanes(p)].reshape(blocks, block_rows, INNER)


def in_vmem(count):
    return [pl.BlockSpec(memory_space=pltpu.VMEM)] * count


def convolve(received, scale):
    constants = [jnp.asarray(table) for table in tables(scale)]
    width = TURNS * INNER
    return pl.pallas_call(
        convolve_kernel,
        out_shape=jax.ShapeDtypeStruct(received.shape, F32),
        in_specs=in_vmem(6),
        out_specs=pl.BlockSpec(memory_space=pltpu.VMEM),
        scratch_shapes=[
            pltpu.VMEM((SIGNALS, 2 * ROWS, width), F32),
            pltpu.VMEM((2, TURNS, SIGNALS, ROWS, 2 * INNER), BF16),
            pltpu.VMEM((TURNS, SIGNALS, ROWS, 2 * INNER), F32),
            pltpu.VMEM((TURNS, SIGNALS, ROWS, 2 * INNER), BF16),
            pltpu.VMEM((TURNS, SIGNALS, ROWS, 2 * INNER), F32),
            pltpu.VMEM((SIGNALS, 2 * ROWS, width), BF16),
        ],
        compiler_params=pltpu.CompilerParams(vmem_limit_bytes=VMEM_BYTES),
        name="convolve",
    )(received, *constants)


def shards(query_proj, key_proj, value_proj, out_cotangent, filter_raw):
    slab, width = query_proj.shape
    parts = lax.axis_size("seq")
    groups = lax.axis_size("chan")
    length = parts * width
    scale = 1.0 / (length * math.sqrt(length))
    block_rows = ROWS // parts
    key_float = key_proj.astype(F32)
    value_float = value_proj.astype(F32)
    cotangent_float = out_cotangent.astype(F32)
    gated = key_float * value_float
    carried = query_proj.astype(F32) * cotangent_float
    sent = jnp.stack([gated, carried, filter_raw], axis=1)
    sent = sent.reshape(slab, SIGNALS, block_rows, TURNS, INNER).transpose(0, 1, 3, 2, 4)
    received = lax.all_to_all(sent, "seq", split_axis=0, concat_axis=0, tiled=True)
    signals = convolve(received, scale)
    back = lax.all_to_all(signals, "seq", split_axis=0, concat_axis=0, tiled=True)
    rows = back[:, 2].reshape(groups, slab // groups, TURNS, block_rows, INNER)
    rows = lax.all_to_all(rows, "chan", split_axis=0, concat_axis=0, tiled=True)
    filter_grad = jnp.sum(rows, axis=0).transpose(0, 2, 1, 3).reshape(-1, width)
    back = back.transpose(0, 1, 3, 2, 4)
    conv_out = back[:, 0].reshape(slab, width)
    adjoint = back[:, 1].reshape(slab, width)
    query_grad = (conv_out * cotangent_float).astype(BF16)
    key_grad = (adjoint * value_float).astype(BF16)
    value_grad = (adjoint * key_float).astype(BF16)
    return (query_grad, key_grad, value_grad, filter_grad)


def solution(mesh):
    placed = (
        P("chan", "seq"),
        P("chan", "seq"),
        P("chan", "seq"),
        P("chan", "seq"),
        P(None, "seq"),
    )
    return jax.shard_map(
        shards,
        mesh=mesh,
        in_specs=placed,
        out_specs=(P("chan", "seq"), P("chan", "seq"), P("chan", "seq"), P("chan", "seq")),
        check_vma=False,
    )
```

time: 112 us -> 87.8 us (0.78)
  between operations: 14.2 us -> 0.85 us
  waiting for transfers between devices: 15.9 us -> 5.89 us
  Pallas kernels: 14.9 us -> 6.09 us
  starting transfers between devices: 0.04 us -> 6.71 us
  local copies, waits for them, and re-layouts: 2.91 us -> 4.46 us
    reduce_scatter x1 -> x0, waiting for transfers between devices: 15.9 us -> none  [shards(): lax.psum_scatter(back[:, 2], 'chan', scatter_dimension=0, tiled=True)]
    pallas_call x1, Pallas kernels: 14.9 us -> 6.09 us  [convolve(): pl.pallas_call(convolve_kernel, out_shape=jax.ShapeDtypeStruct(received.s...]
    all_to_all x0 -> x1, starting transfers between devices: none -> 6.71 us  [shards(): rows = lax.all_to_all(rows, 'chan', split_axis=0, concat_axis=0, tiled=True)]
    all_to_all x0 -> x1, waiting for transfers between devices: none -> 5.89 us  [shards(): rows = lax.all_to_all(rows, 'chan', split_axis=0, concat_axis=0, tiled=True)]
    another operation x0 -> x8, local copies, waits for them, and re-layouts: none -> 1.58 us  [the longest x6 1.16 us: shards(): sent = jnp.stack([gated, carried, filter_raw], axis=1)]
    unnamed x2 -> x0, other arithmetic: 1.21 us -> none
    mul x0 -> x2, other arithmetic: none -> 1.2 us  [the longest x1 1.14 us: shards(): carried = query_proj.astype(F32) * cotangent_float]
    slice x0 -> x4, local copies, waits for them, and re-layouts: none -> 1.17 us  [the longest x1 0.83 us: shards(): rows = back[:, 2].reshape(groups, slab // groups, TURNS, block_rows, INNER)]
  transfers between devices with their start and end apart: 1 -> 1, of which waited for: 1 -> 1; matrix products, arithmetic and copies ran while one was open for 1% -> 2% of each run, Pallas kernels for 0% -> 0%
where the time goes in v3:
time: 87.8 us; the launch traced here: 87.5 us
  blocking collectives  61.2 us (70%)
  starting transfers between devices  6.71 us (8%)
  Pallas kernels  6.09 us (7%)
  waiting for transfers between devices  5.89 us (7%)
  local copies, waits for them, and re-layouts  4.46 us (5%)
  other arithmetic  2.3 us (3%)
    all_to_all x1, blocking collectives, shards(): lax.all_to_all(sent, 'seq', split_axis=0, concat_axis=0, tiled=True)  34 us
    all_to_all x1, blocking collectives, shards(): lax.all_to_all(signals, 'seq', split_axis=0, concat_axis=0, tiled=True)  27.3 us
    all_to_all x1, starting transfers between devices, shards(): rows = lax.all_to_all(rows, 'chan', split_axis=0, concat_axis=0, tiled=True)  6.71 us
    pallas_call x1, Pallas kernels, convolve(): pl.pallas_call(convolve_kernel, out_shape=jax.ShapeDtypeStruct(received.s...  6.09 us
    all_to_all x1, waiting for transfers between devices, shards(): rows = lax.all_to_all(rows, 'chan', split_axis=0, concat_axis=0, tiled=True)  5.89 us
  transfers between devices with their start and end apart: 1, of which 1 were waited for; matrix products, arithmetic and copies ran while one was open for 2% of the time, Pallas kernels for 0%

profile of v3, /device:TPU:1, one launch (start us, length us, event | category | flops | bytes accessed | tf_op | source)
XLA Modules:
  0.0 87.5 jit_solution(10564272041227983672)
XLA Ops:
  0.6 1.1 %convert_multiply_fusion.1 = f32[32,4096]{1,0:T(8,128)S(1)} fusion(bf16[32,4096]{1,0:T(8,128)(2,1)} %param.13, bf16[32,4096]{1,0:T(8,128)(2,1)} %param.10), kind=kLoop, calls=%fused_computation.2 | loop fusion | flops 393216 | bytes 1048576 | tf_op jit(solution)/shard_map/mul | solution.py:220
  1.8 0.4 stack.13
  2.1 0.0 copy-start.6
  2.2 0.0 copy-start.7
  2.2 0.4 stack.14
  2.6 0.5 copy-done.6
  3.1 0.1 copy-done.7
  3.2 0.1 convert_multiply_fusion.3
  3.2 0.4 stack.12
  3.6 0.0 copy-start.3
  3.6 0.0 copy-start.4
  3.7 0.1 maximum_bitcast_fusion
  3.8 0.0 copy-start
  3.8 0.0 copy-start.1
  3.8 0.0 copy-start.2
  3.9 34.0 %all_to_all.15.x_ref = f32[32,3,4,8,128]{4,3,2,1,0:T(8,128)S(1)} all-to-all(f32[32,3,4,8,128]{4,3,2,1,0:T(8,128)S(1)} %maximum_bitcast_fusion), channel_id=1, replica_groups=mesh['seq'=32,'chan'=4] {'seq'}, dimensions={0} | all-to-all | bytes 3145728 | tf_op jit(solution)/shard_map/all_to_all | solution.py:223
  37.8 0.0 copy-done.3
  37.8 0.0 copy-done
  37.8 6.1 %convolve.1 = f32[32,3,4,8,128]{4,3,2,1,0:T(8,128)S(1)} custom-call(f32[32,3,4,8,128]{4,3,2,1,0:T(8,128)S(1)} %all_to_all.15.x_ref, bf16[2,512,256]{2,1,0:T(8,128)(2,1)S(1)} %copy-done.4, bf16[2,256,512]{2,1,0:T(8,128)(2,1)S(1)} %copy-done.3, f32[2,256,512]{2,1,0:T(8,128)S(1)} %copy-done.2, bf16[2,4,256,256]{3,2,1,0:T(8,128)(2,1)S(1)} %copy-done.1, ...), custom_call_target="tpu_custom_call" | custom-call | tf_op jit(solution)/shard_map/convolve/pallas_call | solution.py:191
  43.9 27.3 %all_to_all.16 = f32[32,3,4,8,128]{4,3,2,1,0:T(8,128)S(1)} all-to-all(f32[32,3,4,8,128]{4,3,2,1,0:T(8,128)S(1)} %convolve.1), channel_id=1, replica_groups=mesh['seq'=32,'chan'=4] {'seq'}, dimensions={0} | all-to-all | bytes 3145728 | tf_op jit(solution)/shard_map/all_to_all | solution.py:225
  71.2 0.8 slice.14
  72.1 6.7 %all-to-all-start.2 = ((f32[4,8,4,8,128]{4,3,2,1,0:T(8,128)}), f32[4,8,4,8,128]{4,3,2,1,0:T(8,128)S(1)}, u32[]{:S(2)}, u32[]{:S(2)}) async-start(f32[4,8,4,8,128]{4,3,2,1,0:T(8,128)} %bitcast.2), calls=%async_computation.2 | async-start | bytes 1048576 | tf_op jit(solution)/shard_map/all_to_all | solution.py:227
  78.8 0.1 fusion.3
  78.8 0.1 copy.28
  79.0 0.0 copy-start.5
  79.0 0.2 reshape_squeeze.10
  79.2 0.1 copy.27
  79.4 0.2 reshape_squeeze.9
  79.6 0.4 copy-done.5
  79.9 0.9 %fusion = (bf16[32,4096]{1,0:T(8,128)(2,1)}, bf16[32,4096]{1,0:T(8,128)(2,1)}, bf16[32,4096]{1,0:T(8,128)(2,1)}) fusion(f32[32,4096]{1,0:T(8,128)S(1)} %reshape_squeeze.10, bf16[32,4096]{1,0:T(8,128)(2,1)S(1)} %copy-done.7, bf16[32,4096]{1,0:T(8,128)(2,1)S(1)} %copy-done.6, f32[32,4096]{1,0:T(8,128)S(1)} %reshape_squeeze.9, bf16[32,4096]{1,0:T(8,128)(2,1)S(1)} %copy-done.5), kind=kLoop, calls=%fused_computation.6 | loop fusion | flops 1179648 | bytes 2621440 | tf_op jit(solution)/shard_map/convert_element_type | solution.py:234
  80.9 5.9 %all-to-all-done.2 = f32[4,8,4,8,128]{4,3,2,1,0:T(8,128)S(1)} async-done(((f32[4,8,4,8,128]{4,3,2,1,0:T(8,128)}), f32[4,8,4,8,128]{4,3,2,1,0:T(8,128)S(1)}, u32[]{:S(2)}, u32[]{:S(2)}) %all-to-all-start.2) | async-done | bytes 524320 | tf_op jit(solution)/shard_map/all_to_all | solution.py:227
  86.8 0.7 reshape.18
  (10 shorter events, 0.2 us)
Async XLA Ops:
  0.6 1.6 %copy-start.8 = (f32[32,4096]{1,0:T(8,128)S(1)}, f32[32,4096]{1,0:T(8,128)}, u32[]{:S(2)}) copy-start(f32[32,4096]{1,0:T(8,128)} %param.14) | copy-start | bytes 1572868
  2.1 1.0 %copy-start.6 = (bf16[32,4096]{1,0:T(8,128)(2,1)S(1)}, bf16[32,4096]{1,0:T(8,128)(2,1)}, u32[]{:S(2)}) copy-start(bf16[32,4096]{1,0:T(8,128)(2,1)} %param.12) | copy-start | bytes 786436
  2.2 1.0 %copy-start.7 = (bf16[32,4096]{1,0:T(8,128)(2,1)S(1)}, bf16[32,4096]{1,0:T(8,128)(2,1)}, u32[]{:S(2)}) copy-start(bf16[32,4096]{1,0:T(8,128)(2,1)} %param.11) | copy-start | bytes 786436
  3.6 34.2 %copy-start.3 = (bf16[2,256,512]{2,1,0:T(8,128)(2,1)S(1)}, bf16[2,256,512]{2,1,0:T(8,128)(2,1)}, u32[]{:S(2)}) copy-start(bf16[2,256,512]{2,1,0:T(8,128)(2,1)} %constant.13.clone.first_back_ref) | copy-start | bytes 1572868
  3.6 34.2 %copy-start.4 = (bf16[2,512,256]{2,1,0:T(8,128)(2,1)S(1)}, bf16[2,512,256]{2,1,0:T(8,128)(2,1)}, u32[]{:S(2)}) copy-start(bf16[2,512,256]{2,1,0:T(8,128)(2,1)} %constant.12.clone.first_ref) | copy-start | bytes 1572868
  3.8 34.0 %copy-start = (bf16[2,4,256,256]{3,2,1,0:T(8,128)(2,1)S(1)}, bf16[2,4,256,256]{3,2,1,0:T(8,128)(2,1)}, u32[]{:S(2)}) copy-start(bf16[2,4,256,256]{3,2,1,0:T(8,128)(2,1)} %constant.16.clone.last_back_ref) | copy-start | bytes 3145732
  3.8 34.0 %copy-start.1 = (bf16[2,4,256,256]{3,2,1,0:T(8,128)(2,1)S(1)}, bf16[2,4,256,256]{3,2,1,0:T(8,128)(2,1)}, u32[]{:S(2)}) copy-start(bf16[2,4,256,256]{3,2,1,0:T(8,128)(2,1)} %constant.15.clone.last_ref) | copy-start | bytes 3145732
  3.8 34.0 %copy-start.2 = (f32[2,256,512]{2,1,0:T(8,128)S(1)}, f32[2,256,512]{2,1,0:T(8,128)}, u32[]{:S(2)}) copy-start(f32[2,256,512]{2,1,0:T(8,128)} %constant.14.clone.turn_ref) | copy-start | bytes 3145732
  72.1 14.7 %all-to-all-start.2 = ((f32[4,8,4,8,128]{4,3,2,1,0:T(8,128)}), f32[4,8,4,8,128]{4,3,2,1,0:T(8,128)S(1)}, u32[]{:S(2)}, u32[]{:S(2)}) async-start(f32[4,8,4,8,128]{4,3,2,1,0:T(8,128)} %bitcast.2), calls=%async_computation.2 | async-start | bytes 1048576 | tf_op jit(solution)/shard_map/all_to_all | solution.py:227
  79.0 1.0 %copy-start.5 = (bf16[32,4096]{1,0:T(8,128)(2,1)S(1)}, bf16[32,4096]{1,0:T(8,128)(2,1)}, u32[]{:S(2)}) copy-start(bf16[32,4096]{1,0:T(8,128)(2,1)} %param.13) | copy-start | bytes 786436

commit v4 on v3

--- a/solution.py
+++ b/solution.py
@@ -1,3 +1,4 @@
+import functools
 import math
 
 import jax
@@ -16,6 +17,7 @@
 TURNS = 4
 INNER = 128
 CHUNK = 16
+GROUP = 8
 VMEM_BYTES = 28 * 1024 * 1024
 
 
@@ -159,10 +161,16 @@
             )
             for a in range(SIGNALS):
                 for part in range(2):
-                    product_ref[j, a, rows, lanes(part)] = products[a][part].astype(BF16)
+                    high, low = split(products[a][part])
+                    product_ref[0, j, a, rows, lanes(part)] = high
+                    product_ref[1, j, a, rows, lanes(part)] = low
         for a in range(SIGNALS):
-            data = product_ref[j, a]
-            u_ref[j, a] = dot(data, last_back_ref[0, j]) + dot(data, last_back_ref[1, j])
+            high, low = product_ref[0, j, a], product_ref[1, j, a]
+            u_ref[j, a] = (
+                dot(high, last_back_ref[0, j])
+                + dot(low, last_back_ref[0, j])
+                + dot(high, last_back_ref[1, j])
+            )
 
     for a in range(SIGNALS):
         for rows in chunks:
@@ -172,11 +180,18 @@
             for p in range(TURNS):
                 cos, sin = turn_ref[0, rows, lanes(p)], turn_ref[1, rows, lanes(p)]
                 real, imag = times(z[p], cos, sin)
-                v_ref[a, rows, lanes(p)] = real.astype(BF16)
-                v_ref[a, imag_rows, lanes(p)] = imag.astype(BF16)
+                for part, place in ((real, rows), (imag, imag_rows)):
+                    high, low = split(part)
+                    v_ref[0, a, place, lanes(p)] = high
+                    v_ref[1, a, place, lanes(p)] = low
         for pair in range(TURNS // 2):
-            data = v_ref[a, :, slice(2 * pair * INNER, 2 * (pair + 1) * INNER)]
-            out = dot(first_back_ref[0], data) + dot(first_back_ref[1], data)
+            columns = slice(2 * pair * INNER, 2 * (pair + 1) * INNER)
+            high, low = v_ref[0, a, :, columns], v_ref[1, a, :, columns]
+            out = (
+                dot(first_back_ref[0], high)
+                + dot(first_back_ref[0], low)
+                + dot(first_back_ref[1], high)
+            )
             for p in range(2):
                 y_ref[:, a, 2 * pair + p] = out[:, lanes(p)].reshape(blocks, block_rows, INNER)
 
@@ -197,13 +212,94 @@
             pltpu.VMEM((SIGNALS, 2 * ROWS, width), F32),
             pltpu.VMEM((2, TURNS, SIGNALS, ROWS, 2 * INNER), BF16),
             pltpu.VMEM((TURNS, SIGNALS, ROWS, 2 * INNER), F32),
-            pltpu.VMEM((TURNS, SIGNALS, ROWS, 2 * INNER), BF16),
+            pltpu.VMEM((2, TURNS, SIGNALS, ROWS, 2 * INNER), BF16),
             pltpu.VMEM((TURNS, SIGNALS, ROWS, 2 * INNER), F32),
-            pltpu.VMEM((SIGNALS, 2 * ROWS, width), BF16),
+            pltpu.VMEM((2, SIGNALS, 2 * ROWS, width), BF16),
         ],
         compiler_params=pltpu.CompilerParams(vmem_limit_bytes=VMEM_BYTES),
         name="convolve",
     )(received, *constants)
+
+
+def grid_points(block_rows):
+    for m in range(block_rows):
+        for p in range(TURNS):
+            yield lanes(m * TURNS + p), p * block_rows + m
+
+
+def pack_kernel(block_rows, place_ref, q_ref, k_ref, v_ref, o_ref, f_ref, sent_ref):
+    chan = place_ref[0]
+    signal = TURNS * block_rows
+    stride = SIGNALS * signal
+    for tile in range(0, q_ref.shape[0], 2 * GROUP):
+        rows = slice(tile, tile + 2 * GROUP)
+        bases = [
+            jnp.bitwise_xor(chan, (tile + h * GROUP) // GROUP) * (GROUP * stride) for h in range(2)
+        ]
+        for columns, row in grid_points(block_rows):
+            values = (
+                k_ref[rows, columns].astype(F32) * v_ref[rows, columns].astype(F32),
+                q_ref[rows, columns].astype(F32) * o_ref[rows, columns].astype(F32),
+                f_ref[rows, columns],
+            )
+            for h in range(2):
+                for a in range(SIGNALS):
+                    sent_ref[pl.ds(bases[h] + a * signal + row, GROUP, stride=stride), :] = values[
+                        a
+                    ][h * GROUP : (h + 1) * GROUP]
+
+
+def unpack_kernel(block_rows, place_ref, back_ref, k_ref, v_ref, o_ref, qg_ref, kg_ref, vg_ref):
+    chan = place_ref[0]
+    signal = TURNS * block_rows
+    stride = SIGNALS * signal
+    for tile in range(0, k_ref.shape[0], 2 * GROUP):
+        rows = slice(tile, tile + 2 * GROUP)
+        bases = [
+            jnp.bitwise_xor(chan, (tile + h * GROUP) // GROUP) * (GROUP * stride) for h in range(2)
+        ]
+        for columns, row in grid_points(block_rows):
+            conv_out, adjoint = [
+                jnp.concatenate(
+                    [
+                        back_ref[pl.ds(bases[h] + a * signal + row, GROUP, stride=stride), :]
+                        for h in range(2)
+                    ],
+                    axis=0,
+                )
+                for a in range(2)
+            ]
+            qg_ref[rows, columns] = (conv_out * o_ref[rows, columns].astype(F32)).astype(BF16)
+            kg_ref[rows, columns] = (adjoint * v_ref[rows, columns].astype(F32)).astype(BF16)
+            vg_ref[rows, columns] = (adjoint * k_ref[rows, columns].astype(F32)).astype(BF16)
+
+
+def total_kernel(block_rows, *refs):
+    grad_ref = refs[-1]
+    signal = TURNS * block_rows
+    for columns, row in grid_points(block_rows):
+        values = [ref[pl.ds(row, GROUP, stride=signal), :] for ref in refs[:-1]]
+        total = values[0]
+        for value in values[1:]:
+            total = total + value
+        grad_ref[:, columns] = total
+
+
+def local_call(kernel, name, out_shape, place, *arrays):
+    count = len(arrays)
+    specs = in_vmem(count)
+    if place is not None:
+        specs = [pl.BlockSpec(memory_space=pltpu.SMEM)] + specs
+        arrays = (place,) + arrays
+    single = not isinstance(out_shape, tuple)
+    return pl.pallas_call(
+        kernel,
+        out_shape=out_shape,
+        in_specs=specs,
+        out_specs=in_vmem(1)[0] if single else tuple(in_vmem(len(out_shape))),
+        compiler_params=pltpu.CompilerParams(vmem_limit_bytes=VMEM_BYTES),
+        name=name,
+    )(*arrays)
 
 
 def shards(query_proj, key_proj, value_proj, out_cotangent, filter_raw):
@@ -213,26 +309,47 @@
     length = parts * width
     scale = 1.0 / (length * math.sqrt(length))
     block_rows = ROWS // parts
-    key_float = key_proj.astype(F32)
-    value_float = value_proj.astype(F32)
-    cotangent_float = out_cotangent.astype(F32)
-    gated = key_float * value_float
-    carried = query_proj.astype(F32) * cotangent_float
-    sent = jnp.stack([gated, carried, filter_raw], axis=1)
-    sent = sent.reshape(slab, SIGNALS, block_rows, TURNS, INNER).transpose(0, 1, 3, 2, 4)
+    place = lax.axis_index("chan").astype(jnp.int32).reshape(1)
+    flat = (slab * SIGNALS * TURNS * block_rows, INNER)
+    sent = local_call(
+        functools.partial(pack_kernel, block_rows),
+        "pack",
+        jax.ShapeDtypeStruct(flat, F32),
+        place,
+        query_proj,
+        key_proj,
+        value_proj,
+        out_cotangent,
+        filter_raw,
+    )
+    sent = sent.reshape(slab, SIGNALS, TURNS, block_rows, INNER)
     received = lax.all_to_all(sent, "seq", split_axis=0, concat_axis=0, tiled=True)
     signals = convolve(received, scale)
     back = lax.all_to_all(signals, "seq", split_axis=0, concat_axis=0, tiled=True)
-    rows = back[:, 2].reshape(groups, slab // groups, TURNS, block_rows, INNER)
-    rows = lax.all_to_all(rows, "chan", split_axis=0, concat_axis=0, tiled=True)
-    filter_grad = jnp.sum(rows, axis=0).transpose(0, 2, 1, 3).reshape(-1, width)
-    back = back.transpose(0, 1, 3, 2, 4)
-    conv_out = back[:, 0].reshape(slab, width)
-    adjoint = back[:, 1].reshape(slab, width)
-    query_grad = (conv_out * cotangent_float).astype(BF16)
-    key_grad = (adjoint * value_float).astype(BF16)
-    value_grad = (adjoint * key_float).astype(BF16)
-    return (query_grad, key_grad, value_grad, filter_grad)
+    pieces = []
+    for k in range(groups):
+        piece = back[k * GROUP : (k + 1) * GROUP, 2]
+        if k > 0:
+            piece = lax.ppermute(piece, "chan", [(c, c ^ k) for c in range(groups)])
+        pieces.append(piece.reshape(-1, INNER))
+    grads = local_call(
+        functools.partial(unpack_kernel, block_rows),
+        "unpack",
+        (jax.ShapeDtypeStruct((slab, width), BF16),) * 3,
+        place,
+        back.reshape(flat),
+        key_proj,
+        value_proj,
+        out_cotangent,
+    )
+    filter_grad = local_call(
+        functools.partial(total_kernel, block_rows),
+        "total",
+        jax.ShapeDtypeStruct((slab // groups, width), F32),
+        None,
+        *pieces,
+    )
+    return (*grads, filter_grad)
 
 
 def solution(mesh):

time: 87.8 us -> 87.7 us (level)
  Pallas kernels: 6.09 us -> 11.7 us
  other arithmetic: 2.3 us -> 0 us
  starting transfers between devices: 6.71 us -> 4.71 us
  waiting for transfers between devices: 5.89 us -> 3.9 us
    all_to_all x1 -> x0, starting transfers between devices: 6.71 us -> none  [shards(): rows = lax.all_to_all(rows, 'chan', split_axis=0, concat_axis=0, tiled=True)]
    all_to_all x1 -> x0, waiting for transfers between devices: 5.89 us -> none  [shards(): rows = lax.all_to_all(rows, 'chan', split_axis=0, concat_axis=0, tiled=True)]
    ppermute x0 -> x3, starting transfers between devices: none -> 4.71 us  [shards(): piece = lax.ppermute(piece, 'chan', [(c, c ^ k) for c in range(groups)])]
    pallas_call x0 -> x3, Pallas kernels: none -> 4.02 us  [local_call(): pl.pallas_call(kernel, out_shape=out_shape, in_specs=specs, out_specs=in_...]
    unnamed x18 -> x26, local copies, waits for them, and re-layouts: 0.96 us -> 4.88 us
    ppermute x0 -> x3, waiting for transfers between devices: none -> 3.9 us  [shards(): piece = lax.ppermute(piece, 'chan', [(c, c ^ k) for c in range(groups)])]
    another operation x8 -> x0, local copies, waits for them, and re-layouts: 1.58 us -> none  [the longest x6 1.16 us: shards(): sent = jnp.stack([gated, carried, filter_raw], axis=1)]
    pallas_call x1, Pallas kernels: 6.09 us -> 7.64 us  [convolve(): pl.pallas_call(convolve_kernel, out_shape=jax.ShapeDtypeStruct(received.s...]
  transfers between devices with their start and end apart: 1 -> 3, of which waited for: 1 -> 2; matrix products, arithmetic and copies ran while one was open for 2% -> 0% of each run, Pallas kernels for 0% -> 2%
where the time goes in v4:
time: 87.7 us; the launch traced here: 87.3 us
  blocking collectives  61.4 us (70%)
  Pallas kernels  11.7 us (13%)
  local copies, waits for them, and re-layouts  4.92 us (6%)
  starting transfers between devices  4.71 us (5%)
  waiting for transfers between devices  3.9 us (4%)
    all_to_all x1, blocking collectives, shards(): lax.all_to_all(sent, 'seq', split_axis=0, concat_axis=0, tiled=True)  34 us
    all_to_all x1, blocking collectives, shards(): lax.all_to_all(signals, 'seq', split_axis=0, concat_axis=0, tiled=True)  27.4 us
    pallas_call x1, Pallas kernels, convolve(): pl.pallas_call(convolve_kernel, out_shape=jax.ShapeDtypeStruct(received.s...  7.64 us
    unnamed x26, local copies, waits for them, and re-layouts  4.88 us
    ppermute x3, starting transfers between devices, shards(): piece = lax.ppermute(piece, 'chan', [(c, c ^ k) for c in range(groups)])  4.71 us
    pallas_call x3, Pallas kernels, local_call(): pl.pallas_call(kernel, out_shape=out_shape, in_specs=specs, out_specs=in_...  4.02 us
    ppermute x3, waiting for transfers between devices, shards(): piece = lax.ppermute(piece, 'chan', [(c, c ^ k) for c in range(groups)])  3.9 us
  transfers between devices with their start and end apart: 3, of which 2 were waited for; matrix products, arithmetic and copies ran while one was open for 0% of the time, Pallas kernels for 2%

profile of v4, /device:TPU:1, one launch (start us, length us, event | category | flops | bytes accessed | tf_op | source)
XLA Modules:
  0.0 87.3 jit_solution(10910542811570250510)
XLA Ops:
  0.6 0.0 copy-start.3
  0.6 0.9 %copy-done.3 = bf16[32,4096]{1,0:T(8,128)(2,1)S(1)} copy-done((bf16[32,4096]{1,0:T(8,128)(2,1)S(1)}, bf16[32,4096]{1,0:T(8,128)(2,1)}, u32[]{:S(2)}) %copy-start.3) | copy-done | bytes 262168
  1.6 0.9 %copy-done.5 = bf16[32,4096]{1,0:T(8,128)(2,1)S(1)} copy-done((bf16[32,4096]{1,0:T(8,128)(2,1)S(1)}, bf16[32,4096]{1,0:T(8,128)(2,1)}, u32[]{:S(2)}) %copy-start.5) | copy-done | bytes 262168
  2.5 0.9 %copy-done.7 = bf16[32,4096]{1,0:T(8,128)(2,1)S(1)} copy-done((bf16[32,4096]{1,0:T(8,128)(2,1)S(1)}, bf16[32,4096]{1,0:T(8,128)(2,1)}, u32[]{:S(2)}) %copy-start.7) | copy-done | bytes 262168
  3.5 1.0 %copy-done.11 = f32[32,4096]{1,0:T(8,128)S(1)} copy-done((f32[32,4096]{1,0:T(8,128)S(1)}, f32[32,4096]{1,0:T(8,128)}, u32[]{:S(2)}) %copy-start.11) | copy-done | bytes 524312
  4.5 0.9 %copy-done.12 = bf16[32,4096]{1,0:T(8,128)(2,1)S(1)} copy-done((bf16[32,4096]{1,0:T(8,128)(2,1)S(1)}, bf16[32,4096]{1,0:T(8,128)(2,1)}, u32[]{:S(2)}) %copy-start.12) | copy-done | bytes 262168
  5.5 1.5 %pack.1 = f32[3072,128]{1,0:T(8,128)S(1)} custom-call(s32[1]{0:T(128)} %bitcast.place_ref, bf16[32,4096]{1,0:T(8,128)(2,1)S(1)} %copy-done.12, bf16[32,4096]{1,0:T(8,128)(2,1)S(1)} %copy-done.3, bf16[32,4096]{1,0:T(8,128)(2,1)S(1)} %copy-done.5, bf16[32,4096]{1,0:T(8,128)(2,1)S(1)} %copy-done.7, f32[32,4096]{1,0:T(8,128)S(1)} %copy-done.11), custom_call_target="tpu_custom_call" | custom-call | tf_op jit(solution)/shard_map/pack/pallas_call | solution.py:295
  7.0 0.0 copy-start
  7.0 0.0 copy-start.1
  7.0 0.0 copy-start.2
  7.1 34.0 %all_to_all.10.x_ref = f32[32,3,4,8,128]{4,3,2,1,0:T(8,128)S(1)} all-to-all(f32[32,3,4,8,128]{4,3,2,1,0:T(8,128)S(1)} %bitcast.14), channel_id=1, replica_groups=mesh['seq'=32,'chan'=4] {'seq'}, dimensions={0} | all-to-all | bytes 3145728 | tf_op jit(solution)/shard_map/all_to_all | solution.py:326
  41.0 0.0 copy-done.9
  41.0 0.0 copy-done.10
  41.0 0.0 copy-done
  41.0 0.0 copy-done.1
  41.0 0.0 copy-done.2
  41.0 7.6 %convolve.1 = f32[32,3,4,8,128]{4,3,2,1,0:T(8,128)S(1)} custom-call(f32[32,3,4,8,128]{4,3,2,1,0:T(8,128)S(1)} %all_to_all.10.x_ref, bf16[2,512,256]{2,1,0:T(8,128)(2,1)S(1)} %copy-done.10, bf16[2,256,512]{2,1,0:T(8,128)(2,1)S(1)} %copy-done.9, f32[2,256,512]{2,1,0:T(8,128)S(1)} %copy-done.2, bf16[2,4,256,256]{3,2,1,0:T(8,128)(2,1)S(1)} %copy-done.1, ...), custom_call_target="tpu_custom_call" | custom-call | tf_op jit(solution)/shard_map/convolve/pallas_call | solution.py:206
  48.7 0.0 copy-start.4
  48.7 0.0 copy-start.6
  48.7 0.0 copy-start.8
  48.7 27.4 %all_to_all.11 = f32[32,3,4,8,128]{4,3,2,1,0:T(8,128)S(1)} all-to-all(f32[32,3,4,8,128]{4,3,2,1,0:T(8,128)S(1)} %convolve.1), channel_id=1, replica_groups=mesh['seq'=32,'chan'=4] {'seq'}, dimensions={0} | all-to-all | bytes 3145728 | tf_op jit(solution)/shard_map/all_to_all | solution.py:328
  76.2 3.3 %collective-permute-start.2 = (f32[8,4,8,128]{3,2,1,0:T(8,128)S(1)}, f32[8,4,8,128]{3,2,1,0:T(8,128)S(1)}, u32[]{:S(2)}, u32[]{:S(2)}) collective-permute-start(f32[8,4,8,128]{3,2,1,0:T(8,128)S(1)} %get-tuple-element.10), channel_id=1, source_target_pairs={{0,3},{1,2},{2,1},{3,0},{4,7},{5,6},{6,5},{7,4},{8,11},{9,10},{10,... | collective-permute-start | bytes 393224 | tf_op jit(solution)/shard_map/ppermute | solution.py:333
  79.5 1.4 %collective-permute-start.1 = (f32[8,4,8,128]{3,2,1,0:T(8,128)S(1)}, f32[8,4,8,128]{3,2,1,0:T(8,128)S(1)}, u32[]{:S(2)}, u32[]{:S(2)}) collective-permute-start(f32[8,4,8,128]{3,2,1,0:T(8,128)S(1)} %get-tuple-element.11), channel_id=1, source_target_pairs={{0,2},{1,3},{2,0},{3,1},{4,6},{5,7},{6,4},{7,5},{8,10},{9,11},{10,... | collective-permute-start | bytes 393224 | tf_op jit(solution)/shard_map/ppermute | solution.py:333
  80.9 0.0 collective-permute-start
  80.9 0.0 copy-done.4
  80.9 0.0 copy-done.6
  80.9 0.0 copy-done.8
  80.9 1.6 %unpack.1 = (bf16[32,4096]{1,0:T(8,128)(2,1)}, bf16[32,4096]{1,0:T(8,128)(2,1)}, bf16[32,4096]{1,0:T(8,128)(2,1)}) custom-call(s32[1]{0:T(128)} %bitcast.place_ref, f32[3072,128]{1,0:T(8,128)S(1)} %bitcast.13, bf16[32,4096]{1,0:T(8,128)(2,1)S(1)} %copy-done.4, bf16[32,4096]{1,0:T(8,128)(2,1)S(1)} %copy-done.6, bf16[32,4096]{1,0:T(8,128)(2,1)S(1)} %copy-done.8), custom_call_target="tpu_custom_call" | custom-call | tf_op jit(solution)/shard_map/unpack/pallas_call | solution.py:295
  82.5 0.3 collective-permute-done.2
  82.8 3.6 %collective-permute-done.1 = f32[8,4,8,128]{3,2,1,0:T(8,128)S(1)} collective-permute-done((f32[8,4,8,128]{3,2,1,0:T(8,128)S(1)}, f32[8,4,8,128]{3,2,1,0:T(8,128)S(1)}, u32[]{:S(2)}, u32[]{:S(2)}) %collective-permute-start.1) | collective-permute-done | bytes 131104 | tf_op jit(solution)/shard_map/ppermute | solution.py:333
  86.4 0.0 collective-permute-done
  86.4 0.9 %total.1 = f32[8,4096]{1,0:T(8,128)} custom-call(f32[256,128]{1,0:T(8,128)S(1)} %bitcast.15, f32[256,128]{1,0:T(8,128)S(1)} %bitcast.18, f32[256,128]{1,0:T(8,128)S(1)} %bitcast.17, f32[256,128]{1,0:T(8,128)S(1)} %bitcast.16), custom_call_target="tpu_custom_call" | custom-call | tf_op jit(solution)/shard_map/total/pallas_call | solution.py:295
  (7 shorter events, 0.0 us)
Async XLA Ops:
  0.6 1.0 %copy-start.3 = (bf16[32,4096]{1,0:T(8,128)(2,1)S(1)}, bf16[32,4096]{1,0:T(8,128)(2,1)}, u32[]{:S(2)}) copy-start(bf16[32,4096]{1,0:T(8,128)(2,1)} %k_ref.3) | copy-start | bytes 786436
  1.6 0.9 %copy-start.5 = (bf16[32,4096]{1,0:T(8,128)(2,1)S(1)}, bf16[32,4096]{1,0:T(8,128)(2,1)}, u32[]{:S(2)}) copy-start(bf16[32,4096]{1,0:T(8,128)(2,1)} %v_ref.3) | copy-start | bytes 786436
  2.5 0.9 %copy-start.7 = (bf16[32,4096]{1,0:T(8,128)(2,1)S(1)}, bf16[32,4096]{1,0:T(8,128)(2,1)}, u32[]{:S(2)}) copy-start(bf16[32,4096]{1,0:T(8,128)(2,1)} %o_ref.3) | copy-start | bytes 786436
  3.5 1.0 %copy-start.11 = (f32[32,4096]{1,0:T(8,128)S(1)}, f32[32,4096]{1,0:T(8,128)}, u32[]{:S(2)}) copy-start(f32[32,4096]{1,0:T(8,128)} %f_ref.1) | copy-start | bytes 1572868
  4.5 0.9 %copy-start.12 = (bf16[32,4096]{1,0:T(8,128)(2,1)S(1)}, bf16[32,4096]{1,0:T(8,128)(2,1)}, u32[]{:S(2)}) copy-start(bf16[32,4096]{1,0:T(8,128)(2,1)} %q_ref.1) | copy-start | bytes 786436
  5.5 35.5 %copy-start.9 = (bf16[2,256,512]{2,1,0:T(8,128)(2,1)S(1)}, bf16[2,256,512]{2,1,0:T(8,128)(2,1)}, u32[]{:S(2)}) copy-start(bf16[2,256,512]{2,1,0:T(8,128)(2,1)} %constant.15.clone.first_back_ref) | copy-start | bytes 1572868
  5.5 35.5 %copy-start.10 = (bf16[2,512,256]{2,1,0:T(8,128)(2,1)S(1)}, bf16[2,512,256]{2,1,0:T(8,128)(2,1)}, u32[]{:S(2)}) copy-start(bf16[2,512,256]{2,1,0:T(8,128)(2,1)} %constant.14.clone.first_ref) | copy-start | bytes 1572868
  7.0 34.0 %copy-start = (bf16[2,4,256,256]{3,2,1,0:T(8,128)(2,1)S(1)}, bf16[2,4,256,256]{3,2,1,0:T(8,128)(2,1)}, u32[]{:S(2)}) copy-start(bf16[2,4,256,256]{3,2,1,0:T(8,128)(2,1)} %constant.18.clone.last_back_ref) | copy-start | bytes 3145732
  7.0 34.0 %copy-start.1 = (bf16[2,4,256,256]{3,2,1,0:T(8,128)(2,1)S(1)}, bf16[2,4,256,256]{3,2,1,0:T(8,128)(2,1)}, u32[]{:S(2)}) copy-start(bf16[2,4,256,256]{3,2,1,0:T(8,128)(2,1)} %constant.17.clone.last_ref) | copy-start | bytes 3145732
  7.0 34.0 %copy-start.2 = (f32[2,256,512]{2,1,0:T(8,128)S(1)}, f32[2,256,512]{2,1,0:T(8,128)}, u32[]{:S(2)}) copy-start(f32[2,256,512]{2,1,0:T(8,128)} %constant.16.clone.turn_ref) | copy-start | bytes 3145732
  48.7 32.2 %copy-start.4 = (bf16[32,4096]{1,0:T(8,128)(2,1)S(1)}, bf16[32,4096]{1,0:T(8,128)(2,1)}, u32[]{:S(2)}) copy-start(bf16[32,4096]{1,0:T(8,128)(2,1)} %k_ref.3) | copy-start | bytes 786436
  48.7 32.2 %copy-start.6 = (bf16[32,4096]{1,0:T(8,128)(2,1)S(1)}, bf16[32,4096]{1,0:T(8,128)(2,1)}, u32[]{:S(2)}) copy-start(bf16[32,4096]{1,0:T(8,128)(2,1)} %v_ref.3) | copy-start | bytes 786436
  48.7 32.2 %copy-start.8 = (bf16[32,4096]{1,0:T(8,128)(2,1)S(1)}, bf16[32,4096]{1,0:T(8,128)(2,1)}, u32[]{:S(2)}) copy-start(bf16[32,4096]{1,0:T(8,128)(2,1)} %o_ref.3) | copy-start | bytes 786436
  76.2 6.6 %collective-permute-start.2 = (f32[8,4,8,128]{3,2,1,0:T(8,128)S(1)}, f32[8,4,8,128]{3,2,1,0:T(8,128)S(1)}, u32[]{:S(2)}, u32[]{:S(2)}) collective-permute-start(f32[8,4,8,128]{3,2,1,0:T(8,128)S(1)} %get-tuple-element.10), channel_id=1, source_target_pairs={{0,3},{1,2},{2,1},{3,0},{4,7},{5,6},{6,5},{7,4},{8,11},{9,10},{10,... | collective-permute-start | bytes 393224 | tf_op jit(solution)/shard_map/ppermute | solution.py:333
  79.5 6.9 %collective-permute-start.1 = (f32[8,4,8,128]{3,2,1,0:T(8,128)S(1)}, f32[8,4,8,128]{3,2,1,0:T(8,128)S(1)}, u32[]{:S(2)}, u32[]{:S(2)}) collective-permute-start(f32[8,4,8,128]{3,2,1,0:T(8,128)S(1)} %get-tuple-element.11), channel_id=1, source_target_pairs={{0,2},{1,3},{2,0},{3,1},{4,6},{5,7},{6,4},{7,5},{8,10},{9,11},{10,... | collective-permute-start | bytes 393224 | tf_op jit(solution)/shard_map/ppermute | solution.py:333
  80.9 5.5 %collective-permute-start = (f32[8,4,8,128]{3,2,1,0:T(8,128)S(1)}, f32[8,4,8,128]{3,2,1,0:T(8,128)S(1)}, u32[]{:S(2)}, u32[]{:S(2)}) collective-permute-start(f32[8,4,8,128]{3,2,1,0:T(8,128)S(1)} %get-tuple-element.12), channel_id=1, source_target_pairs={{0,1},{1,0},{2,3},{3,2},{4,5},{5,4},{6,7},{7,6},{8,9},{9,8},{10,11... | collective-permute-start | bytes 393224 | tf_op jit(solution)/shard_map/ppermute | solution.py:333

commit v5 on v4

v5 whole, which is shorter than its diff:
```python
import functools
import itertools
import math

import jax
import jax.numpy as jnp
import ml_dtypes
import numpy as np
from jax import lax
from jax.experimental import pallas as pl
from jax.experimental.pallas import tpu as pltpu
from jax.sharding import PartitionSpec as P

F32 = jnp.float32
BF16 = jnp.bfloat16
SIGNALS = 3
ROWS = 256
TURNS = 4
INNER = 128
CHUNK = 16
GROUP = 8
VMEM_BYTES = 28 * 1024 * 1024
PACK_BYTES = 58 * 1024 * 1024


def halves(table):
    table = table.astype(np.float32)
    high = table.astype(ml_dtypes.bfloat16)
    low = (table - high.astype(np.float32)).astype(ml_dtypes.bfloat16)
    return np.stack([high, low])


def tables(scale):
    width = TURNS * INNER
    k = np.arange(ROWS)[:, None] + 0.25
    angle = 2.0 * np.pi * k * np.arange(ROWS)[None, :] / ROWS
    first = np.concatenate([np.cos(angle), -np.sin(angle)], axis=0)
    turn = 2.0 * np.pi * k * np.arange(width)[None, :] / (ROWS * width)
    turn = np.stack([np.cos(turn), np.sin(turn)]).astype(np.float32)
    l = np.arange(INNER)
    lasts = []
    for j in range(TURNS):
        angle = 2.0 * np.pi * (l[:, None] * (j + TURNS * l[None, :]) % width) / width
        cos, sin = np.cos(angle), np.sin(angle)
        lasts.append(
            np.concatenate(
                [np.concatenate([cos, -sin], axis=1), np.concatenate([sin, cos], axis=1)], axis=0
            )
        )
    last = np.stack(lasts)
    return (
        halves(first),
        halves(first.T),
        turn,
        halves(last),
        halves(last.transpose(0, 2, 1) * scale),
    )


def times(pair, cos, sin):
    return pair[0] * cos - pair[1] * sin, pair[1] * cos + pair[0] * sin


def add(first, second):
    return first[0] + second[0], first[1] + second[1]


def sub(first, second):
    return first[0] - second[0], first[1] - second[1]


def quarter(pair, sign):
    return (-pair[1], pair[0]) if sign > 0 else (pair[1], -pair[0])


def four_point(z, sign):
    s0, d0 = add(z[0], z[2]), sub(z[0], z[2])
    s1, d1 = add(z[1], z[3]), sub(z[1], z[3])
    if sign > 0:
        return [
            add(s0, s1),
            (d0[0] - d1[1], d0[1] + d1[0]),
            sub(s0, s1),
            (d0[0] + d1[1], d0[1] - d1[0]),
        ]
    return [
        add(s0, s1),
        (d0[0] + d1[1], d0[1] - d1[0]),
        sub(s0, s1),
        (d0[0] - d1[1], d0[1] + d1[0]),
    ]


def split(value):
    high = value.astype(BF16)
    return high, (value - high.astype(F32)).astype(BF16)


def dot(first, second):
    return jnp.dot(first, second, preferred_element_type=F32)


def lanes(index):
    return slice(index * INNER, (index + 1) * INNER)


def convolve_kernel(
    x_ref,
    first_ref,
    first_back_ref,
    turn_ref,
    last_ref,
    last_back_ref,
    y_ref,
    mixed_ref,
    z_ref,
    spectra_ref,
    product_ref,
    u_ref,
    v_ref,
):
    blocks, _, _, block_rows, _ = x_ref.shape
    half = ROWS
    chunks = [slice(i, i + CHUNK) for i in range(0, ROWS, CHUNK)]

    def imag(rows):
        return slice(ROWS + rows.start, ROWS + rows.stop)

    def columns(pair):
        return slice(2 * pair * INNER, 2 * (pair + 1) * INNER)

    def mix(a, pair, part):
        data = jnp.concatenate(
            [x_ref[:, a, 2 * pair + p].reshape(ROWS, INNER) for p in range(2)], axis=1
        )
        high, low = split(data)
        rows = slice(part * half, (part + 1) * half)
        mixed_ref[a, rows, columns(pair)] = (
            dot(first_ref[0, rows], high)
            + dot(first_ref[0, rows], low)
            + dot(first_ref[1, rows], high)
        )

    def opening(a, rows):
        z = []
        for p in range(TURNS):
            cos, sin = turn_ref[0, rows, lanes(p)], turn_ref[1, rows, lanes(p)]
            pair = (mixed_ref[a, rows, lanes(p)], mixed_ref[a, imag(rows), lanes(p)])
            z.append(times(pair, cos, -sin))
        z = four_point(z, -1)
        for j in range(TURNS):
            for part in range(2):
                high, low = split(z[j][part])
                z_ref[0, j, a, rows, lanes(part)] = high
                z_ref[1, j, a, rows, lanes(part)] = low

    def last(j, a):
        high, low = z_ref[0, j, a], z_ref[1, j, a]
        spectra_ref[j, a] = (
            dot(high, last_ref[0, j]) + dot(low, last_ref[0, j]) + dot(high, last_ref[1, j])
        )

    def product(j, rows):
        gated, carried, filters = [
            (spectra_ref[j, a, rows, lanes(0)], spectra_ref[j, a, rows, lanes(1)])
            for a in range(SIGNALS)
        ]
        products = (
            times(gated, filters[0], filters[1]),
            times(carried, filters[0], -filters[1]),
            times(carried, gated[0], -gated[1]),
        )
        for a in range(SIGNALS):
            for part in range(2):
                high, low = split(products[a][part])
                product_ref[0, j, a, rows, lanes(part)] = high
                product_ref[1, j, a, rows, lanes(part)] = low

    def last_back(j, a):
        high, low = product_ref[0, j, a], product_ref[1, j, a]
        u_ref[j, a] = (
            dot(high, last_back_ref[0, j])
            + dot(low, last_back_ref[0, j])
            + dot(high, last_back_ref[1, j])
        )

    def closing(a, rows):
        z = [(u_ref[j, a, rows, lanes(0)], u_ref[j, a, rows, lanes(1)]) for j in range(TURNS)]
        z = four_point(z, 1)
        for p in range(TURNS):
            cos, sin = turn_ref[0, rows, lanes(p)], turn_ref[1, rows, lanes(p)]
            pair = times(z[p], cos, sin)
            for part, place in zip(pair, (rows, imag(rows))):
                high, low = split(part)
                v_ref[0, a, place, lanes(p)] = high
                v_ref[1, a, place, lanes(p)] = low

    def unmix(a, pair):
        high, low = v_ref[0, a, :, columns(pair)], v_ref[1, a, :, columns(pair)]
        out = (
            dot(first_back_ref[0], high)
            + dot(first_back_ref[0], low)
            + dot(first_back_ref[1], high)
        )
        for p in range(2):
            y_ref[:, a, 2 * pair + p] = out[:, lanes(p)].reshape(blocks, block_rows, INNER)

    def steps(function, *ranges):
        return [functools.partial(function, *place) for place in itertools.product(*ranges)]

    pairs, turns = range(TURNS // 2), range(TURNS)
    for matrix, vector in (
        (steps(mix, [2], pairs, range(2)), []),
        (steps(mix, [0], pairs, range(2)), steps(opening, [2], chunks)),
        (steps(mix, [1], pairs, range(2)), steps(opening, [0], chunks)),
        (steps(last, turns, [2, 0]), steps(opening, [1], chunks)),
        (steps(last, [0], [1]), []),
        (steps(last, turns[1:], [1]), steps(product, [0], chunks)),
        (steps(last_back, [0], range(SIGNALS)), steps(product, [1], chunks)),
        (steps(last_back, [1], range(SIGNALS)), steps(product, [2], chunks)),
        (steps(last_back, [2], range(SIGNALS)), steps(product, [3], chunks)),
        (steps(last_back, [3], [0]), []),
        (steps(last_back, [3], [1, 2]), steps(closing, [0], chunks)),
        (steps(unmix, [0], pairs), steps(closing, [1], chunks)),
        (steps(unmix, [1], pairs), steps(closing, [2], chunks)),
        (steps(unmix, [2], pairs), []),
    ):
        for i, step in enumerate(matrix):
            step()
            for other in vector[i * len(vector) // len(matrix) : (i + 1) * len(vector) // len(matrix)]:
                other()


def in_vmem(count):
    return [pl.BlockSpec(memory_space=pltpu.VMEM)] * count


def convolve(received, scale):
    constants = [jnp.asarray(table) for table in tables(scale)]
    width = TURNS * INNER
    return pl.pallas_call(
        convolve_kernel,
        out_shape=jax.ShapeDtypeStruct(received.shape, F32),
        in_specs=in_vmem(6),
        out_specs=pl.BlockSpec(memory_space=pltpu.VMEM),
        scratch_shapes=[
            pltpu.VMEM((SIGNALS, 2 * ROWS, width), F32),
            pltpu.VMEM((2, TURNS, SIGNALS, ROWS, 2 * INNER), BF16),
            pltpu.VMEM((TURNS, SIGNALS, ROWS, 2 * INNER), F32),
            pltpu.VMEM((2, TURNS, SIGNALS, ROWS, 2 * INNER), BF16),
            pltpu.VMEM((TURNS, SIGNALS, ROWS, 2 * INNER), F32),
            pltpu.VMEM((2, SIGNALS, 2 * ROWS, width), BF16),
        ],
        compiler_params=pltpu.CompilerParams(vmem_limit_bytes=VMEM_BYTES),
        name="convolve",
    )(received, *constants)


def pack_kernel(block_rows, place_ref, *refs):
    sources, sent_ref, held, sems = refs[:5], refs[5], refs[6:11], refs[11]
    chan = place_ref[0]
    signal = TURNS * block_rows
    stride = SIGNALS * signal
    tall = 2 * GROUP
    tiles = range(0, sources[0].shape[0], tall)
    copies = []
    for t, tile in enumerate(tiles):
        for n in range(5):
            rows = pl.ds(tile, tall)
            copies.append(pltpu.make_async_copy(sources[n].at[rows], held[n].at[rows], sems.at[t, n]))
    for copy in copies:
        copy.start()
    q_ref, k_ref, v_ref, o_ref, f_ref = held
    for t, tile in enumerate(tiles):
        for copy in copies[5 * t : 5 * t + 5]:
            copy.wait()
        rows = slice(tile, tile + tall)
        bases = [jnp.bitwise_xor(chan, (tile + h * GROUP) // GROUP) * GROUP for h in range(2)]
        for p in range(TURNS):
            values = [[], [], []]
            for m in range(block_rows):
                columns = lanes(m * TURNS + p)
                values[0].append(k_ref[rows, columns].astype(F32) * v_ref[rows, columns].astype(F32))
                values[1].append(q_ref[rows, columns].astype(F32) * o_ref[rows, columns].astype(F32))
                values[2].append(f_ref[rows, columns])
            for h in range(2):
                for a in range(SIGNALS):
                    block = jnp.stack([value[h * GROUP : (h + 1) * GROUP] for value in values[a]])
                    sent_ref[pl.ds(bases[h], GROUP), a, p] = jnp.swapaxes(block, 0, 1)


def unpack_kernel(block_rows, place_ref, back_ref, k_ref, v_ref, o_ref, qg_ref, kg_ref, vg_ref):
    chan = place_ref[0]
    tall = 2 * GROUP
    for tile in range(0, k_ref.shape[0], tall):
        rows = slice(tile, tile + tall)
        bases = [jnp.bitwise_xor(chan, (tile + h * GROUP) // GROUP) * GROUP for h in range(2)]
        for p in range(TURNS):
            conv_out, adjoint = [
                jnp.concatenate(
                    [
                        jnp.swapaxes(back_ref[pl.ds(bases[h], GROUP), a, p], 0, 1)
                        for h in range(2)
                    ],
                    axis=1,
                )
                for a in range(2)
            ]
            for m in range(block_rows):
                columns = lanes(m * TURNS + p)
                qg_ref[rows, columns] = (conv_out[m] * o_ref[rows, columns].astype(F32)).astype(BF16)
                kg_ref[rows, columns] = (adjoint[m] * v_ref[rows, columns].astype(F32)).astype(BF16)
                vg_ref[rows, columns] = (adjoint[m] * k_ref[rows, columns].astype(F32)).astype(BF16)


def total_kernel(block_rows, *refs):
    grad_ref = refs[-1]
    for p in range(TURNS):
        total = refs[0][:, p]
        for ref in refs[1:-1]:
            total = total + ref[:, p]
        total = jnp.swapaxes(total, 0, 1)
        for m in range(block_rows):
            grad_ref[:, lanes(m * TURNS + p)] = total[m]


def local_call(kernel, name, out_shape, place, *arrays):
    count = len(arrays)
    specs = in_vmem(count)
    if place is not None:
        specs = [pl.BlockSpec(memory_space=pltpu.SMEM)] + specs
        arrays = (place,) + arrays
    single = not isinstance(out_shape, tuple)
    return pl.pallas_call(
        kernel,
        out_shape=out_shape,
        in_specs=specs,
        out_specs=in_vmem(1)[0] if single else tuple(in_vmem(len(out_shape))),
        compiler_params=pltpu.CompilerParams(vmem_limit_bytes=VMEM_BYTES),
        name=name,
    )(*arrays)


def pack(block_rows, place, arrays):
    slab, width = arrays[0].shape
    shape = (slab, SIGNALS, TURNS, block_rows, INNER)
    return pl.pallas_call(
        functools.partial(pack_kernel, block_rows),
        out_shape=jax.ShapeDtypeStruct(shape, F32),
        in_specs=[pl.BlockSpec(memory_space=pltpu.SMEM)] + [pl.BlockSpec(memory_space=pl.ANY)] * 5,
        out_specs=pl.BlockSpec(memory_space=pltpu.VMEM),
        scratch_shapes=[pltpu.VMEM((slab, width), array.dtype) for array in arrays]
        + [pltpu.SemaphoreType.DMA((slab // (2 * GROUP), 5))],
        compiler_params=pltpu.CompilerParams(vmem_limit_bytes=PACK_BYTES),
        name="pack",
    )(place, *arrays)


def shards(query_proj, key_proj, value_proj, out_cotangent, filter_raw):
    slab, width = query_proj.shape
    parts = lax.axis_size("seq")
    groups = lax.axis_size("chan")
    length = parts * width
    scale = 1.0 / (length * math.sqrt(length))
    block_rows = ROWS // parts
    place = lax.axis_index("chan").astype(jnp.int32).reshape(1)
    sent = pack(
        block_rows, place, (query_proj, key_proj, value_proj, out_cotangent, filter_raw)
    )
    received = lax.all_to_all(sent, "seq", split_axis=0, concat_axis=0, tiled=True)
    signals = convolve(received, scale)
    back = lax.all_to_all(signals, "seq", split_axis=0, concat_axis=0, tiled=True)
    pieces = []
    for k in range(groups):
        piece = back[k * GROUP : (k + 1) * GROUP, 2]
        if k > 0:
            piece = lax.ppermute(piece, "chan", [(c, c ^ k) for c in range(groups)])
        pieces.append(piece)
    grads = local_call(
        functools.partial(unpack_kernel, block_rows),
        "unpack",
        (jax.ShapeDtypeStruct((slab, width), BF16),) * 3,
        place,
        back,
        key_proj,
        value_proj,
        out_cotangent,
    )
    filter_grad = local_call(
        functools.partial(total_kernel, block_rows),
        "total",
        jax.ShapeDtypeStruct((slab // groups, width), F32),
        None,
        *pieces,
    )
    return (*grads, filter_grad)


def solution(mesh):
    placed = (
        P("chan", "seq"),
        P("chan", "seq"),
        P("chan", "seq"),
        P("chan", "seq"),
        P(None, "seq"),
    )
    return jax.shard_map(
        shards,
        mesh=mesh,
        in_specs=placed,
        out_specs=(P("chan", "seq"), P("chan", "seq"), P("chan", "seq"), P("chan", "seq")),
        check_vma=False,
    )
```

time: 87.7 us -> 83.4 us (0.951)
  local copies, waits for them, and re-layouts: 4.92 us -> 0.09 us
    unnamed x26 -> x16, local copies, waits for them, and re-layouts: 4.88 us -> 0.05 us
    pallas_call x0 -> x1, Pallas kernels: none -> 2.97 us  [pack(): pl.pallas_call(functools.partial(pack_kernel, block_rows), out_shape=jax....]
    pallas_call x3 -> x2, Pallas kernels: 4.02 us -> 1.86 us  [local_call(): pl.pallas_call(kernel, out_shape=out_shape, in_specs=specs, out_specs=in_...]
  transfers between devices with their start and end apart: 3 -> 3, of which waited for: 2 -> 2; matrix products, arithmetic and copies ran while one was open for 0% -> 0% of each run, Pallas kernels for 2% -> 1%
where the time goes in v5:
time: 83.4 us; the launch traced here: 83.2 us
  blocking collectives  61.6 us (74%)
  Pallas kernels  11.7 us (14%)
  starting transfers between devices  4.69 us (6%)
  waiting for transfers between devices  4.32 us (5%)
    all_to_all x1, blocking collectives, shards(): lax.all_to_all(sent, 'seq', split_axis=0, concat_axis=0, tiled=True)  34.2 us
    all_to_all x1, blocking collectives, shards(): lax.all_to_all(signals, 'seq', split_axis=0, concat_axis=0, tiled=True)  27.4 us
    pallas_call x1, Pallas kernels, convolve(): pl.pallas_call(convolve_kernel, out_shape=jax.ShapeDtypeStruct(received.s...  6.88 us
    ppermute x3, starting transfers between devices, shards(): piece = lax.ppermute(piece, 'chan', [(c, c ^ k) for c in range(groups)])  4.69 us
    ppermute x3, waiting for transfers between devices, shards(): piece = lax.ppermute(piece, 'chan', [(c, c ^ k) for c in range(groups)])  4.32 us
    pallas_call x1, Pallas kernels, pack(): pl.pallas_call(functools.partial(pack_kernel, block_rows), out_shape=jax....  2.97 us
    pallas_call x2, Pallas kernels, local_call(): pl.pallas_call(kernel, out_shape=out_shape, in_specs=specs, out_specs=in_...  1.86 us
  transfers between devices with their start and end apart: 3, of which 2 were waited for; matrix products, arithmetic and copies ran while one was open for 0% of the time, Pallas kernels for 1%

profile of v5, /device:TPU:1, one launch (start us, length us, event | category | flops | bytes accessed | tf_op | source)
XLA Modules:
  0.0 83.2 jit_solution(14416182971944934239)
XLA Ops:
  0.6 0.0 copy-start.6
  0.6 0.0 copy-start.7
  0.7 3.0 %pack.1 = f32[32,3,4,8,128]{4,3,2,1,0:T(8,128)} custom-call(s32[1]{0:T(128)} %bitcast.place_ref, bf16[32,4096]{1,0:T(8,128)(2,1)} %refs_0_.1, bf16[32,4096]{1,0:T(8,128)(2,1)} %k_ref.1, bf16[32,4096]{1,0:T(8,128)(2,1)} %v_ref.1, bf16[32,4096]{1,0:T(8,128)(2,1)} %o_ref.1, f32[32,4096]{1,0:T(8,128)} %refs_4_.1), custom_call_target="tpu_custom_call" | custom-call | tf_op jit(solution)/shard_map/pack/pallas_call | solution.py:347
  3.6 0.0 copy-start
  3.6 0.0 copy-start.1
  3.7 0.0 copy-start.2
  3.7 34.2 %all_to_all.10.x_ref = f32[32,3,4,8,128]{4,3,2,1,0:T(8,128)S(1)} all-to-all(f32[32,3,4,8,128]{4,3,2,1,0:T(8,128)} %pack.1), channel_id=1, replica_groups=mesh['seq'=32,'chan'=4] {'seq'}, dimensions={0} | all-to-all | bytes 3145728 | tf_op jit(solution)/shard_map/all_to_all | solution.py:370
  37.8 0.0 copy-done.6
  37.8 0.0 copy-done.7
  37.8 0.0 copy-done
  37.8 0.0 copy-done.1
  37.9 0.0 copy-done.2
  37.9 6.9 %convolve.1 = f32[32,3,4,8,128]{4,3,2,1,0:T(8,128)S(1)} custom-call(f32[32,3,4,8,128]{4,3,2,1,0:T(8,128)S(1)} %all_to_all.10.x_ref, bf16[2,512,256]{2,1,0:T(8,128)(2,1)S(1)} %copy-done.7, bf16[2,256,512]{2,1,0:T(8,128)(2,1)S(1)} %copy-done.6, f32[2,256,512]{2,1,0:T(8,128)S(1)} %copy-done.2, bf16[2,4,256,256]{3,2,1,0:T(8,128)(2,1)S(1)} %copy-done.1, ...), custom_call_target="tpu_custom_call" | custom-call | tf_op jit(solution)/shard_map/convolve/pallas_call | solution.py:241
  44.8 0.0 copy-start.3
  44.8 0.0 copy-start.4
  44.8 0.0 copy-start.5
  44.8 27.4 %all_to_all.11.back_ref = f32[32,3,4,8,128]{4,3,2,1,0:T(8,128)S(1)} all-to-all(f32[32,3,4,8,128]{4,3,2,1,0:T(8,128)S(1)} %convolve.1), channel_id=1, replica_groups=mesh['seq'=32,'chan'=4] {'seq'}, dimensions={0} | all-to-all | bytes 3145728 | tf_op jit(solution)/shard_map/all_to_all | solution.py:372
  72.3 3.3 %collective-permute-start.2 = (f32[8,4,8,128]{3,2,1,0:T(8,128)S(1)}, f32[8,4,8,128]{3,2,1,0:T(8,128)S(1)}, u32[]{:S(2)}, u32[]{:S(2)}) collective-permute-start(f32[8,4,8,128]{3,2,1,0:T(8,128)S(1)} %get-tuple-element.10), channel_id=1, source_target_pairs={{0,3},{1,2},{2,1},{3,0},{4,7},{5,6},{6,5},{7,4},{8,11},{9,10},{10,... | collective-permute-start | bytes 393224 | tf_op jit(solution)/shard_map/ppermute | solution.py:377
  75.6 1.4 %collective-permute-start.1 = (f32[8,4,8,128]{3,2,1,0:T(8,128)S(1)}, f32[8,4,8,128]{3,2,1,0:T(8,128)S(1)}, u32[]{:S(2)}, u32[]{:S(2)}) collective-permute-start(f32[8,4,8,128]{3,2,1,0:T(8,128)S(1)} %get-tuple-element.11), channel_id=1, source_target_pairs={{0,2},{1,3},{2,0},{3,1},{4,6},{5,7},{6,4},{7,5},{8,10},{9,11},{10,... | collective-permute-start | bytes 393224 | tf_op jit(solution)/shard_map/ppermute | solution.py:377
  77.0 0.0 collective-permute-start
  77.0 0.0 copy-done.3
  77.0 0.0 copy-done.4
  77.0 0.0 copy-done.5
  77.0 1.1 %unpack.1 = (bf16[32,4096]{1,0:T(8,128)(2,1)}, bf16[32,4096]{1,0:T(8,128)(2,1)}, bf16[32,4096]{1,0:T(8,128)(2,1)}) custom-call(s32[1]{0:T(128)} %bitcast.place_ref, f32[32,3,4,8,128]{4,3,2,1,0:T(8,128)S(1)} %all_to_all.11.back_ref, bf16[32,4096]{1,0:T(8,128)(2,1)S(1)} %copy-done.3, bf16[32,4096]{1,0:T(8,128)(2,1)S(1)} %copy-done.4, ...), custom_call_target="tpu_custom_call" | custom-call | tf_op jit(solution)/shard_map/unpack/pallas_call | solution.py:334
  78.1 0.7 collective-permute-done.2.refs_3_
  78.8 3.6 %collective-permute-done.1.refs_2_ = f32[8,4,8,128]{3,2,1,0:T(8,128)S(1)} collective-permute-done((f32[8,4,8,128]{3,2,1,0:T(8,128)S(1)}, f32[8,4,8,128]{3,2,1,0:T(8,128)S(1)}, u32[]{:S(2)}, u32[]{:S(2)}) %collective-permute-start.1) | collective-permute-done | bytes 131104 | tf_op jit(solution)/shard_map/ppermute | solution.py:377
  82.4 0.0 collective-permute-done.refs_1_
  82.4 0.7 total.1
  (1 shorter events, 0.0 us)
Async XLA Ops:
  0.6 37.2 %copy-start.6 = (bf16[2,256,512]{2,1,0:T(8,128)(2,1)S(1)}, bf16[2,256,512]{2,1,0:T(8,128)(2,1)}, u32[]{:S(2)}) copy-start(bf16[2,256,512]{2,1,0:T(8,128)(2,1)} %constant.15.clone.first_back_ref) | copy-start | bytes 1572868
  0.6 37.2 %copy-start.7 = (bf16[2,512,256]{2,1,0:T(8,128)(2,1)S(1)}, bf16[2,512,256]{2,1,0:T(8,128)(2,1)}, u32[]{:S(2)}) copy-start(bf16[2,512,256]{2,1,0:T(8,128)(2,1)} %constant.14.clone.first_ref) | copy-start | bytes 1572868
  3.6 34.2 %copy-start = (bf16[2,4,256,256]{3,2,1,0:T(8,128)(2,1)S(1)}, bf16[2,4,256,256]{3,2,1,0:T(8,128)(2,1)}, u32[]{:S(2)}) copy-start(bf16[2,4,256,256]{3,2,1,0:T(8,128)(2,1)} %constant.18.clone.last_back_ref) | copy-start | bytes 3145732
  3.6 34.2 %copy-start.1 = (bf16[2,4,256,256]{3,2,1,0:T(8,128)(2,1)S(1)}, bf16[2,4,256,256]{3,2,1,0:T(8,128)(2,1)}, u32[]{:S(2)}) copy-start(bf16[2,4,256,256]{3,2,1,0:T(8,128)(2,1)} %constant.17.clone.last_ref) | copy-start | bytes 3145732
  3.7 34.2 %copy-start.2 = (f32[2,256,512]{2,1,0:T(8,128)S(1)}, f32[2,256,512]{2,1,0:T(8,128)}, u32[]{:S(2)}) copy-start(f32[2,256,512]{2,1,0:T(8,128)} %constant.16.clone.turn_ref) | copy-start | bytes 3145732
  44.8 32.2 %copy-start.3 = (bf16[32,4096]{1,0:T(8,128)(2,1)S(1)}, bf16[32,4096]{1,0:T(8,128)(2,1)}, u32[]{:S(2)}) copy-start(bf16[32,4096]{1,0:T(8,128)(2,1)} %k_ref.1) | copy-start | bytes 786436
  44.8 32.2 %copy-start.4 = (bf16[32,4096]{1,0:T(8,128)(2,1)S(1)}, bf16[32,4096]{1,0:T(8,128)(2,1)}, u32[]{:S(2)}) copy-start(bf16[32,4096]{1,0:T(8,128)(2,1)} %v_ref.1) | copy-start | bytes 786436
  44.8 32.2 %copy-start.5 = (bf16[32,4096]{1,0:T(8,128)(2,1)S(1)}, bf16[32,4096]{1,0:T(8,128)(2,1)}, u32[]{:S(2)}) copy-start(bf16[32,4096]{1,0:T(8,128)(2,1)} %o_ref.1) | copy-start | bytes 786436
  72.3 6.6 %collective-permute-start.2 = (f32[8,4,8,128]{3,2,1,0:T(8,128)S(1)}, f32[8,4,8,128]{3,2,1,0:T(8,128)S(1)}, u32[]{:S(2)}, u32[]{:S(2)}) collective-permute-start(f32[8,4,8,128]{3,2,1,0:T(8,128)S(1)} %get-tuple-element.10), channel_id=1, source_target_pairs={{0,3},{1,2},{2,1},{3,0},{4,7},{5,6},{6,5},{7,4},{8,11},{9,10},{10,... | collective-permute-start | bytes 393224 | tf_op jit(solution)/shard_map/ppermute | solution.py:377
  75.6 6.9 %collective-permute-start.1 = (f32[8,4,8,128]{3,2,1,0:T(8,128)S(1)}, f32[8,4,8,128]{3,2,1,0:T(8,128)S(1)}, u32[]{:S(2)}, u32[]{:S(2)}) collective-permute-start(f32[8,4,8,128]{3,2,1,0:T(8,128)S(1)} %get-tuple-element.11), channel_id=1, source_target_pairs={{0,2},{1,3},{2,0},{3,1},{4,6},{5,7},{6,4},{7,5},{8,10},{9,11},{10,... | collective-permute-start | bytes 393224 | tf_op jit(solution)/shard_map/ppermute | solution.py:377
  77.0 5.5 %collective-permute-start = (f32[8,4,8,128]{3,2,1,0:T(8,128)S(1)}, f32[8,4,8,128]{3,2,1,0:T(8,128)S(1)}, u32[]{:S(2)}, u32[]{:S(2)}) collective-permute-start(f32[8,4,8,128]{3,2,1,0:T(8,128)S(1)} %get-tuple-element.12), channel_id=1, source_target_pairs={{0,1},{1,0},{2,3},{3,2},{4,5},{5,4},{6,7},{7,6},{8,9},{9,8},{10,11... | collective-permute-start | bytes 393224 | tf_op jit(solution)/shard_map/ppermute | solution.py:377

commit v6 on v5

v6 whole, which is shorter than its diff:
```python
import functools
import itertools
import math

import jax
import jax.numpy as jnp
import ml_dtypes
import numpy as np
from jax import lax
from jax.experimental import pallas as pl
from jax.experimental.pallas import tpu as pltpu
from jax.sharding import PartitionSpec as P

F32 = jnp.float32
BF16 = jnp.bfloat16
SIGNALS = 3
ROWS = 256
TURNS = 4
INNER = 128
CHUNK = 16
GROUP = 8
VMEM_BYTES = 28 * 1024 * 1024
PACK_BYTES = 58 * 1024 * 1024


def halves(table):
    table = table.astype(np.float32)
    high = table.astype(ml_dtypes.bfloat16)
    low = (table - high.astype(np.float32)).astype(ml_dtypes.bfloat16)
    return np.stack([high, low])


def tables(scale):
    width = TURNS * INNER
    k = np.arange(ROWS)[:, None] + 0.25
    angle = 2.0 * np.pi * k * np.arange(ROWS)[None, :] / ROWS
    first = np.concatenate([np.cos(angle), -np.sin(angle)], axis=0)
    turn = 2.0 * np.pi * k * np.arange(width)[None, :] / (ROWS * width)
    turn = np.stack([np.cos(turn), np.sin(turn)]).astype(np.float32)
    l = np.arange(INNER)
    lasts = []
    for j in range(TURNS):
        angle = 2.0 * np.pi * (l[:, None] * (j + TURNS * l[None, :]) % width) / width
        cos, sin = np.cos(angle), np.sin(angle)
        lasts.append(
            np.concatenate(
                [np.concatenate([cos, -sin], axis=1), np.concatenate([sin, cos], axis=1)], axis=0
            )
        )
    last = np.stack(lasts)
    return (
        halves(first),
        halves(first.T),
        turn,
        halves(last),
        halves(last.transpose(0, 2, 1) * scale),
    )


def times(pair, cos, sin):
    return pair[0] * cos - pair[1] * sin, pair[1] * cos + pair[0] * sin


def add(first, second):
    return first[0] + second[0], first[1] + second[1]


def sub(first, second):
    return first[0] - second[0], first[1] - second[1]


def quarter(pair, sign):
    return (-pair[1], pair[0]) if sign > 0 else (pair[1], -pair[0])


def four_point(z, sign):
    s0, d0 = add(z[0], z[2]), sub(z[0], z[2])
    s1, d1 = add(z[1], z[3]), sub(z[1], z[3])
    if sign > 0:
        return [
            add(s0, s1),
            (d0[0] - d1[1], d0[1] + d1[0]),
            sub(s0, s1),
            (d0[0] + d1[1], d0[1] - d1[0]),
        ]
    return [
        add(s0, s1),
        (d0[0] + d1[1], d0[1] - d1[0]),
        sub(s0, s1),
        (d0[0] - d1[1], d0[1] + d1[0]),
    ]


def split(value):
    high = value.astype(BF16)
    return high, (value - high.astype(F32)).astype(BF16)


def dot(first, second):
    return jnp.dot(first, second, preferred_element_type=F32)


def lanes(index):
    return slice(index * INNER, (index + 1) * INNER)


def imag(rows):
    return slice(ROWS + rows.start, ROWS + rows.stop)


def columns(pair):
    return slice(2 * pair * INNER, 2 * (pair + 1) * INNER)


def mix(x_ref, first_ref, mixed_ref, a, pair, part):
    data = jnp.concatenate(
        [x_ref[:, a, 2 * pair + p].reshape(ROWS, INNER) for p in range(2)], axis=1
    )
    high, low = split(data)
    rows = slice(part * ROWS, (part + 1) * ROWS)
    mixed_ref[rows, columns(pair)] = (
        dot(first_ref[0, rows], high)
        + dot(first_ref[0, rows], low)
        + dot(first_ref[1, rows], high)
    )


def opening(mixed_ref, turn_ref, z_ref, rows):
    z = []
    for p in range(TURNS):
        cos, sin = turn_ref[0, rows, lanes(p)], turn_ref[1, rows, lanes(p)]
        pair = (mixed_ref[rows, lanes(p)], mixed_ref[imag(rows), lanes(p)])
        z.append(times(pair, cos, -sin))
    z = four_point(z, -1)
    for j in range(TURNS):
        for part in range(2):
            high, low = split(z[j][part])
            z_ref[0, j, rows, lanes(part)] = high
            z_ref[1, j, rows, lanes(part)] = low


def last(z_ref, last_ref, spectra_ref, j):
    high, low = z_ref[0, j], z_ref[1, j]
    spectra_ref[j] = (
        dot(high, last_ref[0, j]) + dot(low, last_ref[0, j]) + dot(high, last_ref[1, j])
    )


def product(one_ref, two_ref, conjugate, product_ref, j, rows):
    one = (one_ref[j, rows, lanes(0)], one_ref[j, rows, lanes(1)])
    two = (two_ref[j, rows, lanes(0)], two_ref[j, rows, lanes(1)])
    pair = times(one, two[0], -two[1] if conjugate else two[1])
    for part in range(2):
        high, low = split(pair[part])
        product_ref[0, j, rows, lanes(part)] = high
        product_ref[1, j, rows, lanes(part)] = low


def closing(u_ref, turn_ref, v_ref, rows):
    z = [(u_ref[j, rows, lanes(0)], u_ref[j, rows, lanes(1)]) for j in range(TURNS)]
    z = four_point(z, 1)
    for p in range(TURNS):
        cos, sin = turn_ref[0, rows, lanes(p)], turn_ref[1, rows, lanes(p)]
        pair = times(z[p], cos, sin)
        for part, place in zip(pair, (rows, imag(rows))):
            high, low = split(part)
            v_ref[0, place, lanes(p)] = high
            v_ref[1, place, lanes(p)] = low


def unmix(v_ref, first_back_ref, store, pair):
    high, low = v_ref[0, :, columns(pair)], v_ref[1, :, columns(pair)]
    out = (
        dot(first_back_ref[0], high)
        + dot(first_back_ref[0], low)
        + dot(first_back_ref[1], high)
    )
    for p in range(2):
        store(2 * pair + p, out[:, lanes(p)])


def steps(function, *ranges):
    return [functools.partial(function, *place) for place in itertools.product(*ranges)]


def interleave(*lines):
    for matrix, vector in lines:
        count = max(len(matrix), 1)
        for i in range(count):
            for step in matrix[i : i + 1]:
                step()
            for step in vector[i * len(vector) // count : (i + 1) * len(vector) // count]:
                step()


CHUNKS = [slice(i, i + CHUNK) for i in range(0, ROWS, CHUNK)]
PAIRS = range(TURNS // 2)
ALL_TURNS = range(TURNS)


def correlate_kernel(
    core_ref,
    x_ref,
    first_ref,
    first_back_ref,
    turn_ref,
    last_ref,
    last_back_ref,
    gated_ref,
    carried_ref,
    kept_ref,
    given_ref,
    mixed_ref,
    z_ref,
    product_ref,
    u_ref,
    v_ref,
    halves_ref,
):
    blocks, _, _, block_rows, _ = x_ref.shape
    core = core_ref[0]

    def store(p, value):
        halves_ref[p // 2, :, p % 2] = value.reshape(blocks, block_rows, INNER)

    spectra = (gated_ref, carried_ref)
    mixes = [functools.partial(mix, x_ref, first_ref, mixed_ref.at[a], a) for a in range(2)]
    opens = [functools.partial(opening, mixed_ref.at[a], turn_ref, z_ref.at[a]) for a in range(2)]
    lasts = [functools.partial(last, z_ref.at[a], last_ref, spectra[a]) for a in range(2)]
    products = functools.partial(product, carried_ref, gated_ref, True, product_ref)
    last_back = functools.partial(last, product_ref, last_back_ref, u_ref)
    close = functools.partial(closing, u_ref, turn_ref, v_ref)
    interleave(
        (steps(mixes[0], PAIRS, range(2)), []),
        (steps(mixes[1], PAIRS, range(2)), steps(opens[0], CHUNKS)),
        (steps(lasts[0], ALL_TURNS), steps(opens[1], CHUNKS)),
        (steps(lasts[1], [0]), []),
        (steps(lasts[1], ALL_TURNS[1:]), steps(products, ALL_TURNS[:-1], CHUNKS)),
        (steps(last_back, ALL_TURNS[:-1]), steps(products, ALL_TURNS[-1:], CHUNKS)),
        (steps(last_back, ALL_TURNS[-1:]), []),
        ([], steps(close, CHUNKS)),
        (steps(functools.partial(unmix, v_ref, first_back_ref, store), PAIRS), []),
    )
    kept_ref[...] = halves_ref[core]
    given_ref[...] = halves_ref[1 - core]


def convolve_kernel(
    x_ref,
    gated_ref,
    carried_ref,
    first_ref,
    first_back_ref,
    turn_ref,
    last_ref,
    last_back_ref,
    conv_ref,
    v_ref,
    mixed_ref,
    z_ref,
    filter_ref,
    product_ref,
    u_ref,
    v_conv_ref,
):
    blocks, _, _, block_rows, _ = x_ref.shape

    def store(p, value):
        conv_ref[:, p] = value.reshape(blocks, block_rows, INNER)

    v_refs = (v_conv_ref, v_ref)
    mixes = functools.partial(mix, x_ref, first_ref, mixed_ref, 2)
    opens = functools.partial(opening, mixed_ref, turn_ref, z_ref)
    lasts = functools.partial(last, z_ref, last_ref, filter_ref)

    def products(j, rows):
        product(gated_ref, filter_ref, False, product_ref.at[0], j, rows)
        product(carried_ref, filter_ref, True, product_ref.at[1], j, rows)

    def last_back(j, a):
        last(product_ref.at[a], last_back_ref, u_ref.at[a], j)

    close = [
        functools.partial(closing, u_ref.at[a], turn_ref, v_refs[a]) for a in range(2)
    ]
    interleave(
        (steps(mixes, PAIRS, range(2)), []),
        ([], steps(opens, CHUNKS)),
        (steps(lasts, [0]), []),
        (steps(lasts, ALL_TURNS[1:]), steps(products, ALL_TURNS[:-1], CHUNKS)),
        (steps(last_back, ALL_TURNS[:-1], range(2)), steps(products, ALL_TURNS[-1:], CHUNKS)),
        (steps(last_back, ALL_TURNS[-1:], [0]), []),
        (steps(last_back, ALL_TURNS[-1:], [1]), steps(close[0], CHUNKS)),
        (
            steps(functools.partial(unmix, v_conv_ref, first_back_ref, store), PAIRS),
            steps(close[1], CHUNKS),
        ),
    )


def gather_kernel(conv_ref, v_ref, first_back_ref, kept_ref, taken_ref, out_ref):
    blocks, _, block_rows, _ = conv_ref.shape

    def store(p, value):
        out_ref[:, TURNS + p] = value.reshape(blocks, block_rows, INNER)

    def rest(p):
        out_ref[:, p] = conv_ref[:, p]
        if p < 2:
            out_ref[:, 2 * TURNS + p] = kept_ref[:, p] + taken_ref[:, p]

    interleave(
        (steps(functools.partial(unmix, v_ref, first_back_ref, store), PAIRS), steps(rest, ALL_TURNS))
    )


def in_vmem(count):
    return [pl.BlockSpec(memory_space=pltpu.VMEM)] * count


def convolve(core, received, scale, exchange):
    first, first_back, turn, last_table, last_back = [
        jnp.asarray(table) for table in tables(scale)
    ]
    width = TURNS * INNER
    blocks, _, _, block_rows, _ = received.shape
    spectrum = (TURNS, ROWS, 2 * INNER)
    two_halves = jax.ShapeDtypeStruct((blocks, 2, block_rows, INNER), F32)
    params = pltpu.CompilerParams(vmem_limit_bytes=VMEM_BYTES)
    gated, carried, kept, given = pl.pallas_call(
        correlate_kernel,
        out_shape=(jax.ShapeDtypeStruct(spectrum, F32),) * 2 + (two_halves,) * 2,
        in_specs=[pl.BlockSpec(memory_space=pltpu.SMEM)] + in_vmem(6),
        out_specs=tuple(in_vmem(4)),
        scratch_shapes=[
            pltpu.VMEM((2, 2 * ROWS, width), F32),
            pltpu.VMEM((2, 2, *spectrum), BF16),
            pltpu.VMEM((2, *spectrum), BF16),
            pltpu.VMEM(spectrum, F32),
            pltpu.VMEM((2, 2 * ROWS, width), BF16),
            pltpu.VMEM((2, *two_halves.shape), F32),
        ],
        compiler_params=params,
        name="correlate",
    )(core, received, first, first_back, turn, last_table, last_back)
    taken = exchange(given)
    conv_out, mixed_adjoint = pl.pallas_call(
        convolve_kernel,
        out_shape=(
            jax.ShapeDtypeStruct((blocks, TURNS, block_rows, INNER), F32),
            jax.ShapeDtypeStruct((2, 2 * ROWS, width), BF16),
        ),
        in_specs=in_vmem(8),
        out_specs=tuple(in_vmem(2)),
        scratch_shapes=[
            pltpu.VMEM((2 * ROWS, width), F32),
            pltpu.VMEM((2, *spectrum), BF16),
            pltpu.VMEM(spectrum, F32),
            pltpu.VMEM((2, 2, *spectrum), BF16),
            pltpu.VMEM((2, *spectrum), F32),
            pltpu.VMEM((2, 2 * ROWS, width), BF16),
        ],
        compiler_params=params,
        name="convolve",
    )(received, gated, carried, first, first_back, turn, last_table, last_back)
    return pl.pallas_call(
        gather_kernel,
        out_shape=jax.ShapeDtypeStruct((blocks, 2 * TURNS + 2, block_rows, INNER), F32),
        in_specs=in_vmem(5),
        out_specs=in_vmem(1)[0],
        compiler_params=params,
        name="gather",
    )(conv_out, mixed_adjoint, first_back, kept, taken)


def pack_kernel(block_rows, place_ref, *refs):
    sources, sent_ref, held, built, sems, out_sems = refs[:5], refs[5], refs[6:11], *refs[11:]
    chan = place_ref[0]
    tall = 2 * GROUP
    tiles = range(0, sources[0].shape[0], tall)
    copies = []
    for t, tile in enumerate(tiles):
        for n in range(5):
            rows = pl.ds(tile, tall)
            copies.append(pltpu.make_async_copy(sources[n].at[rows], held[n].at[rows], sems.at[t, n]))
    for copy in copies:
        copy.start()
    outgoing = []
    q_ref, k_ref, v_ref, o_ref, f_ref = held
    for t, tile in enumerate(tiles):
        for copy in copies[5 * t : 5 * t + 5]:
            copy.wait()
        rows = slice(tile, tile + tall)
        for p in range(TURNS):
            values = [[], [], []]
            for m in range(block_rows):
                columns = lanes(m * TURNS + p)
                values[0].append(k_ref[rows, columns].astype(F32) * v_ref[rows, columns].astype(F32))
                values[1].append(q_ref[rows, columns].astype(F32) * o_ref[rows, columns].astype(F32))
                values[2].append(f_ref[rows, columns])
            for h in range(2):
                for a in range(SIGNALS):
                    block = jnp.stack([value[h * GROUP : (h + 1) * GROUP] for value in values[a]])
                    start = tile + h * GROUP
                    built[start : start + GROUP, a, p] = jnp.swapaxes(block, 0, 1)
        for h in range(2):
            start = tile + h * GROUP
            target = jnp.bitwise_xor(chan, start // GROUP) * GROUP
            copy = pltpu.make_async_copy(
                built.at[pl.ds(start, GROUP)], sent_ref.at[pl.ds(target, GROUP)], out_sems.at[t, h]
            )
            copy.start()
            outgoing.append(copy)
    for copy in outgoing:
        copy.wait()


def unpack_kernel(block_rows, place_ref, back_ref, k_ref, v_ref, o_ref, qg_ref, kg_ref, vg_ref):
    chan = place_ref[0]
    tall = 2 * GROUP
    for tile in range(0, k_ref.shape[0], tall):
        rows = slice(tile, tile + tall)
        bases = [jnp.bitwise_xor(chan, (tile + h * GROUP) // GROUP) * GROUP for h in range(2)]
        for p in range(TURNS):
            conv_out, adjoint = [
                jnp.concatenate(
                    [
                        jnp.swapaxes(back_ref[pl.ds(bases[h], GROUP), a * TURNS + p], 0, 1)
                        for h in range(2)
                    ],
                    axis=1,
                )
                for a in range(2)
            ]
            for m in range(block_rows):
                columns = lanes(m * TURNS + p)
                qg_ref[rows, columns] = (conv_out[m] * o_ref[rows, columns].astype(F32)).astype(BF16)
                kg_ref[rows, columns] = (adjoint[m] * v_ref[rows, columns].astype(F32)).astype(BF16)
                vg_ref[rows, columns] = (adjoint[m] * k_ref[rows, columns].astype(F32)).astype(BF16)


def total_kernel(block_rows, core_ref, *refs):
    grad_ref = refs[-1]
    for other in range(2):
        half = jnp.bitwise_xor(core_ref[0], other)
        for p in range(2):
            total = jnp.swapaxes(refs[other][:, p] + refs[other + 2][:, p], 0, 1)
            for m in range(block_rows):
                start = pl.multiple_of((m * TURNS + 2 * half + p) * INNER, INNER)
                grad_ref[:, pl.ds(start, INNER)] = total[m]


def local_call(kernel, name, out_shape, place, *arrays):
    count = len(arrays)
    specs = in_vmem(count)
    if place is not None:
        specs = [pl.BlockSpec(memory_space=pltpu.SMEM)] + specs
        arrays = (place,) + arrays
    single = not isinstance(out_shape, tuple)
    return pl.pallas_call(
        kernel,
        out_shape=out_shape,
        in_specs=specs,
        out_specs=in_vmem(1)[0] if single else tuple(in_vmem(len(out_shape))),
        compiler_params=pltpu.CompilerParams(vmem_limit_bytes=VMEM_BYTES),
        name=name,
    )(*arrays)


def pack(block_rows, place, arrays):
    slab, width = arrays[0].shape
    shape = (slab, SIGNALS, TURNS, block_rows, INNER)
    return pl.pallas_call(
        functools.partial(pack_kernel, block_rows),
        out_shape=jax.ShapeDtypeStruct(shape, F32),
        in_specs=[pl.BlockSpec(memory_space=pltpu.SMEM)] + [pl.BlockSpec(memory_space=pl.ANY)] * 5,
        out_specs=pl.BlockSpec(memory_space=pl.ANY),
        scratch_shapes=[pltpu.VMEM((slab, width), array.dtype) for array in arrays]
        + [
            pltpu.VMEM(shape, F32),
            pltpu.SemaphoreType.DMA((slab // (2 * GROUP), 5)),
            pltpu.SemaphoreType.DMA((slab // (2 * GROUP), 2)),
        ],
        compiler_params=pltpu.CompilerParams(vmem_limit_bytes=PACK_BYTES),
        name="pack",
    )(place, *arrays)


def shards(query_proj, key_proj, value_proj, out_cotangent, filter_raw):
    slab, width = query_proj.shape
    parts = lax.axis_size("seq")
    groups = lax.axis_size("chan")
    length = parts * width
    scale = 1.0 / (length * math.sqrt(length))
    block_rows = ROWS // parts
    chan = lax.axis_index("chan").astype(jnp.int32)
    core, place = (chan & 1).reshape(1), (chan & 2).reshape(1)

    def exchange(value, distance):
        return lax.ppermute(value, "chan", [(c, c ^ distance) for c in range(groups)])

    sent = pack(
        block_rows, place, (query_proj, key_proj, value_proj, out_cotangent, filter_raw)
    )
    starts = [((chan & 1) ^ k).astype(jnp.uint32) * GROUP for k in range(groups)]
    sent, core, place, starts = lax.optimization_barrier((sent, core, place, starts))
    received = lax.all_to_all(sent, "seq", split_axis=0, concat_axis=0, tiled=True)
    signals = convolve(core, received, scale, lambda value: exchange(value, 1))
    back = lax.all_to_all(signals, "seq", split_axis=0, concat_axis=0, tiled=True)
    pieces = []
    for k in range(groups):
        zero = jnp.uint32(0)
        place_of = (starts[k], jnp.uint32(2 * TURNS), zero, zero)
        piece = lax.dynamic_slice(back, place_of, (GROUP, 2, block_rows, INNER))
        pieces.append(exchange(piece, k) if k > 0 else piece)
    grads = local_call(
        functools.partial(unpack_kernel, block_rows),
        "unpack",
        (jax.ShapeDtypeStruct((slab, width), BF16),) * 3,
        place,
        back,
        key_proj,
        value_proj,
        out_cotangent,
    )
    filter_grad = local_call(
        functools.partial(total_kernel, block_rows),
        "total",
        jax.ShapeDtypeStruct((slab // groups, width), F32),
        core,
        *pieces,
    )
    return (*grads, filter_grad)


def solution(mesh):
    placed = (
        P("chan", "seq"),
        P("chan", "seq"),
        P("chan", "seq"),
        P("chan", "seq"),
        P(None, "seq"),
    )
    return jax.shard_map(
        shards,
        mesh=mesh,
        in_specs=placed,
        out_specs=(P("chan", "seq"), P("chan", "seq"), P("chan", "seq"), P("chan", "seq")),
        check_vma=False,
    )
```

time: 83.4 us -> 80.9 us (0.970)
  blocking collectives: 61.6 us -> 59.1 us
  waiting for transfers between devices: 4.32 us -> 2.11 us
  starting transfers between devices: 4.69 us -> 6.1 us
    all_to_all x1, blocking collectives: 27.4 us -> 24.9 us  [shards(): lax.all_to_all(signals, 'seq', split_axis=0, concat_axis=0, tiled=True)]
    ppermute x3 -> x4, waiting for transfers between devices: 4.32 us -> 2.11 us  [exchange(): lax.ppermute(value, 'chan', [(c, c ^ distance) for c in range(groups)])]
    ppermute x3 -> x4, starting transfers between devices: 4.69 us -> 6.1 us  [exchange(): lax.ppermute(value, 'chan', [(c, c ^ distance) for c in range(groups)])]
    pallas_call x1 -> x3, Pallas kernels: 6.88 us -> 7.85 us  [the longest x1 3.66 us: convolve(): pl.pallas_call(correlate_kernel, out_shape=(jax.ShapeDtypeStruct(spectrum...]
  transfers between devices with their start and end apart: 3 -> 4, of which waited for: 2 -> 1; matrix products, arithmetic and copies ran while one was open for 0% -> 0% of each run, Pallas kernels for 1% -> 6%
where the time goes in v6:
time: 80.9 us; the launch traced here: 80.6 us
  blocking collectives  59.1 us (73%)
  Pallas kernels  12.4 us (15%)
  starting transfers between devices  6.1 us (8%)
  waiting for transfers between devices  2.11 us (3%)
    all_to_all x1, blocking collectives, shards(): lax.all_to_all(sent, 'seq', split_axis=0, concat_axis=0, tiled=True)  34.2 us
    all_to_all x1, blocking collectives, shards(): lax.all_to_all(signals, 'seq', split_axis=0, concat_axis=0, tiled=True)  24.9 us
    ppermute x4, starting transfers between devices, exchange(): lax.ppermute(value, 'chan', [(c, c ^ distance) for c in range(groups)])  6.1 us
    pallas_call x1, Pallas kernels, convolve(): pl.pallas_call(correlate_kernel, out_shape=(jax.ShapeDtypeStruct(spectrum...  3.66 us
    pallas_call x1, Pallas kernels, convolve(): pl.pallas_call(convolve_kernel, out_shape=(jax.ShapeDtypeStruct((blocks,...  3.58 us
    pallas_call x1, Pallas kernels, pack(): pl.pallas_call(functools.partial(pack_kernel, block_rows), out_shape=jax....  2.77 us
    ppermute x4, waiting for transfers between devices, exchange(): lax.ppermute(value, 'chan', [(c, c ^ distance) for c in range(groups)])  2.11 us
    pallas_call x2, Pallas kernels, local_call(): pl.pallas_call(kernel, out_shape=out_shape, in_specs=specs, out_specs=in_...  1.83 us
  transfers between devices with their start and end apart: 4, of which 1 were waited for; matrix products, arithmetic and copies ran while one was open for 0% of the time, Pallas kernels for 6%

profile of v6, /device:TPU:1, one launch (start us, length us, event | category | flops | bytes accessed | tf_op | source)
XLA Modules:
  0.0 80.6 jit_solution(13239749001896027740)
XLA Ops:
  0.6 0.0 copy-start.3
  0.7 2.8 %pack.1 = f32[32,3,4,8,128]{4,3,2,1,0:T(8,128)} custom-call(s32[1]{0:T(128)} %bitcast.place_ref, bf16[32,4096]{1,0:T(8,128)(2,1)} %refs_0_.1, bf16[32,4096]{1,0:T(8,128)(2,1)} %k_ref.1, bf16[32,4096]{1,0:T(8,128)(2,1)} %v_ref.1, bf16[32,4096]{1,0:T(8,128)(2,1)} %o_ref.1, f32[32,4096]{1,0:T(8,128)} %refs_4_.1), custom_call_target="tpu_custom_call" | custom-call | tf_op jit(solution)/shard_map/pack/pallas_call | solution.py:473
  3.4 0.0 copy-start
  3.4 0.0 copy-start.1
  3.5 0.0 copy-start.2
  3.5 0.0 copy-start.4
  3.5 34.2 %all_to_all.10.x_ref = f32[32,3,4,8,128]{4,3,2,1,0:T(8,128)S(1)} all-to-all(f32[32,3,4,8,128]{4,3,2,1,0:T(8,128)} %pack.1), channel_id=1, replica_groups=mesh['seq'=32,'chan'=4] {'seq'}, dimensions={0} | all-to-all | bytes 3145728 | tf_op jit(solution)/shard_map/all_to_all | solution.py:507
  37.6 0.0 copy-done.3
  37.6 0.0 copy-done
  37.6 0.0 copy-done.1
  37.7 0.0 copy-done.2
  37.7 0.0 copy-done.4
  37.7 3.7 %correlate.1 = (f32[4,256,256]{2,1,0:T(8,128)S(1)}, f32[4,256,256]{2,1,0:T(8,128)S(1)}, f32[32,2,8,128]{3,2,1,0:T(8,128)S(1)}, f32[32,2,8,128]{3,2,1,0:T(8,128)S(1)}) custom-call(s32[1]{0:T(128)} %bitcast.1.core_ref, f32[32,3,4,8,128]{4,3,2,1,0:T(8,128)S(1)} %all_to_all.10.x_ref, bf16[2,512,256]{2,1,0:T(8,128)(2,1)S(1)} %copy-done.4, ...), custom_call_target="tpu_custom_call" | custom-call | tf_op jit(solution)/shard_map/correlate/pallas_call | solution.py:330
  41.3 2.8 %collective-permute-start = (f32[32,2,8,128]{3,2,1,0:T(8,128)S(1)}, f32[32,2,8,128]{3,2,1,0:T(8,128)S(1)}, u32[]{:S(2)}, u32[]{:S(2)}) collective-permute-start(f32[32,2,8,128]{3,2,1,0:T(8,128)S(1)} %get-tuple-element.28), channel_id=1, source_target_pairs={{0,1},{1,0},{2,3},{3,2},{4,5},{5,4},{6,7},{7,6},{8,9},{9,8},{10,11... | collective-permute-start | bytes 786440 | tf_op jit(solution)/shard_map/ppermute | solution.py:500
  44.2 3.6 %convolve.1 = (f32[32,4,8,128]{3,2,1,0:T(8,128)S(1)}, bf16[2,512,512]{2,1,0:T(8,128)(2,1)S(1)}) custom-call(f32[32,3,4,8,128]{4,3,2,1,0:T(8,128)S(1)} %all_to_all.10.x_ref, f32[4,256,256]{2,1,0:T(8,128)S(1)} %get-tuple-element.23.gated_ref, f32[4,256,256]{2,1,0:T(8,128)S(1)} %get-tuple-element.24.carried_ref, bf16[2,512,256]{2,1,0:T(8,128)(2,1)S(1)} %copy-done.4, ...), custom_call_target="tpu_custom_call" | custom-call | tf_op jit(solution)/shard_map/convolve/pallas_call | solution.py:347
  47.8 0.0 collective-permute-done.taken_ref
  47.8 0.6 gather.1
  48.4 0.0 copy-start.5
  48.4 0.0 copy-start.6
  48.4 0.0 copy-start.7
  48.4 24.9 %all_to_all.11.back_ref = f32[32,10,8,128]{3,2,1,0:T(8,128)S(1)} all-to-all(f32[32,10,8,128]{3,2,1,0:T(8,128)S(1)} %gather.1), channel_id=1, replica_groups=mesh['seq'=32,'chan'=4] {'seq'}, dimensions={0} | all-to-all | bytes 2621440 | tf_op jit(solution)/shard_map/all_to_all | solution.py:509
  73.4 2.2 %collective-permute-start.3 = (f32[8,2,8,128]{3,2,1,0:T(8,128)S(1)}, f32[8,2,8,128]{3,2,1,0:T(8,128)S(1)}, u32[]{:S(2)}, u32[]{:S(2)}) collective-permute-start(f32[8,2,8,128]{3,2,1,0:T(8,128)S(1)} %get-tuple-element.36), channel_id=1, source_target_pairs={{0,3},{1,2},{2,1},{3,0},{4,7},{5,6},{6,5},{7,4},{8,11},{9,10},{10,... | collective-permute-start | bytes 196616 | tf_op jit(solution)/shard_map/ppermute | solution.py:500
  75.6 1.1 %collective-permute-start.2 = (f32[8,2,8,128]{3,2,1,0:T(8,128)S(1)}, f32[8,2,8,128]{3,2,1,0:T(8,128)S(1)}, u32[]{:S(2)}, u32[]{:S(2)}) collective-permute-start(f32[8,2,8,128]{3,2,1,0:T(8,128)S(1)} %get-tuple-element.37), channel_id=1, source_target_pairs={{0,2},{1,3},{2,0},{3,1},{4,6},{5,7},{6,4},{7,5},{8,10},{9,11},{10,... | collective-permute-start | bytes 196616 | tf_op jit(solution)/shard_map/ppermute | solution.py:500
  76.7 0.0 collective-permute-start.1
  76.7 0.0 copy-done.5
  76.7 0.0 copy-done.6
  76.7 0.0 copy-done.7
  76.7 1.1 %unpack.1 = (bf16[32,4096]{1,0:T(8,128)(2,1)}, bf16[32,4096]{1,0:T(8,128)(2,1)}, bf16[32,4096]{1,0:T(8,128)(2,1)}) custom-call(s32[1]{0:T(128)} %bitcast.place_ref, f32[32,10,8,128]{3,2,1,0:T(8,128)S(1)} %all_to_all.11.back_ref, bf16[32,4096]{1,0:T(8,128)(2,1)S(1)} %copy-done.5, bf16[32,4096]{1,0:T(8,128)(2,1)S(1)} %copy-done.6, bf16[32,4096]{1,0:T(8,128)(2,1)S(1)} %copy-done.7), custom_call_target="tpu_custom_call" | custom-call | tf_op jit(solution)/shard_map/unpack/pallas_call | solution.py:460
  77.8 0.0 collective-permute-done.3.refs_3_
  77.8 2.1 %collective-permute-done.2.refs_2_ = f32[8,2,8,128]{3,2,1,0:T(8,128)S(1)} collective-permute-done((f32[8,2,8,128]{3,2,1,0:T(8,128)S(1)}, f32[8,2,8,128]{3,2,1,0:T(8,128)S(1)}, u32[]{:S(2)}, u32[]{:S(2)}) %collective-permute-start.2) | collective-permute-done | bytes 65568 | tf_op jit(solution)/shard_map/ppermute | solution.py:500
  79.9 0.0 collective-permute-done.1.refs_1_
  79.9 0.7 total.1
  (1 shorter events, 0.0 us)
Async XLA Ops:
  0.6 37.0 %copy-start.3 = (f32[2,256,512]{2,1,0:T(8,128)S(1)}, f32[2,256,512]{2,1,0:T(8,128)}, u32[]{:S(2)}) copy-start(f32[2,256,512]{2,1,0:T(8,128)} %constant.26.clone.turn_ref) | copy-start | bytes 3145732
  3.4 34.2 %copy-start = (bf16[2,256,512]{2,1,0:T(8,128)(2,1)S(1)}, bf16[2,256,512]{2,1,0:T(8,128)(2,1)}, u32[]{:S(2)}) copy-start(bf16[2,256,512]{2,1,0:T(8,128)(2,1)} %constant.25.clone.first_back_ref) | copy-start | bytes 1572868
  3.4 34.2 %copy-start.1 = (bf16[2,4,256,256]{3,2,1,0:T(8,128)(2,1)S(1)}, bf16[2,4,256,256]{3,2,1,0:T(8,128)(2,1)}, u32[]{:S(2)}) copy-start(bf16[2,4,256,256]{3,2,1,0:T(8,128)(2,1)} %constant.28.clone.last_back_ref) | copy-start | bytes 3145732
  3.5 34.2 %copy-start.2 = (bf16[2,4,256,256]{3,2,1,0:T(8,128)(2,1)S(1)}, bf16[2,4,256,256]{3,2,1,0:T(8,128)(2,1)}, u32[]{:S(2)}) copy-start(bf16[2,4,256,256]{3,2,1,0:T(8,128)(2,1)} %constant.27.clone.last_ref) | copy-start | bytes 3145732
  3.5 34.2 %copy-start.4 = (bf16[2,512,256]{2,1,0:T(8,128)(2,1)S(1)}, bf16[2,512,256]{2,1,0:T(8,128)(2,1)}, u32[]{:S(2)}) copy-start(bf16[2,512,256]{2,1,0:T(8,128)(2,1)} %constant.24.clone.first_ref) | copy-start | bytes 1572868
  41.3 6.4 %collective-permute-start = (f32[32,2,8,128]{3,2,1,0:T(8,128)S(1)}, f32[32,2,8,128]{3,2,1,0:T(8,128)S(1)}, u32[]{:S(2)}, u32[]{:S(2)}) collective-permute-start(f32[32,2,8,128]{3,2,1,0:T(8,128)S(1)} %get-tuple-element.28), channel_id=1, source_target_pairs={{0,1},{1,0},{2,3},{3,2},{4,5},{5,4},{6,7},{7,6},{8,9},{9,8},{10,11... | collective-permute-start | bytes 786440 | tf_op jit(solution)/shard_map/ppermute | solution.py:500
  48.4 28.3 %copy-start.5 = (bf16[32,4096]{1,0:T(8,128)(2,1)S(1)}, bf16[32,4096]{1,0:T(8,128)(2,1)}, u32[]{:S(2)}) copy-start(bf16[32,4096]{1,0:T(8,128)(2,1)} %k_ref.1) | copy-start | bytes 786436
  48.4 28.3 %copy-start.6 = (bf16[32,4096]{1,0:T(8,128)(2,1)S(1)}, bf16[32,4096]{1,0:T(8,128)(2,1)}, u32[]{:S(2)}) copy-start(bf16[32,4096]{1,0:T(8,128)(2,1)} %v_ref.1) | copy-start | bytes 786436
  48.4 28.3 %copy-start.7 = (bf16[32,4096]{1,0:T(8,128)(2,1)S(1)}, bf16[32,4096]{1,0:T(8,128)(2,1)}, u32[]{:S(2)}) copy-start(bf16[32,4096]{1,0:T(8,128)(2,1)} %o_ref.1) | copy-start | bytes 786436
  73.4 4.4 %collective-permute-start.3 = (f32[8,2,8,128]{3,2,1,0:T(8,128)S(1)}, f32[8,2,8,128]{3,2,1,0:T(8,128)S(1)}, u32[]{:S(2)}, u32[]{:S(2)}) collective-permute-start(f32[8,2,8,128]{3,2,1,0:T(8,128)S(1)} %get-tuple-element.36), channel_id=1, source_target_pairs={{0,3},{1,2},{2,1},{3,0},{4,7},{5,6},{6,5},{7,4},{8,11},{9,10},{10,... | collective-permute-start | bytes 196616 | tf_op jit(solution)/shard_map/ppermute | solution.py:500
  75.6 4.4 %collective-permute-start.2 = (f32[8,2,8,128]{3,2,1,0:T(8,128)S(1)}, f32[8,2,8,128]{3,2,1,0:T(8,128)S(1)}, u32[]{:S(2)}, u32[]{:S(2)}) collective-permute-start(f32[8,2,8,128]{3,2,1,0:T(8,128)S(1)} %get-tuple-element.37), channel_id=1, source_target_pairs={{0,2},{1,3},{2,0},{3,1},{4,6},{5,7},{6,4},{7,5},{8,10},{9,11},{10,... | collective-permute-start | bytes 196616 | tf_op jit(solution)/shard_map/ppermute | solution.py:500
  76.7 3.3 %collective-permute-start.1 = (f32[8,2,8,128]{3,2,1,0:T(8,128)S(1)}, f32[8,2,8,128]{3,2,1,0:T(8,128)S(1)}, u32[]{:S(2)}, u32[]{:S(2)}) collective-permute-start(f32[8,2,8,128]{3,2,1,0:T(8,128)S(1)} %get-tuple-element.38), channel_id=1, source_target_pairs={{0,1},{1,0},{2,3},{3,2},{4,5},{5,4},{6,7},{7,6},{8,9},{9,8},{10,11... | collective-permute-start | bytes 196616 | tf_op jit(solution)/shard_map/ppermute | solution.py:500

commit v7 on v6

--- a/solution.py
+++ b/solution.py
@@ -112,13 +112,13 @@
     return slice(2 * pair * INNER, 2 * (pair + 1) * INNER)
 
 
-def mix(x_ref, first_ref, mixed_ref, a, pair, part):
+def mix(x_ref, first_ref, mixed_ref, place, first_slot, part):
     data = jnp.concatenate(
-        [x_ref[:, a, 2 * pair + p].reshape(ROWS, INNER) for p in range(2)], axis=1
+        [x_ref[:, first_slot + p].reshape(ROWS, INNER) for p in range(2)], axis=1
     )
     high, low = split(data)
     rows = slice(part * ROWS, (part + 1) * ROWS)
-    mixed_ref[rows, columns(pair)] = (
+    mixed_ref[rows, place] = (
         dot(first_ref[0, rows], high)
         + dot(first_ref[0, rows], low)
         + dot(first_ref[1, rows], high)
@@ -217,22 +217,24 @@
     v_ref,
     halves_ref,
 ):
-    blocks, _, _, block_rows, _ = x_ref.shape
+    blocks, _, block_rows, _ = x_ref.shape
     core = core_ref[0]
 
     def store(p, value):
         halves_ref[p // 2, :, p % 2] = value.reshape(blocks, block_rows, INNER)
 
     spectra = (gated_ref, carried_ref)
-    mixes = [functools.partial(mix, x_ref, first_ref, mixed_ref.at[a], a) for a in range(2)]
+    def mixes(a, pair, part):
+        mix(x_ref, first_ref, mixed_ref.at[a], columns(pair), a * TURNS + 2 * pair, part)
+
     opens = [functools.partial(opening, mixed_ref.at[a], turn_ref, z_ref.at[a]) for a in range(2)]
     lasts = [functools.partial(last, z_ref.at[a], last_ref, spectra[a]) for a in range(2)]
     products = functools.partial(product, carried_ref, gated_ref, True, product_ref)
     last_back = functools.partial(last, product_ref, last_back_ref, u_ref)
     close = functools.partial(closing, u_ref, turn_ref, v_ref)
     interleave(
-        (steps(mixes[0], PAIRS, range(2)), []),
-        (steps(mixes[1], PAIRS, range(2)), steps(opens[0], CHUNKS)),
+        (steps(mixes, [0], PAIRS, range(2)), []),
+        (steps(mixes, [1], PAIRS, range(2)), steps(opens[0], CHUNKS)),
         (steps(lasts[0], ALL_TURNS), steps(opens[1], CHUNKS)),
         (steps(lasts[1], [0]), []),
         (steps(lasts[1], ALL_TURNS[1:]), steps(products, ALL_TURNS[:-1], CHUNKS)),
@@ -246,7 +248,9 @@
 
 
 def convolve_kernel(
+    core_ref,
     x_ref,
+    other_ref,
     gated_ref,
     carried_ref,
     first_ref,
@@ -263,13 +267,19 @@
     u_ref,
     v_conv_ref,
 ):
-    blocks, _, _, block_rows, _ = x_ref.shape
+    blocks, _, block_rows, _ = x_ref.shape
+    wide = 2 * INNER
 
     def store(p, value):
         conv_ref[:, p] = value.reshape(blocks, block_rows, INNER)
 
     v_refs = (v_conv_ref, v_ref)
-    mixes = functools.partial(mix, x_ref, first_ref, mixed_ref, 2)
+
+    def mixes(other, part):
+        start = pl.multiple_of(jnp.bitwise_xor(core_ref[0], other) * wide, wide)
+        source, first_slot = ((x_ref, 2 * TURNS), (other_ref, 0))[other]
+        mix(source, first_ref, mixed_ref, pl.ds(start, wide), first_slot, part)
+
     opens = functools.partial(opening, mixed_ref, turn_ref, z_ref)
     lasts = functools.partial(last, z_ref, last_ref, filter_ref)
 
@@ -284,7 +294,7 @@
         functools.partial(closing, u_ref.at[a], turn_ref, v_refs[a]) for a in range(2)
     ]
     interleave(
-        (steps(mixes, PAIRS, range(2)), []),
+        (steps(mixes, range(2), range(2)), []),
         ([], steps(opens, CHUNKS)),
         (steps(lasts, [0]), []),
         (steps(lasts, ALL_TURNS[1:]), steps(products, ALL_TURNS[:-1], CHUNKS)),
@@ -323,7 +333,8 @@
         jnp.asarray(table) for table in tables(scale)
     ]
     width = TURNS * INNER
-    blocks, _, _, block_rows, _ = received.shape
+    blocks, _, block_rows, _ = received.shape
+    other_filter = exchange(received[:, 2 * TURNS :])
     spectrum = (TURNS, ROWS, 2 * INNER)
     two_halves = jax.ShapeDtypeStruct((blocks, 2, block_rows, INNER), F32)
     params = pltpu.CompilerParams(vmem_limit_bytes=VMEM_BYTES)
@@ -350,7 +361,7 @@
             jax.ShapeDtypeStruct((blocks, TURNS, block_rows, INNER), F32),
             jax.ShapeDtypeStruct((2, 2 * ROWS, width), BF16),
         ),
-        in_specs=in_vmem(8),
+        in_specs=[pl.BlockSpec(memory_space=pltpu.SMEM)] + in_vmem(9),
         out_specs=tuple(in_vmem(2)),
         scratch_shapes=[
             pltpu.VMEM((2 * ROWS, width), F32),
@@ -362,7 +373,7 @@
         ],
         compiler_params=params,
         name="convolve",
-    )(received, gated, carried, first, first_back, turn, last_table, last_back)
+    )(core, received, other_filter, gated, carried, first, first_back, turn, last_table, last_back)
     return pl.pallas_call(
         gather_kernel,
         out_shape=jax.ShapeDtypeStruct((blocks, 2 * TURNS + 2, block_rows, INNER), F32),
@@ -373,7 +384,7 @@
     )(conv_out, mixed_adjoint, first_back, kept, taken)
 
 
-def pack_kernel(block_rows, place_ref, *refs):
+def pack_kernel(block_rows, place_ref, core_ref, *refs):
     sources, sent_ref, held, built, sems, out_sems = refs[:5], refs[5], refs[6:11], *refs[11:]
     chan = place_ref[0]
     tall = 2 * GROUP
@@ -393,16 +404,19 @@
         rows = slice(tile, tile + tall)
         for p in range(TURNS):
             values = [[], [], []]
+            half = 2 * core_ref[0] + p
             for m in range(block_rows):
                 columns = lanes(m * TURNS + p)
                 values[0].append(k_ref[rows, columns].astype(F32) * v_ref[rows, columns].astype(F32))
                 values[1].append(q_ref[rows, columns].astype(F32) * o_ref[rows, columns].astype(F32))
-                values[2].append(f_ref[rows, columns])
+                if p < 2:
+                    start = pl.multiple_of((m * TURNS + half) * INNER, INNER)
+                    values[2].append(f_ref[rows, pl.ds(start, INNER)])
             for h in range(2):
-                for a in range(SIGNALS):
+                for a in range(SIGNALS if p < 2 else 2):
                     block = jnp.stack([value[h * GROUP : (h + 1) * GROUP] for value in values[a]])
                     start = tile + h * GROUP
-                    built[start : start + GROUP, a, p] = jnp.swapaxes(block, 0, 1)
+                    built[start : start + GROUP, a * TURNS + p] = jnp.swapaxes(block, 0, 1)
         for h in range(2):
             start = tile + h * GROUP
             target = jnp.bitwise_xor(chan, start // GROUP) * GROUP
@@ -467,13 +481,14 @@
     )(*arrays)
 
 
-def pack(block_rows, place, arrays):
+def pack(block_rows, place, core, arrays):
     slab, width = arrays[0].shape
-    shape = (slab, SIGNALS, TURNS, block_rows, INNER)
+    shape = (slab, 2 * TURNS + 2, block_rows, INNER)
     return pl.pallas_call(
         functools.partial(pack_kernel, block_rows),
         out_shape=jax.ShapeDtypeStruct(shape, F32),
-        in_specs=[pl.BlockSpec(memory_space=pltpu.SMEM)] + [pl.BlockSpec(memory_space=pl.ANY)] * 5,
+        in_specs=[pl.BlockSpec(memory_space=pltpu.SMEM)] * 2
+        + [pl.BlockSpec(memory_space=pl.ANY)] * 5,
         out_specs=pl.BlockSpec(memory_space=pl.ANY),
         scratch_shapes=[pltpu.VMEM((slab, width), array.dtype) for array in arrays]
         + [
@@ -483,7 +498,7 @@
         ],
         compiler_params=pltpu.CompilerParams(vmem_limit_bytes=PACK_BYTES),
         name="pack",
-    )(place, *arrays)
+    )(place, core, *arrays)
 
 
 def shards(query_proj, key_proj, value_proj, out_cotangent, filter_raw):
@@ -500,7 +515,7 @@
         return lax.ppermute(value, "chan", [(c, c ^ distance) for c in range(groups)])
 
     sent = pack(
-        block_rows, place, (query_proj, key_proj, value_proj, out_cotangent, filter_raw)
+        block_rows, place, core, (query_proj, key_proj, value_proj, out_cotangent, filter_raw)
     )
     starts = [((chan & 1) ^ k).astype(jnp.uint32) * GROUP for k in range(groups)]
     sent, core, place, starts = lax.optimization_barrier((sent, core, place, starts))

time: 80.9 us -> 78.2 us (0.967)
  blocking collectives: 59.1 us -> 56.1 us
    all_to_all x1, blocking collectives: 34.2 us -> 32.1 us  [shards(): lax.all_to_all(sent, 'seq', split_axis=0, concat_axis=0, tiled=True)]
    all_to_all x1, blocking collectives: 24.9 us -> 24 us  [shards(): lax.all_to_all(signals, 'seq', split_axis=0, concat_axis=0, tiled=True)]
    ppermute x4 -> x5, starting transfers between devices: 6.1 us -> 6.44 us  [exchange(): lax.ppermute(value, 'chan', [(c, c ^ distance) for c in range(groups)])]
    ppermute x4 -> x5, waiting for transfers between devices: 2.11 us -> 2.12 us  [exchange(): lax.ppermute(value, 'chan', [(c, c ^ distance) for c in range(groups)])]
  transfers between devices with their start and end apart: 4 -> 5, of which waited for: 1 -> 1; matrix products, arithmetic and copies ran while one was open for 0% -> 0% of each run, Pallas kernels for 6% -> 11%
where the time goes in v7:
time: 78.2 us; the launch traced here: 77.9 us
  blocking collectives  56.1 us (72%)
  Pallas kernels  12.4 us (16%)
  starting transfers between devices  6.44 us (8%)
  waiting for transfers between devices  2.12 us (3%)
    all_to_all x1, blocking collectives, shards(): lax.all_to_all(sent, 'seq', split_axis=0, concat_axis=0, tiled=True)  32.1 us
    all_to_all x1, blocking collectives, shards(): lax.all_to_all(signals, 'seq', split_axis=0, concat_axis=0, tiled=True)  24 us
    ppermute x5, starting transfers between devices, exchange(): lax.ppermute(value, 'chan', [(c, c ^ distance) for c in range(groups)])  6.44 us
    pallas_call x1, Pallas kernels, convolve(): pl.pallas_call(convolve_kernel, out_shape=(jax.ShapeDtypeStruct((blocks,...  3.63 us
    pallas_call x1, Pallas kernels, convolve(): pl.pallas_call(correlate_kernel, out_shape=(jax.ShapeDtypeStruct(spectrum...  3.61 us
    pallas_call x1, Pallas kernels, pack(): pl.pallas_call(functools.partial(pack_kernel, block_rows), out_shape=jax....  2.67 us
    ppermute x5, waiting for transfers between devices, exchange(): lax.ppermute(value, 'chan', [(c, c ^ distance) for c in range(groups)])  2.12 us
    pallas_call x2, Pallas kernels, local_call(): pl.pallas_call(kernel, out_shape=out_shape, in_specs=specs, out_specs=in_...  1.82 us
  transfers between devices with their start and end apart: 5, of which 1 were waited for; matrix products, arithmetic and copies ran while one was open for 0% of the time, Pallas kernels for 11%

profile of v7, /device:TPU:1, one launch (start us, length us, event | category | flops | bytes accessed | tf_op | source)
XLA Modules:
  0.0 77.9 jit_solution(8930082726489275152)
XLA Ops:
  0.6 0.0 copy-start.3
  0.7 2.7 %pack.1 = f32[32,10,8,128]{3,2,1,0:T(8,128)} custom-call(s32[1]{0:T(128)} %bitcast.place_ref, s32[1]{0:T(128)} %bitcast.1.core_ref, bf16[32,4096]{1,0:T(8,128)(2,1)} %refs_0_.1, bf16[32,4096]{1,0:T(8,128)(2,1)} %k_ref.1, bf16[32,4096]{1,0:T(8,128)(2,1)} %v_ref.1, bf16[32,4096]{1,0:T(8,128)(2,1)} %o_ref.1, f32[32,4096]{1,0:T(8,128)} %refs_4_.1), custom_call_target="tpu_custom_call" | custom-call | tf_op jit(solution)/shard_map/pack/pallas_call | solution.py:487
  3.3 0.0 copy-start
  3.3 0.0 copy-start.1
  3.4 0.0 copy-start.2
  3.4 0.0 copy-start.4
  3.4 32.1 %all_to_all.10.x_ref = f32[32,10,8,128]{3,2,1,0:T(8,128)S(1)} all-to-all(f32[32,10,8,128]{3,2,1,0:T(8,128)} %pack.1), channel_id=1, replica_groups=mesh['seq'=32,'chan'=4] {'seq'}, dimensions={0} | all-to-all | bytes 2621440 | tf_op jit(solution)/shard_map/all_to_all | solution.py:522
  35.5 2.5 %collective-permute-start = (f32[32,2,8,128]{3,2,1,0:T(8,128)S(1)}, f32[32,2,8,128]{3,2,1,0:T(8,128)S(1)}, u32[]{:S(2)}, u32[]{:S(2)}) collective-permute-start(f32[32,2,8,128]{3,2,1,0:T(8,128)S(1)} %slice.4), channel_id=1, source_target_pairs={{0,1},{1,0},{2,3},{3,2},{4,5},{5,4},{6,7},{7,6},{8,9},{9,8},{10,11... | collective-permute-start | bytes 786440 | tf_op jit(solution)/shard_map/ppermute | solution.py:515
  38.0 0.0 copy-done.3
  38.0 0.0 copy-done
  38.0 0.0 copy-done.1
  38.0 0.0 copy-done.2
  38.0 0.0 copy-done.4
  38.0 3.6 %correlate.1 = (f32[4,256,256]{2,1,0:T(8,128)S(1)}, f32[4,256,256]{2,1,0:T(8,128)S(1)}, f32[32,2,8,128]{3,2,1,0:T(8,128)S(1)}, f32[32,2,8,128]{3,2,1,0:T(8,128)S(1)}) custom-call(s32[1]{0:T(128)} %bitcast.1.core_ref, f32[32,10,8,128]{3,2,1,0:T(8,128)S(1)} %all_to_all.10.x_ref, bf16[2,512,256]{2,1,0:T(8,128)(2,1)S(1)} %copy-done.4, ...), custom_call_target="tpu_custom_call" | custom-call | tf_op jit(solution)/shard_map/correlate/pallas_call | solution.py:341
  41.7 0.1 collective-permute-start.1
  41.8 0.0 collective-permute-done.other_ref
  41.8 3.6 %convolve.1 = (f32[32,4,8,128]{3,2,1,0:T(8,128)S(1)}, bf16[2,512,512]{2,1,0:T(8,128)(2,1)S(1)}) custom-call(s32[1]{0:T(128)} %bitcast.1.core_ref, f32[32,10,8,128]{3,2,1,0:T(8,128)S(1)} %all_to_all.10.x_ref, f32[32,2,8,128]{3,2,1,0:T(8,128)S(1)} %collective-permute-done.other_ref, f32[4,256,256]{2,1,0:T(8,128)S(1)} %get-tuple-element.23.gated_ref, ...), custom_call_target="tpu_custom_call" | custom-call | tf_op jit(solution)/shard_map/convolve/pallas_call | solution.py:358
  45.4 0.0 collective-permute-done.1.taken_ref
  45.4 0.6 gather.1
  46.1 0.0 copy-start.5
  46.1 0.0 copy-start.6
  46.1 0.0 copy-start.7
  46.1 24.0 %all_to_all.11.back_ref = f32[32,10,8,128]{3,2,1,0:T(8,128)S(1)} all-to-all(f32[32,10,8,128]{3,2,1,0:T(8,128)S(1)} %gather.1), channel_id=1, replica_groups=mesh['seq'=32,'chan'=4] {'seq'}, dimensions={0} | all-to-all | bytes 2621440 | tf_op jit(solution)/shard_map/all_to_all | solution.py:524
  70.1 2.7 %collective-permute-start.4 = (f32[8,2,8,128]{3,2,1,0:T(8,128)S(1)}, f32[8,2,8,128]{3,2,1,0:T(8,128)S(1)}, u32[]{:S(2)}, u32[]{:S(2)}) collective-permute-start(f32[8,2,8,128]{3,2,1,0:T(8,128)S(1)} %get-tuple-element.36), channel_id=1, source_target_pairs={{0,3},{1,2},{2,1},{3,0},{4,7},{5,6},{6,5},{7,4},{8,11},{9,10},{10,... | collective-permute-start | bytes 196616 | tf_op jit(solution)/shard_map/ppermute | solution.py:515
  72.9 1.1 %collective-permute-start.3 = (f32[8,2,8,128]{3,2,1,0:T(8,128)S(1)}, f32[8,2,8,128]{3,2,1,0:T(8,128)S(1)}, u32[]{:S(2)}, u32[]{:S(2)}) collective-permute-start(f32[8,2,8,128]{3,2,1,0:T(8,128)S(1)} %get-tuple-element.37), channel_id=1, source_target_pairs={{0,2},{1,3},{2,0},{3,1},{4,6},{5,7},{6,4},{7,5},{8,10},{9,11},{10,... | collective-permute-start | bytes 196616 | tf_op jit(solution)/shard_map/ppermute | solution.py:515
  73.9 0.0 collective-permute-start.2
  73.9 0.0 copy-done.5
  74.0 1.1 %unpack.1 = (bf16[32,4096]{1,0:T(8,128)(2,1)}, bf16[32,4096]{1,0:T(8,128)(2,1)}, bf16[32,4096]{1,0:T(8,128)(2,1)}) custom-call(s32[1]{0:T(128)} %bitcast.place_ref, f32[32,10,8,128]{3,2,1,0:T(8,128)S(1)} %all_to_all.11.back_ref, bf16[32,4096]{1,0:T(8,128)(2,1)S(1)} %copy-done.5, bf16[32,4096]{1,0:T(8,128)(2,1)S(1)} %copy-done.6, bf16[32,4096]{1,0:T(8,128)(2,1)S(1)} %copy-done.7), custom_call_target="tpu_custom_call" | custom-call | tf_op jit(solution)/shard_map/unpack/pallas_call | solution.py:474
  75.1 0.0 collective-permute-done.4.refs_3_
  75.1 2.1 %collective-permute-done.3.refs_2_ = f32[8,2,8,128]{3,2,1,0:T(8,128)S(1)} collective-permute-done((f32[8,2,8,128]{3,2,1,0:T(8,128)S(1)}, f32[8,2,8,128]{3,2,1,0:T(8,128)S(1)}, u32[]{:S(2)}, u32[]{:S(2)}) %collective-permute-start.3) | collective-permute-done | bytes 65568 | tf_op jit(solution)/shard_map/ppermute | solution.py:515
  77.2 0.0 collective-permute-done.2.refs_1_
  77.2 0.7 total.1
  (4 shorter events, 0.0 us)
Async XLA Ops:
  0.6 37.4 %copy-start.3 = (f32[2,256,512]{2,1,0:T(8,128)S(1)}, f32[2,256,512]{2,1,0:T(8,128)}, u32[]{:S(2)}) copy-start(f32[2,256,512]{2,1,0:T(8,128)} %constant.26.clone.turn_ref) | copy-start | bytes 3145732
  3.3 34.7 %copy-start = (bf16[2,256,512]{2,1,0:T(8,128)(2,1)S(1)}, bf16[2,256,512]{2,1,0:T(8,128)(2,1)}, u32[]{:S(2)}) copy-start(bf16[2,256,512]{2,1,0:T(8,128)(2,1)} %constant.25.clone.first_back_ref) | copy-start | bytes 1572868
  3.3 34.7 %copy-start.1 = (bf16[2,4,256,256]{3,2,1,0:T(8,128)(2,1)S(1)}, bf16[2,4,256,256]{3,2,1,0:T(8,128)(2,1)}, u32[]{:S(2)}) copy-start(bf16[2,4,256,256]{3,2,1,0:T(8,128)(2,1)} %constant.28.clone.last_back_ref) | copy-start | bytes 3145732
  3.4 34.7 %copy-start.2 = (bf16[2,4,256,256]{3,2,1,0:T(8,128)(2,1)S(1)}, bf16[2,4,256,256]{3,2,1,0:T(8,128)(2,1)}, u32[]{:S(2)}) copy-start(bf16[2,4,256,256]{3,2,1,0:T(8,128)(2,1)} %constant.27.clone.last_ref) | copy-start | bytes 3145732
  3.4 34.7 %copy-start.4 = (bf16[2,512,256]{2,1,0:T(8,128)(2,1)S(1)}, bf16[2,512,256]{2,1,0:T(8,128)(2,1)}, u32[]{:S(2)}) copy-start(bf16[2,512,256]{2,1,0:T(8,128)(2,1)} %constant.24.clone.first_ref) | copy-start | bytes 1572868
  35.5 6.3 %collective-permute-start = (f32[32,2,8,128]{3,2,1,0:T(8,128)S(1)}, f32[32,2,8,128]{3,2,1,0:T(8,128)S(1)}, u32[]{:S(2)}, u32[]{:S(2)}) collective-permute-start(f32[32,2,8,128]{3,2,1,0:T(8,128)S(1)} %slice.4), channel_id=1, source_target_pairs={{0,1},{1,0},{2,3},{3,2},{4,5},{5,4},{6,7},{7,6},{8,9},{9,8},{10,11... | collective-permute-start | bytes 786440 | tf_op jit(solution)/shard_map/ppermute | solution.py:515
  41.7 3.8 %collective-permute-start.1 = (f32[32,2,8,128]{3,2,1,0:T(8,128)S(1)}, f32[32,2,8,128]{3,2,1,0:T(8,128)S(1)}, u32[]{:S(2)}, u32[]{:S(2)}) collective-permute-start(f32[32,2,8,128]{3,2,1,0:T(8,128)S(1)} %get-tuple-element.28), channel_id=1, source_target_pairs={{0,1},{1,0},{2,3},{3,2},{4,5},{5,4},{6,7},{7,6},{8,9},{9,8},{10,11... | collective-permute-start | bytes 786440 | tf_op jit(solution)/shard_map/ppermute | solution.py:515
  46.1 27.9 %copy-start.5 = (bf16[32,4096]{1,0:T(8,128)(2,1)S(1)}, bf16[32,4096]{1,0:T(8,128)(2,1)}, u32[]{:S(2)}) copy-start(bf16[32,4096]{1,0:T(8,128)(2,1)} %k_ref.1) | copy-start | bytes 786436
  46.1 27.9 %copy-start.6 = (bf16[32,4096]{1,0:T(8,128)(2,1)S(1)}, bf16[32,4096]{1,0:T(8,128)(2,1)}, u32[]{:S(2)}) copy-start(bf16[32,4096]{1,0:T(8,128)(2,1)} %v_ref.1) | copy-start | bytes 786436
  46.1 27.9 %copy-start.7 = (bf16[32,4096]{1,0:T(8,128)(2,1)S(1)}, bf16[32,4096]{1,0:T(8,128)(2,1)}, u32[]{:S(2)}) copy-start(bf16[32,4096]{1,0:T(8,128)(2,1)} %o_ref.1) | copy-start | bytes 786436
  70.1 4.9 %collective-permute-start.4 = (f32[8,2,8,128]{3,2,1,0:T(8,128)S(1)}, f32[8,2,8,128]{3,2,1,0:T(8,128)S(1)}, u32[]{:S(2)}, u32[]{:S(2)}) collective-permute-start(f32[8,2,8,128]{3,2,1,0:T(8,128)S(1)} %get-tuple-element.36), channel_id=1, source_target_pairs={{0,3},{1,2},{2,1},{3,0},{4,7},{5,6},{6,5},{7,4},{8,11},{9,10},{10,... | collective-permute-start | bytes 196616 | tf_op jit(solution)/shard_map/ppermute | solution.py:515
  72.9 4.3 %collective-permute-start.3 = (f32[8,2,8,128]{3,2,1,0:T(8,128)S(1)}, f32[8,2,8,128]{3,2,1,0:T(8,128)S(1)}, u32[]{:S(2)}, u32[]{:S(2)}) collective-permute-start(f32[8,2,8,128]{3,2,1,0:T(8,128)S(1)} %get-tuple-element.37), channel_id=1, source_target_pairs={{0,2},{1,3},{2,0},{3,1},{4,6},{5,7},{6,4},{7,5},{8,10},{9,11},{10,... | collective-permute-start | bytes 196616 | tf_op jit(solution)/shard_map/ppermute | solution.py:515
  73.9 3.3 %collective-permute-start.2 = (f32[8,2,8,128]{3,2,1,0:T(8,128)S(1)}, f32[8,2,8,128]{3,2,1,0:T(8,128)S(1)}, u32[]{:S(2)}, u32[]{:S(2)}) collective-permute-start(f32[8,2,8,128]{3,2,1,0:T(8,128)S(1)} %get-tuple-element.38), channel_id=1, source_target_pairs={{0,1},{1,0},{2,3},{3,2},{4,5},{5,4},{6,7},{7,6},{8,9},{9,8},{10,11... | collective-permute-start | bytes 196616 | tf_op jit(solution)/shard_map/ppermute | solution.py:515

commit v8 on v7

--- a/solution.py
+++ b/solution.py
@@ -210,6 +210,7 @@
     carried_ref,
     kept_ref,
     given_ref,
+    own_ref,
     mixed_ref,
     z_ref,
     product_ref,
@@ -222,6 +223,9 @@
 
     def store(p, value):
         halves_ref[p // 2, :, p % 2] = value.reshape(blocks, block_rows, INNER)
+
+    def mix_own(part):
+        mix(x_ref, first_ref, own_ref, slice(None), 2 * TURNS, part)
 
     spectra = (gated_ref, carried_ref)
     def mixes(a, pair, part):
@@ -240,7 +244,7 @@
         (steps(lasts[1], ALL_TURNS[1:]), steps(products, ALL_TURNS[:-1], CHUNKS)),
         (steps(last_back, ALL_TURNS[:-1]), steps(products, ALL_TURNS[-1:], CHUNKS)),
         (steps(last_back, ALL_TURNS[-1:]), []),
-        ([], steps(close, CHUNKS)),
+        (steps(mix_own, range(2)), steps(close, CHUNKS)),
         (steps(functools.partial(unmix, v_ref, first_back_ref, store), PAIRS), []),
     )
     kept_ref[...] = halves_ref[core]
@@ -249,7 +253,7 @@
 
 def convolve_kernel(
     core_ref,
-    x_ref,
+    own_ref,
     other_ref,
     gated_ref,
     carried_ref,
@@ -267,21 +271,29 @@
     u_ref,
     v_conv_ref,
 ):
-    blocks, _, block_rows, _ = x_ref.shape
+    blocks, _, block_rows, _ = other_ref.shape
     wide = 2 * INNER
+
+    def place(other):
+        start = jnp.bitwise_xor(core_ref[0], other) * wide
+        return pl.ds(pl.multiple_of(start, wide), wide)
 
     def store(p, value):
         conv_ref[:, p] = value.reshape(blocks, block_rows, INNER)
 
+    def mix_other(part):
+        mix(other_ref, first_ref, mixed_ref, place(1), 0, part)
+
+    def copy_own(part):
+        rows = slice(part * ROWS, (part + 1) * ROWS)
+        mixed_ref[rows, place(0)] = own_ref[rows]
+
     v_refs = (v_conv_ref, v_ref)
-
-    def mixes(other, part):
-        start = pl.multiple_of(jnp.bitwise_xor(core_ref[0], other) * wide, wide)
-        source, first_slot = ((x_ref, 2 * TURNS), (other_ref, 0))[other]
-        mix(source, first_ref, mixed_ref, pl.ds(start, wide), first_slot, part)
-
     opens = functools.partial(opening, mixed_ref, turn_ref, z_ref)
-    lasts = functools.partial(last, z_ref, last_ref, filter_ref)
+
+    def lasts(part, j):
+        rows = slice(part * ROWS // 2, (part + 1) * ROWS // 2)
+        last(z_ref.at[:, :, rows], last_ref, filter_ref.at[:, rows], j)
 
     def products(j, rows):
         product(gated_ref, filter_ref, False, product_ref.at[0], j, rows)
@@ -294,10 +306,11 @@
         functools.partial(closing, u_ref.at[a], turn_ref, v_refs[a]) for a in range(2)
     ]
     interleave(
-        (steps(mixes, range(2), range(2)), []),
-        ([], steps(opens, CHUNKS)),
-        (steps(lasts, [0]), []),
-        (steps(lasts, ALL_TURNS[1:]), steps(products, ALL_TURNS[:-1], CHUNKS)),
+        (steps(mix_other, range(2)), steps(copy_own, range(2))),
+        ([], steps(opens, CHUNKS[: len(CHUNKS) // 2])),
+        (steps(lasts, [0], ALL_TURNS), steps(opens, CHUNKS[len(CHUNKS) // 2 :])),
+        (steps(lasts, [1], [0]), []),
+        (steps(lasts, [1], ALL_TURNS[1:]), steps(products, ALL_TURNS[:-1], CHUNKS)),
         (steps(last_back, ALL_TURNS[:-1], range(2)), steps(products, ALL_TURNS[-1:], CHUNKS)),
         (steps(last_back, ALL_TURNS[-1:], [0]), []),
         (steps(last_back, ALL_TURNS[-1:], [1]), steps(close[0], CHUNKS)),
@@ -338,11 +351,12 @@
     spectrum = (TURNS, ROWS, 2 * INNER)
     two_halves = jax.ShapeDtypeStruct((blocks, 2, block_rows, INNER), F32)
     params = pltpu.CompilerParams(vmem_limit_bytes=VMEM_BYTES)
-    gated, carried, kept, given = pl.pallas_call(
+    gated, carried, kept, given, own = pl.pallas_call(
         correlate_kernel,
-        out_shape=(jax.ShapeDtypeStruct(spectrum, F32),) * 2 + (two_halves,) * 2,
+        out_shape=(jax.ShapeDtypeStruct(spectrum, F32),) * 2 + (two_halves,) * 2
+        + (jax.ShapeDtypeStruct((2 * ROWS, 2 * INNER), F32),),
         in_specs=[pl.BlockSpec(memory_space=pltpu.SMEM)] + in_vmem(6),
-        out_specs=tuple(in_vmem(4)),
+        out_specs=tuple(in_vmem(5)),
         scratch_shapes=[
             pltpu.VMEM((2, 2 * ROWS, width), F32),
             pltpu.VMEM((2, 2, *spectrum), BF16),
@@ -373,7 +387,7 @@
         ],
         compiler_params=params,
         name="convolve",
-    )(core, received, other_filter, gated, carried, first, first_back, turn, last_table, last_back)
+    )(core, own, other_filter, gated, carried, first, first_back, turn, last_table, last_back)
     return pl.pallas_call(
         gather_kernel,
         out_shape=jax.ShapeDtypeStruct((blocks, 2 * TURNS + 2, block_rows, INNER), F32),
@@ -389,42 +403,48 @@
     chan = place_ref[0]
     tall = 2 * GROUP
     tiles = range(0, sources[0].shape[0], tall)
-    copies = []
+    needs = ((1, 2), (0, 3), (4,))
+    copies = {}
     for t, tile in enumerate(tiles):
-        for n in range(5):
+        for n in itertools.chain(*needs):
             rows = pl.ds(tile, tall)
-            copies.append(pltpu.make_async_copy(sources[n].at[rows], held[n].at[rows], sems.at[t, n]))
-    for copy in copies:
-        copy.start()
+            copies[t, n] = pltpu.make_async_copy(sources[n].at[rows], held[n].at[rows], sems.at[t, n])
+            copies[t, n].start()
     outgoing = []
     q_ref, k_ref, v_ref, o_ref, f_ref = held
     for t, tile in enumerate(tiles):
-        for copy in copies[5 * t : 5 * t + 5]:
-            copy.wait()
         rows = slice(tile, tile + tall)
-        for p in range(TURNS):
-            values = [[], [], []]
-            half = 2 * core_ref[0] + p
-            for m in range(block_rows):
-                columns = lanes(m * TURNS + p)
-                values[0].append(k_ref[rows, columns].astype(F32) * v_ref[rows, columns].astype(F32))
-                values[1].append(q_ref[rows, columns].astype(F32) * o_ref[rows, columns].astype(F32))
-                if p < 2:
-                    start = pl.multiple_of((m * TURNS + half) * INNER, INNER)
-                    values[2].append(f_ref[rows, pl.ds(start, INNER)])
-            for h in range(2):
-                for a in range(SIGNALS if p < 2 else 2):
-                    block = jnp.stack([value[h * GROUP : (h + 1) * GROUP] for value in values[a]])
+        for a in range(SIGNALS):
+            for n in needs[a]:
+                copies[t, n].wait()
+            count = TURNS if a < 2 else 2
+            for p in range(count):
+                values = []
+                for m in range(block_rows):
+                    columns = lanes(m * TURNS + p)
+                    if a == 0:
+                        value = k_ref[rows, columns].astype(F32) * v_ref[rows, columns].astype(F32)
+                    elif a == 1:
+                        value = q_ref[rows, columns].astype(F32) * o_ref[rows, columns].astype(F32)
+                    else:
+                        start = pl.multiple_of((m * TURNS + 2 * core_ref[0] + p) * INNER, INNER)
+                        value = f_ref[rows, pl.ds(start, INNER)]
+                    values.append(value)
+                for h in range(2):
+                    block = jnp.stack([value[h * GROUP : (h + 1) * GROUP] for value in values])
                     start = tile + h * GROUP
                     built[start : start + GROUP, a * TURNS + p] = jnp.swapaxes(block, 0, 1)
-        for h in range(2):
-            start = tile + h * GROUP
-            target = jnp.bitwise_xor(chan, start // GROUP) * GROUP
-            copy = pltpu.make_async_copy(
-                built.at[pl.ds(start, GROUP)], sent_ref.at[pl.ds(target, GROUP)], out_sems.at[t, h]
-            )
-            copy.start()
-            outgoing.append(copy)
+            for h in range(2):
+                start = tile + h * GROUP
+                target = jnp.bitwise_xor(chan, start // GROUP) * GROUP
+                slots = pl.ds(a * TURNS, count)
+                copy = pltpu.make_async_copy(
+                    built.at[pl.ds(start, GROUP), slots],
+                    sent_ref.at[pl.ds(target, GROUP), slots],
+                    out_sems.at[t, a, h],
+                )
+                copy.start()
+                outgoing.append(copy)
     for copy in outgoing:
         copy.wait()
 
@@ -494,7 +514,7 @@
         + [
             pltpu.VMEM(shape, F32),
             pltpu.SemaphoreType.DMA((slab // (2 * GROUP), 5)),
-            pltpu.SemaphoreType.DMA((slab // (2 * GROUP), 2)),
+            pltpu.SemaphoreType.DMA((slab // (2 * GROUP), SIGNALS, 2)),
         ],
         compiler_params=pltpu.CompilerParams(vmem_limit_bytes=PACK_BYTES),
         name="pack",

time: 78.2 us -> 77.8 us (level)
  no operation moved by 1% of the time
where the time goes in v8:
time: 77.8 us; the launch traced here: 77.5 us
  blocking collectives  56.1 us (72%)
  Pallas kernels  11.9 us (15%)
  starting transfers between devices  6.43 us (8%)
  waiting for transfers between devices  2.12 us (3%)
  between operations  0.78 us (1%)
    all_to_all x1, blocking collectives, shards(): lax.all_to_all(sent, 'seq', split_axis=0, concat_axis=0, tiled=True)  32.1 us
    all_to_all x1, blocking collectives, shards(): lax.all_to_all(signals, 'seq', split_axis=0, concat_axis=0, tiled=True)  24 us
    ppermute x5, starting transfers between devices, exchange(): lax.ppermute(value, 'chan', [(c, c ^ distance) for c in range(groups)])  6.43 us
    pallas_call x1, Pallas kernels, convolve(): pl.pallas_call(correlate_kernel, out_shape=(jax.ShapeDtypeStruct(spectrum...  3.58 us
    pallas_call x1, Pallas kernels, convolve(): pl.pallas_call(convolve_kernel, out_shape=(jax.ShapeDtypeStruct((blocks,...  3.44 us
    pallas_call x1, Pallas kernels, pack(): pl.pallas_call(functools.partial(pack_kernel, block_rows), out_shape=jax....  2.48 us
    ppermute x5, waiting for transfers between devices, exchange(): lax.ppermute(value, 'chan', [(c, c ^ distance) for c in range(groups)])  2.12 us
    pallas_call x2, Pallas kernels, local_call(): pl.pallas_call(kernel, out_shape=out_shape, in_specs=specs, out_specs=in_...  1.82 us
  transfers between devices with their start and end apart: 5, of which 1 were waited for; matrix products, arithmetic and copies ran while one was open for 0% of the time, Pallas kernels for 11%

profile of v8, /device:TPU:1, one launch (start us, length us, event | category | flops | bytes accessed | tf_op | source)
XLA Modules:
  0.0 77.5 jit_solution(2668500849575905827)
XLA Ops:
  0.6 0.0 copy-start.3
  0.7 2.5 %pack.1 = f32[32,10,8,128]{3,2,1,0:T(8,128)} custom-call(s32[1]{0:T(128)} %bitcast.place_ref, s32[1]{0:T(128)} %bitcast.1.core_ref, bf16[32,4096]{1,0:T(8,128)(2,1)} %refs_0_.1, bf16[32,4096]{1,0:T(8,128)(2,1)} %k_ref.1, bf16[32,4096]{1,0:T(8,128)(2,1)} %v_ref.1, bf16[32,4096]{1,0:T(8,128)(2,1)} %o_ref.1, f32[32,4096]{1,0:T(8,128)} %refs_4_.1), custom_call_target="tpu_custom_call" | custom-call | tf_op jit(solution)/shard_map/pack/pallas_call | solution.py:507
  3.1 0.0 copy-start
  3.2 0.0 copy-start.1
  3.2 0.0 copy-start.2
  3.2 0.0 copy-start.4
  3.2 32.1 %all_to_all.10.x_ref = f32[32,10,8,128]{3,2,1,0:T(8,128)S(1)} all-to-all(f32[32,10,8,128]{3,2,1,0:T(8,128)} %pack.1), channel_id=1, replica_groups=mesh['seq'=32,'chan'=4] {'seq'}, dimensions={0} | all-to-all | bytes 2621440 | tf_op jit(solution)/shard_map/all_to_all | solution.py:542
  35.3 2.5 %collective-permute-start = (f32[32,2,8,128]{3,2,1,0:T(8,128)S(1)}, f32[32,2,8,128]{3,2,1,0:T(8,128)S(1)}, u32[]{:S(2)}, u32[]{:S(2)}) collective-permute-start(f32[32,2,8,128]{3,2,1,0:T(8,128)S(1)} %slice.4), channel_id=1, source_target_pairs={{0,1},{1,0},{2,3},{3,2},{4,5},{5,4},{6,7},{7,6},{8,9},{9,8},{10,11... | collective-permute-start | bytes 786440 | tf_op jit(solution)/shard_map/ppermute | solution.py:535
  37.8 0.0 copy-done.3
  37.8 0.0 copy-done
  37.8 0.0 copy-done.1
  37.8 0.0 copy-done.2
  37.8 0.0 copy-done.4
  37.8 3.6 %correlate.1 = (f32[4,256,256]{2,1,0:T(8,128)S(1)}, f32[4,256,256]{2,1,0:T(8,128)S(1)}, f32[32,2,8,128]{3,2,1,0:T(8,128)S(1)}, f32[32,2,8,128]{3,2,1,0:T(8,128)S(1)}, f32[512,256]{1,0:T(8,128)S(1)}) custom-call(s32[1]{0:T(128)} %bitcast.1.core_ref, f32[32,10,8,128]{3,2,1,0:T(8,128)S(1)} %all_to_all.10.x_ref, bf16[2,512,256]{2,1,0:T(8,128)(2,1)S(1)} %copy-done.4, ...), custom_call_target="tpu_custom_call" | custom-call | tf_op jit(solution)/shard_map/correlate/pallas_call | solution.py:354
  41.4 0.1 collective-permute-start.1
  41.6 0.0 collective-permute-done.other_ref
  41.6 3.4 %convolve.1 = (f32[32,4,8,128]{3,2,1,0:T(8,128)S(1)}, bf16[2,512,512]{2,1,0:T(8,128)(2,1)S(1)}) custom-call(s32[1]{0:T(128)} %bitcast.1.core_ref, f32[512,256]{1,0:T(8,128)S(1)} %get-tuple-element.24.own_ref, f32[32,2,8,128]{3,2,1,0:T(8,128)S(1)} %collective-permute-done.other_ref, f32[4,256,256]{2,1,0:T(8,128)S(1)} %get-tuple-element.25.gated_ref, ...), custom_call_target="tpu_custom_call" | custom-call | tf_op jit(solution)/shard_map/convolve/pallas_call | solution.py:372
  45.0 0.0 collective-permute-done.1.taken_ref
  45.0 0.6 gather.1
  45.6 0.0 copy-start.5
  45.6 0.0 copy-start.6
  45.7 0.0 copy-start.7
  45.7 24.0 %all_to_all.11.back_ref = f32[32,10,8,128]{3,2,1,0:T(8,128)S(1)} all-to-all(f32[32,10,8,128]{3,2,1,0:T(8,128)S(1)} %gather.1), channel_id=1, replica_groups=mesh['seq'=32,'chan'=4] {'seq'}, dimensions={0} | all-to-all | bytes 2621440 | tf_op jit(solution)/shard_map/all_to_all | solution.py:544
  69.7 2.7 %collective-permute-start.4 = (f32[8,2,8,128]{3,2,1,0:T(8,128)S(1)}, f32[8,2,8,128]{3,2,1,0:T(8,128)S(1)}, u32[]{:S(2)}, u32[]{:S(2)}) collective-permute-start(f32[8,2,8,128]{3,2,1,0:T(8,128)S(1)} %get-tuple-element.38), channel_id=1, source_target_pairs={{0,3},{1,2},{2,1},{3,0},{4,7},{5,6},{6,5},{7,4},{8,11},{9,10},{10,... | collective-permute-start | bytes 196616 | tf_op jit(solution)/shard_map/ppermute | solution.py:535
  72.5 1.1 %collective-permute-start.3 = (f32[8,2,8,128]{3,2,1,0:T(8,128)S(1)}, f32[8,2,8,128]{3,2,1,0:T(8,128)S(1)}, u32[]{:S(2)}, u32[]{:S(2)}) collective-permute-start(f32[8,2,8,128]{3,2,1,0:T(8,128)S(1)} %get-tuple-element.39), channel_id=1, source_target_pairs={{0,2},{1,3},{2,0},{3,1},{4,6},{5,7},{6,4},{7,5},{8,10},{9,11},{10,... | collective-permute-start | bytes 196616 | tf_op jit(solution)/shard_map/ppermute | solution.py:535
  73.5 0.0 collective-permute-start.2
  73.5 0.0 copy-done.7
  73.6 1.1 %unpack.1 = (bf16[32,4096]{1,0:T(8,128)(2,1)}, bf16[32,4096]{1,0:T(8,128)(2,1)}, bf16[32,4096]{1,0:T(8,128)(2,1)}) custom-call(s32[1]{0:T(128)} %bitcast.place_ref, f32[32,10,8,128]{3,2,1,0:T(8,128)S(1)} %all_to_all.11.back_ref, bf16[32,4096]{1,0:T(8,128)(2,1)S(1)} %copy-done.5, bf16[32,4096]{1,0:T(8,128)(2,1)S(1)} %copy-done.6, bf16[32,4096]{1,0:T(8,128)(2,1)S(1)} %copy-done.7), custom_call_target="tpu_custom_call" | custom-call | tf_op jit(solution)/shard_map/unpack/pallas_call | solution.py:494
  74.7 0.0 collective-permute-done.4.refs_3_
  74.7 2.1 %collective-permute-done.3.refs_2_ = f32[8,2,8,128]{3,2,1,0:T(8,128)S(1)} collective-permute-done((f32[8,2,8,128]{3,2,1,0:T(8,128)S(1)}, f32[8,2,8,128]{3,2,1,0:T(8,128)S(1)}, u32[]{:S(2)}, u32[]{:S(2)}) %collective-permute-start.3) | collective-permute-done | bytes 65568 | tf_op jit(solution)/shard_map/ppermute | solution.py:535
  76.8 0.0 collective-permute-done.2.refs_1_
  76.8 0.7 total.1
  (4 shorter events, 0.0 us)
Async XLA Ops:
  0.6 37.2 %copy-start.3 = (f32[2,256,512]{2,1,0:T(8,128)S(1)}, f32[2,256,512]{2,1,0:T(8,128)}, u32[]{:S(2)}) copy-start(f32[2,256,512]{2,1,0:T(8,128)} %constant.26.clone.turn_ref) | copy-start | bytes 3145732
  3.1 34.7 %copy-start = (bf16[2,256,512]{2,1,0:T(8,128)(2,1)S(1)}, bf16[2,256,512]{2,1,0:T(8,128)(2,1)}, u32[]{:S(2)}) copy-start(bf16[2,256,512]{2,1,0:T(8,128)(2,1)} %constant.25.clone.first_back_ref) | copy-start | bytes 1572868
  3.2 34.7 %copy-start.1 = (bf16[2,4,256,256]{3,2,1,0:T(8,128)(2,1)S(1)}, bf16[2,4,256,256]{3,2,1,0:T(8,128)(2,1)}, u32[]{:S(2)}) copy-start(bf16[2,4,256,256]{3,2,1,0:T(8,128)(2,1)} %constant.28.clone.last_back_ref) | copy-start | bytes 3145732
  3.2 34.7 %copy-start.2 = (bf16[2,4,256,256]{3,2,1,0:T(8,128)(2,1)S(1)}, bf16[2,4,256,256]{3,2,1,0:T(8,128)(2,1)}, u32[]{:S(2)}) copy-start(bf16[2,4,256,256]{3,2,1,0:T(8,128)(2,1)} %constant.27.clone.last_ref) | copy-start | bytes 3145732
  3.2 34.7 %copy-start.4 = (bf16[2,512,256]{2,1,0:T(8,128)(2,1)S(1)}, bf16[2,512,256]{2,1,0:T(8,128)(2,1)}, u32[]{:S(2)}) copy-start(bf16[2,512,256]{2,1,0:T(8,128)(2,1)} %constant.24.clone.first_ref) | copy-start | bytes 1572868
  35.3 6.3 %collective-permute-start = (f32[32,2,8,128]{3,2,1,0:T(8,128)S(1)}, f32[32,2,8,128]{3,2,1,0:T(8,128)S(1)}, u32[]{:S(2)}, u32[]{:S(2)}) collective-permute-start(f32[32,2,8,128]{3,2,1,0:T(8,128)S(1)} %slice.4), channel_id=1, source_target_pairs={{0,1},{1,0},{2,3},{3,2},{4,5},{5,4},{6,7},{7,6},{8,9},{9,8},{10,11... | collective-permute-start | bytes 786440 | tf_op jit(solution)/shard_map/ppermute | solution.py:535
  41.4 3.6 %collective-permute-start.1 = (f32[32,2,8,128]{3,2,1,0:T(8,128)S(1)}, f32[32,2,8,128]{3,2,1,0:T(8,128)S(1)}, u32[]{:S(2)}, u32[]{:S(2)}) collective-permute-start(f32[32,2,8,128]{3,2,1,0:T(8,128)S(1)} %get-tuple-element.30), channel_id=1, source_target_pairs={{0,1},{1,0},{2,3},{3,2},{4,5},{5,4},{6,7},{7,6},{8,9},{9,8},{10,11... | collective-permute-start | bytes 786440 | tf_op jit(solution)/shard_map/ppermute | solution.py:535
  45.6 27.9 %copy-start.5 = (bf16[32,4096]{1,0:T(8,128)(2,1)S(1)}, bf16[32,4096]{1,0:T(8,128)(2,1)}, u32[]{:S(2)}) copy-start(bf16[32,4096]{1,0:T(8,128)(2,1)} %k_ref.1) | copy-start | bytes 786436
  45.6 27.9 %copy-start.6 = (bf16[32,4096]{1,0:T(8,128)(2,1)S(1)}, bf16[32,4096]{1,0:T(8,128)(2,1)}, u32[]{:S(2)}) copy-start(bf16[32,4096]{1,0:T(8,128)(2,1)} %v_ref.1) | copy-start | bytes 786436
  45.7 27.9 %copy-start.7 = (bf16[32,4096]{1,0:T(8,128)(2,1)S(1)}, bf16[32,4096]{1,0:T(8,128)(2,1)}, u32[]{:S(2)}) copy-start(bf16[32,4096]{1,0:T(8,128)(2,1)} %o_ref.1) | copy-start | bytes 786436
  69.7 4.9 %collective-permute-start.4 = (f32[8,2,8,128]{3,2,1,0:T(8,128)S(1)}, f32[8,2,8,128]{3,2,1,0:T(8,128)S(1)}, u32[]{:S(2)}, u32[]{:S(2)}) collective-permute-start(f32[8,2,8,128]{3,2,1,0:T(8,128)S(1)} %get-tuple-element.38), channel_id=1, source_target_pairs={{0,3},{1,2},{2,1},{3,0},{4,7},{5,6},{6,5},{7,4},{8,11},{9,10},{10,... | collective-permute-start | bytes 196616 | tf_op jit(solution)/shard_map/ppermute | solution.py:535
  72.5 4.3 %collective-permute-start.3 = (f32[8,2,8,128]{3,2,1,0:T(8,128)S(1)}, f32[8,2,8,128]{3,2,1,0:T(8,128)S(1)}, u32[]{:S(2)}, u32[]{:S(2)}) collective-permute-start(f32[8,2,8,128]{3,2,1,0:T(8,128)S(1)} %get-tuple-element.39), channel_id=1, source_target_pairs={{0,2},{1,3},{2,0},{3,1},{4,6},{5,7},{6,4},{7,5},{8,10},{9,11},{10,... | collective-permute-start | bytes 196616 | tf_op jit(solution)/shard_map/ppermute | solution.py:535
  73.5 3.3 %collective-permute-start.2 = (f32[8,2,8,128]{3,2,1,0:T(8,128)S(1)}, f32[8,2,8,128]{3,2,1,0:T(8,128)S(1)}, u32[]{:S(2)}, u32[]{:S(2)}) collective-permute-start(f32[8,2,8,128]{3,2,1,0:T(8,128)S(1)} %get-tuple-element.40), channel_id=1, source_target_pairs={{0,1},{1,0},{2,3},{3,2},{4,5},{5,4},{6,7},{7,6},{8,9},{9,8},{10,11... | collective-permute-start | bytes 196616 | tf_op jit(solution)/shard_map/ppermute | solution.py:535
